TPU v7x, 32 devices: a whole 2x2x4 slice. The times are simulated.
32 devices in a mesh: rep: 1, expert: 32 (over z, y, x, core), fsdp: 1.
Axes of the slice: x: 2, y: 2, z: 4, core: 2. Of those that a mesh axis runs over, the one named last changes fastest.
Arguments:
- tokens: bfloat16 [512, 3584], P(('rep', 'expert', 'fsdp')), may hold values from -6 to 6
- expert_ids: int32 [512, 8], P(('rep', 'expert', 'fsdp')), may hold values from 0 to 31, all different within a row; in each aligned block of 16 rows (0 to 15, 16 to 31, ...) at most 8 rows name the same one
- gate_logits: float32 [512, 8], P(('rep', 'expert', 'fsdp')), may hold values from -6 to 6
- bin_ids: int32 [512, 8, 8], P(('rep', 'expert', 'fsdp')), may hold values from 0 to 2047
- up_weight: bfloat16 [32, 3584, 1024], P('expert', 'fsdp'), may hold values from -0.09375 to 0.09375
Outputs:
- mixed: bfloat16 [512, 1024], P(('rep', 'expert', 'fsdp'))
- histogram: float32 [32, 8, 2048], P(('rep', 'expert'), None, 'fsdp')
Inputs may be any that keep to these rules, and one draw needn't show every extreme that they name: `expert_ids`: each token names 8 different experts; among the tokens of one device no expert is named by more than 8 of them, a bound that some block reaches.
All inputs are finite; a program needn't handle non-finite values.
Results may differ from a plain program's by a relative error of at most 0.015.
Values may be sent and summed in bfloat16 or wider, within the bound.
No kernel may reach another device: no remote copies, remote signals or barrier semaphores. Data moves between devices by JAX's collectives and lax.ppermute only.
A program may use at most 64 MiB of HBM per device.

v0:
```python
import jax
import jax.numpy as jnp
from jax import lax
from jax.sharding import PartitionSpec as P

BLOCK = 128
NBINS = 2048


route_scale = 2.827


def shards(tokens, expert_ids, gate_logits, bin_ids, up_weight):
    tok_rows, chosen = expert_ids.shape
    groups = lax.axis_size("expert")
    capacity = min(tok_rows, 2 * tok_rows * chosen // groups)
    slot_count = groups * capacity
    model_width = tokens.shape[1]
    block_count = bin_ids.shape[2]
    hidden_width = up_weight.shape[2]
    row_count = tok_rows * chosen
    flat_ids = expert_ids.reshape(-1)
    row_order = jnp.arange(row_count, dtype=jnp.int32)
    same_expert = (flat_ids[:, None] == flat_ids[None, :]) & (
        row_order[None, :] < row_order[:, None]
    )
    slot_rank = jnp.sum(same_expert.astype(jnp.int32), axis=1)
    slot_index = flat_ids * capacity + slot_rank
    placed = slot_index[None, :] == jnp.arange(slot_count, dtype=jnp.int32)[:, None]
    source_row = jnp.sum(jnp.where(placed, row_order[None, :], 0), axis=1)
    filled = jnp.any(placed, axis=1)
    placed_tokens = jnp.any(placed.reshape(slot_count, tok_rows, chosen), axis=2).astype(
        jnp.bfloat16
    )
    outgoing = jnp.dot(placed_tokens, tokens, preferred_element_type=jnp.float32).astype(
        jnp.bfloat16
    )
    out_bins = jnp.where(filled[:, None], bin_ids.reshape(row_count, block_count)[source_row], 0)
    arrived, arrived_bins = (
        lax.all_to_all(
            outgoing.reshape(groups, capacity, model_width),
            "expert",
            split_axis=0,
            concat_axis=0,
            tiled=True,
        ),
        lax.all_to_all(
            out_bins.reshape(groups, capacity, block_count),
            "expert",
            split_axis=0,
            concat_axis=0,
            tiled=True,
        ),
    )
    incoming = arrived.reshape(slot_count, model_width)
    bin_rows = arrived_bins.reshape(slot_count, block_count)
    up_rows = jnp.dot(
        incoming,
        lax.all_gather(up_weight, "fsdp", axis=1, tiled=True)[0],
        preferred_element_type=jnp.float32,
    )
    energy = jnp.mean((up_rows * up_rows).reshape(slot_count, block_count, BLOCK), axis=2)
    levels = jnp.arange(NBINS, dtype=jnp.int32)
    hist_rows = []
    for block_idx in range(block_count):
        onehot = (bin_rows[:, block_idx][:, None] == levels[None, :]).astype(jnp.float32)
        hist_rows.append(
            jnp.dot(energy[:, block_idx][None, :], onehot, precision=lax.Precision.HIGHEST)
        )
    partial_hist = jnp.concatenate(hist_rows, axis=0)[None]
    histogram = lax.psum_scatter(
        partial_hist.astype(jnp.bfloat16), "fsdp", scatter_dimension=2, tiled=True
    ).astype(jnp.float32)
    returned = lax.all_to_all(
        up_rows.astype(jnp.bfloat16).reshape(groups, capacity, hidden_width),
        "expert",
        split_axis=0,
        concat_axis=0,
        tiled=True,
    ).reshape(slot_count, hidden_width)
    scores = jax.nn.sigmoid(gate_logits)
    route_weight = (route_scale * scores / jnp.sum(scores, axis=1, keepdims=True)).astype(
        jnp.bfloat16
    )
    placed_back = placed.T.reshape(tok_rows, chosen, slot_count)
    combine = jnp.sum(jnp.where(placed_back, route_weight[:, :, None], jnp.bfloat16(0.0)), axis=1)
    mixed = jnp.dot(combine, returned, preferred_element_type=jnp.float32).astype(jnp.bfloat16)
    return (mixed, histogram)


def solution(mesh):
    return jax.shard_map(
        shards,
        mesh=mesh,
        in_specs=(
            P(("rep", "expert", "fsdp"), None),
            P(("rep", "expert", "fsdp"), None),
            P(("rep", "expert", "fsdp"), None),
            P(("rep", "expert", "fsdp"), None, None),
            P("expert", "fsdp", None),
        ),
        out_specs=(P(("rep", "expert", "fsdp"), None), P(("rep", "expert"), None, "fsdp")),
        check_vma=False,
    )
```

profile of v0, /device:TPU:0, one launch (start us, length us, event | category | flops | bytes accessed | tf_op | source)
XLA Modules:
  0.0 92.1 jit_solution(815803576078673076)
XLA Ops:
  0.6 0.0 copy-start
  0.6 0.8 copy.27
  1.4 0.1 eq.163
  1.5 0.2 convert_reduce_fusion
  1.7 0.1 select_reduce_fusion
  1.8 0.1 fusion.21
  2.0 0.8 copy.30
  2.8 0.7 gather_fusion
  3.6 0.1 copy.31
  3.7 0.1 broadcast_in_dim.36
  3.8 0.7 broadcast_select_fusion
  4.4 7.3 %all-to-all-start.2 = ((s32[32,8,8]{1,2,0:T(8,128)}), s32[32,8,8]{1,2,0:T(8,128)S(1)}, u32[]{:S(2)}, u32[]{:S(2)}) async-start(s32[32,8,8]{1,2,0:T(8,128)} %broadcast_select_fusion), calls=%async_computation.2 | async-start | bytes 262144 | tf_op jit(solution)/shard_map/all_to_all | solution.py:47
  11.7 0.1 reduce_sum.53
  11.8 0.1 fusion.23
  12.0 0.0 copy-done
  12.0 1.9 %fusion.2 = bf16[32,8,3584]{2,1,0:T(8,128)(2,1)} fusion(pred[256,16]{0,1:T(8,128)(4,1)S(1)} %fusion.23, bf16[16,3584]{1,0:T(8,128)(2,1)S(1)} %copy-done), kind=kOutput, calls=%fused_computation.4 | convolution fusion | flops 30277632 | bytes 1953792 | tf_op jit(solution)/shard_map/dot_general | solution.py:35
  13.9 0.0 copy-start.1
  13.9 6.1 %all-to-all-done.2 = s32[32,8,8]{1,2,0:T(8,128)S(1)} async-done(((s32[32,8,8]{1,2,0:T(8,128)}), s32[32,8,8]{1,2,0:T(8,128)S(1)}, u32[]{:S(2)}, u32[]{:S(2)}) %all-to-all-start.2) | async-done | bytes 8224 | tf_op jit(solution)/shard_map/all_to_all | solution.py:47
  20.0 2.7 %all-to-all-start = ((bf16[32,8,3584]{2,1,0:T(8,128)(2,1)}), bf16[32,8,3584]{2,1,0:T(8,128)(2,1)S(1)}, u32[]{:S(2)}, u32[]{:S(2)}) async-start(bf16[32,8,3584]{2,1,0:T(8,128)(2,1)} %fusion.2), calls=%async_computation | async-start | bytes 3670016 | tf_op jit(solution)/shard_map/all_to_all | solution.py:40
  22.7 0.0 copy-done.1
  22.7 0.1 copy.29
  22.8 0.1 fusion.24
  23.0 0.1 reshape.253
  23.1 42.8 %all-to-all-done = bf16[32,8,3584]{2,1,0:T(8,128)(2,1)S(1)} async-done(((bf16[32,8,3584]{2,1,0:T(8,128)(2,1)}), bf16[32,8,3584]{2,1,0:T(8,128)(2,1)S(1)}, u32[]{:S(2)}, u32[]{:S(2)}) %all-to-all-start) | async-done | bytes 1835040 | tf_op jit(solution)/shard_map/all_to_all | solution.py:40
  65.9 5.9 %multiply_bitcast_fusion = (f32[32,8,8,128]{3,1,2,0:T(8,128)S(1)}, bf16[32,8,1024]{2,1,0:T(8,128)(2,1)}) fusion(bf16[1,3584,1024]{2,1,0:T(8,128)(2,1)} %param.9, bf16[32,8,3584]{2,1,0:T(8,128)(2,1)S(1)} %all-to-all-done), kind=kOutput, calls=%fused_computation.31 | convolution fusion | flops 1879572480 | bytes 10747904 | tf_op jit(solution)/shard_map/dot_general | solution.py:57
  71.9 3.9 %all-to-all-start.1 = ((bf16[32,8,1024]{2,1,0:T(8,128)(2,1)}), bf16[32,8,1024]{2,1,0:T(8,128)(2,1)S(1)}, u32[]{:S(2)}, u32[]{:S(2)}) async-start(bf16[32,8,1024]{2,1,0:T(8,128)(2,1)} %get-tuple-element.11), calls=%async_computation.1 | async-start | bytes 1048576 | tf_op jit(solution)/shard_map/all_to_all | solution.py:74
  75.8 0.2 copy.33
  76.0 0.3 reduce_sum.56
  76.3 0.6 slice_reduce_fusion
  77.0 0.8 fusion.3
  77.8 0.8 fusion.4
  78.7 0.8 fusion.5
  79.5 0.8 fusion.6
  80.3 0.8 fusion.7
  81.2 0.8 fusion.8
  82.0 0.8 fusion.9
  82.9 0.8 fusion.10
  83.7 0.1 concatenate.35
  83.8 0.6 convert_element_type.51
  84.5 6.9 %all-to-all-done.1 = bf16[32,8,1024]{2,1,0:T(8,128)(2,1)S(1)} async-done(((bf16[32,8,1024]{2,1,0:T(8,128)(2,1)}), bf16[32,8,1024]{2,1,0:T(8,128)(2,1)S(1)}, u32[]{:S(2)}, u32[]{:S(2)}) %all-to-all-start.1) | async-done | bytes 524320 | tf_op jit(solution)/shard_map/all_to_all | solution.py:74
  91.3 0.8 convolution_convert_fusion.1
  (25 shorter events, 0.2 us)
Async XLA Ops:
  0.6 11.3 %copy-start = (bf16[16,3584]{1,0:T(8,128)(2,1)S(1)}, bf16[16,3584]{1,0:T(8,128)(2,1)}, u32[]{:S(2)}) copy-start(bf16[16,3584]{1,0:T(8,128)(2,1)} %param.5) | copy-start | bytes 344068
  4.4 15.5 %all-to-all-start.2 = ((s32[32,8,8]{1,2,0:T(8,128)}), s32[32,8,8]{1,2,0:T(8,128)S(1)}, u32[]{:S(2)}, u32[]{:S(2)}) async-start(s32[32,8,8]{1,2,0:T(8,128)} %broadcast_select_fusion), calls=%async_computation.2 | async-start | bytes 262144 | tf_op jit(solution)/shard_map/all_to_all | solution.py:47
  13.9 8.8 %copy-start.1 = (f32[16,8]{0,1:T(8,128)S(1)}, f32[16,8]{0,1:T(8,128)}, u32[]{:S(2)}) copy-start(f32[16,8]{0,1:T(8,128)} %param.7) | copy-start | bytes 1540
  20.0 46.0 %all-to-all-start = ((bf16[32,8,3584]{2,1,0:T(8,128)(2,1)}), bf16[32,8,3584]{2,1,0:T(8,128)(2,1)S(1)}, u32[]{:S(2)}, u32[]{:S(2)}) async-start(bf16[32,8,3584]{2,1,0:T(8,128)(2,1)} %fusion.2), calls=%async_computation | async-start | bytes 3670016 | tf_op jit(solution)/shard_map/all_to_all | solution.py:40
  71.9 19.5 %all-to-all-start.1 = ((bf16[32,8,1024]{2,1,0:T(8,128)(2,1)}), bf16[32,8,1024]{2,1,0:T(8,128)(2,1)S(1)}, u32[]{:S(2)}, u32[]{:S(2)}) async-start(bf16[32,8,1024]{2,1,0:T(8,128)(2,1)} %get-tuple-element.11), calls=%async_computation.1 | async-start | bytes 1048576 | tf_op jit(solution)/shard_map/all_to_all | solution.py:74
where the time goes:
time: 92.6 us; the launch traced here: 92.1 us
  waiting for transfers between devices  55.7 us (60%)
  matrix products  15.3 us (17%)
  starting transfers between devices  13.9 us (15%)
  local copies, waits for them, and re-layouts  3.97 us (4%)
  other arithmetic  2.46 us (3%)
    all_to_all x1, waiting for transfers between devices, shards(): lax.all_to_all(outgoing.reshape(groups, capacity, model_width), 'expert',...  42.8 us
    all_to_all x1, starting transfers between devices, shards(): lax.all_to_all(out_bins.reshape(groups, capacity, block_count), 'expert',...  7.3 us
    all_to_all x1, waiting for transfers between devices, shards(): lax.all_to_all(up_rows.astype(jnp.bfloat16).reshape(groups, capacity, hid...  6.87 us
    dot_general x8, matrix products, shards(): jnp.dot(energy[:, block_idx][None, :], onehot, precision=lax.Precision.HI...  6.59 us
    all_to_all x1, waiting for transfers between devices, shards(): lax.all_to_all(out_bins.reshape(groups, capacity, block_count), 'expert',...  6.06 us
    dot_general x1, matrix products, shards(): jnp.dot(incoming, lax.all_gather(up_weight, 'fsdp', axis=1, tiled=True)[0...  5.93 us
    all_to_all x1, starting transfers between devices, shards(): lax.all_to_all(up_rows.astype(jnp.bfloat16).reshape(groups, capacity, hid...  3.9 us
    all_to_all x1, starting transfers between devices, shards(): lax.all_to_all(outgoing.reshape(groups, capacity, model_width), 'expert',...  2.71 us
  transfers between devices with their start and end apart: 3, of which 3 were waited for; matrix products, arithmetic and copies ran while one was open for 12% of the time, Pallas kernels for 0%

commit v1 on v0

v1 whole, which is shorter than its diff:
```python
import functools

import jax
import jax.numpy as jnp
from jax import lax
from jax.experimental import pallas as pl
from jax.experimental.pallas import tpu as pltpu
from jax.sharding import PartitionSpec as P

BLOCK = 128
NBINS = 2048
LANES = 128
TILE_N = 256

route_scale = 2.827


def pack_rows(tokens, expert_ids, gate_logits, bin_ids):
    tok_rows, chosen = expert_ids.shape
    scores = jax.nn.sigmoid(gate_logits)
    route_weight = (route_scale * scores / jnp.sum(scores, axis=1, keepdims=True)).astype(
        jnp.bfloat16
    )
    bins = bin_ids.reshape(tok_rows, -1)
    code = ((128 + (bins & 127)) << (bins >> 7)).astype(jnp.float32).astype(jnp.bfloat16)
    tail = jnp.concatenate([expert_ids.astype(jnp.bfloat16), route_weight, code], axis=1)
    tail = jnp.pad(tail, ((0, 0), (0, LANES - tail.shape[1])))
    return jnp.concatenate([tokens, tail], axis=1)


def expert_kernel(chosen, blocks, n_parts, me_ref, *refs):
    parts = refs[:n_parts]
    w_ref = refs[n_parts]
    outs = refs[n_parts + 1 : 2 * n_parts + 1]
    code_ref, energy_ref = refs[2 * n_parts + 1 : 2 * n_parts + 3]
    step = pl.program_id(0)
    width, tile = w_ref.shape

    @pl.when(step == 0)
    def _():
        tail = jnp.concatenate([p[:, width:] for p in parts], axis=0)
        row = lax.broadcasted_iota(jnp.int32, (LANES, LANES), 0)
        col = lax.broadcasted_iota(jnp.int32, (LANES, LANES), 1)
        bins_at = 2 * chosen
        bins_end = bins_at + chosen * blocks
        choice = jnp.where(col < bins_at, col - chosen, (col - bins_at) // blocks)
        carries = (col >= chosen) & (col < bins_end)
        spread = jnp.where((row == choice) & carries, 1.0, 0.0).astype(jnp.bfloat16)
        ids = jnp.dot(tail, spread, preferred_element_type=jnp.float32)
        lane = lax.broadcasted_iota(jnp.int32, tail.shape, 1)
        mine = (
            (ids == me_ref[0].astype(jnp.float32)) & (lane >= chosen) & (lane < bins_end)
        )
        picked = jnp.where(mine, tail, jnp.zeros_like(tail))
        target = jnp.where(row < bins_at, blocks, (row - bins_at) % blocks)
        usable = (row >= chosen) & (row < bins_end)
        fold = jnp.where((col == target) & usable, 1.0, 0.0).astype(jnp.bfloat16)
        code_ref[...] = jnp.dot(picked, fold, preferred_element_type=jnp.float32)
        energy_ref[...] = jnp.zeros_like(energy_ref)

    rows = jnp.concatenate([p[:, :width] for p in parts], axis=0)
    up = jnp.dot(rows, w_ref[...], preferred_element_type=jnp.float32)
    unit = lax.broadcasted_iota(jnp.int32, (tile, LANES), 0)
    lane = lax.broadcasted_iota(jnp.int32, (tile, LANES), 1)
    mean = jnp.where(
        (unit + step * tile) // BLOCK == lane % blocks, 1.0 / BLOCK, 0.0
    ).astype(jnp.bfloat16)
    energy_ref[...] += jnp.dot(
        (up * up).astype(jnp.bfloat16), mean, preferred_element_type=jnp.float32
    )
    weight = code_ref[:, blocks : blocks + 1]
    scaled = (weight * up.astype(jnp.bfloat16).astype(jnp.float32)).astype(jnp.bfloat16)
    at = 0
    for part, out in zip(parts, outs):
        out[...] = scaled[at : at + part.shape[0]]
        at += part.shape[0]


def expert_rows(me, parts, weight, chosen, blocks):
    width, hidden = weight.shape
    total = sum(p.shape[0] for p in parts)
    tile = min(TILE_N, hidden)
    small = jax.ShapeDtypeStruct((total, LANES), jnp.float32)
    return pl.pallas_call(
        functools.partial(expert_kernel, chosen, blocks, len(parts)),
        grid=(hidden // tile,),
        in_specs=[pl.BlockSpec(memory_space=pltpu.SMEM)]
        + [pl.BlockSpec(p.shape, lambda j: (0, 0)) for p in parts]
        + [pl.BlockSpec((width, tile), lambda j: (0, j))],
        out_specs=[pl.BlockSpec((p.shape[0], tile), lambda j: (0, j)) for p in parts]
        + [pl.BlockSpec((total, LANES), lambda j: (0, 0))] * 2,
        out_shape=[jax.ShapeDtypeStruct((p.shape[0], hidden), jnp.bfloat16) for p in parts]
        + [small, small],
        compiler_params=pltpu.CompilerParams(
            dimension_semantics=("arbitrary",), vmem_limit_bytes=24 * 1024 * 1024
        ),
        cost_estimate=pl.CostEstimate(
            flops=2 * total * width * hidden,
            bytes_accessed=2 * width * hidden,
            transcendentals=0,
        ),
        name="expert_rows",
    )(me, *parts, weight)


def histogram_kernel(blocks, n_parts, *refs):
    codes, energies = refs[:n_parts], refs[n_parts : 2 * n_parts]
    out_ref = refs[2 * n_parts]
    levels = NBINS // LANES
    row = lax.broadcasted_iota(jnp.int32, (LANES, LANES), 0)
    col = lax.broadcasted_iota(jnp.int32, (LANES, LANES), 1)
    repeat = jnp.where(row == col % blocks, 1.0, 0.0).astype(jnp.bfloat16)
    wide_row = lax.broadcasted_iota(jnp.int32, (LANES, blocks * LANES), 0)
    wide_col = lax.broadcasted_iota(jnp.int32, (LANES, blocks * LANES), 1)
    stretch = jnp.where(wide_row == wide_col // LANES, 1.0, 0.0).astype(jnp.bfloat16)
    total = jnp.zeros((LANES, blocks * LANES), jnp.float32)
    for code_ref, energy_ref in zip(codes, energies):
        code = code_ref[...]
        lane = lax.broadcasted_iota(jnp.int32, code.shape, 1)
        code = jnp.where(lane < blocks, code, 0.0)
        low = code
        high = jnp.where(code > 0.0, 0.0, -1.0)
        for _ in range(levels - 1):
            above = low >= 256.0
            low = jnp.where(above, low * 0.5, low)
            high = jnp.where(above, high + 1.0, high)
        low = jnp.where(code > 0.0, low - 128.0, -1.0)
        high_all = jnp.dot(high.astype(jnp.bfloat16), repeat, preferred_element_type=jnp.float32)
        low_all = jnp.dot(low.astype(jnp.bfloat16), stretch, preferred_element_type=jnp.float32)
        energy = jnp.where(high_all == (lane // blocks).astype(jnp.float32), energy_ref[...], 0.0)
        near = energy.astype(jnp.bfloat16)
        rest = (energy - near.astype(jnp.float32)).astype(jnp.bfloat16)
        spot = lax.broadcasted_iota(jnp.int32, low_all.shape, 1) % LANES
        onehot = jnp.where(low_all == spot.astype(jnp.float32), 1.0, 0.0).astype(jnp.bfloat16)
        for piece in (near, rest):
            total += lax.dot_general(
                piece, onehot, (((0,), (0,)), ((), ())), preferred_element_type=jnp.float32
            )
    pick = lax.broadcasted_iota(jnp.int32, (blocks, LANES), 0)
    for level in range(levels):
        band = total[level * blocks : (level + 1) * blocks]
        line = jnp.zeros((blocks, LANES), jnp.float32)
        for block in range(blocks):
            line = jnp.where(pick == block, band[:, block * LANES : (block + 1) * LANES], line)
        out_ref[:, level * LANES : (level + 1) * LANES] = line


def expert_histogram(codes, energies, blocks):
    rows = sum(c.shape[0] for c in codes)
    return pl.pallas_call(
        functools.partial(histogram_kernel, blocks, len(codes)),
        out_shape=jax.ShapeDtypeStruct((blocks, NBINS), jnp.float32),
        compiler_params=pltpu.CompilerParams(vmem_limit_bytes=24 * 1024 * 1024),
        cost_estimate=pl.CostEstimate(
            flops=4 * rows * LANES * LANES * blocks,
            bytes_accessed=8 * rows * LANES,
            transcendentals=0,
        ),
        name="expert_histogram",
    )(*codes, *energies)


def swap(array, even, odd=None):
    odd = even if odd is None else odd
    size = lax.axis_size("expert")
    return lax.ppermute(array, "expert", [(i, i ^ (odd if i & 1 else even)) for i in range(size)])


def add32(*arrays):
    return functools.reduce(lambda a, b: a + b, [a.astype(jnp.float32) for a in arrays])


def boxed(packed, me, weight, chosen, blocks):
    layers = [packed, swap(packed, 8), swap(packed, 16), swap(packed, 24)]
    keeps, sends, codes, energies = [], [], [], []
    for rows in layers:
        first = swap(rows, 2, 4)
        second = swap(rows, 4, 2)
        third = swap(first, 4, 2)
        half = jnp.concatenate([rows, first, second, third], axis=0)
        other = swap(half, 1)
        keep, send, code, energy = expert_rows(me, [half, other], weight, chosen, blocks)
        keeps.append(keep)
        sends.append(send)
        codes.append(code)
        energies.append(energy)
    tok_rows = packed.shape[0]
    four = len(layers)
    keep = jnp.stack(keeps).reshape(four, 4, tok_rows, -1)
    came = swap(jnp.stack(sends), 1).reshape(keep.shape)
    partial = add32(keep, came)
    crossed = swap(partial[:, 2:].astype(jnp.bfloat16), 4, 2)
    partial = add32(partial[:, :2], crossed)
    crossed = swap(partial[:, 1].astype(jnp.bfloat16), 2, 4)
    partial = add32(partial[:, 0], crossed)
    home = [swap(partial[i].astype(jnp.bfloat16), 8 * i) for i in range(1, four)]
    mixed = add32(partial[0], *home).astype(jnp.bfloat16)
    return mixed, expert_histogram(codes, energies, blocks)


def plain(packed, me, weight, chosen, blocks):
    rows = lax.all_gather(packed, "expert", axis=0, tiled=True)
    step = LANES if rows.shape[0] % LANES == 0 else packed.shape[0]
    scaled, codes, energies = [], [], []
    for at in range(0, rows.shape[0], step):
        part, code, energy = expert_rows(me, [rows[at : at + step]], weight, chosen, blocks)
        scaled.append(part)
        codes.append(code)
        energies.append(energy)
    mixed = lax.psum_scatter(
        jnp.concatenate(scaled, axis=0).astype(jnp.float32),
        "expert",
        scatter_dimension=0,
        tiled=True,
    )
    return mixed.astype(jnp.bfloat16), expert_histogram(codes, energies, blocks)


def shards(tokens, expert_ids, gate_logits, bin_ids, up_weight):
    chosen, blocks = bin_ids.shape[1:]
    packed = pack_rows(tokens, expert_ids, gate_logits, bin_ids)
    me = lax.axis_index("expert").astype(jnp.int32)[None]
    weight = lax.all_gather(up_weight, "fsdp", axis=1, tiled=True)[0]
    route = boxed if lax.axis_size("expert") == 32 else plain
    mixed, histogram = route(packed, me, weight, chosen, blocks)
    histogram = lax.psum_scatter(histogram[None], "fsdp", scatter_dimension=2, tiled=True)
    return mixed, histogram


def solution(mesh):
    return jax.shard_map(
        shards,
        mesh=mesh,
        in_specs=(
            P(("rep", "expert", "fsdp"), None),
            P(("rep", "expert", "fsdp"), None),
            P(("rep", "expert", "fsdp"), None),
            P(("rep", "expert", "fsdp"), None, None),
            P("expert", "fsdp", None),
        ),
        out_specs=(P(("rep", "expert", "fsdp"), None), P(("rep", "expert"), None, "fsdp")),
        check_vma=False,
    )
```

time: 92.6 us -> 81.9 us (0.88)
  waiting for transfers between devices: 55.7 us -> 26.2 us
  Pallas kernels: 0 us -> 18 us
  matrix products: 15.3 us -> 0 us
  starting transfers between devices: 13.9 us -> 27.6 us
  other arithmetic: 2.46 us -> 4.58 us
    all_to_all x3 -> x0, waiting for transfers between devices: 55.7 us -> none  [the longest x1 42.8 us: shards(): lax.all_to_all(outgoing.reshape(groups, capacity, model_width), 'expert',...]
    ppermute x0 -> x25, starting transfers between devices: none -> 27.6 us  [swap(): lax.ppermute(array, 'expert', [(i, i ^ (odd if i & 1 else even)) for i in...]
    ppermute x0 -> x25, waiting for transfers between devices: none -> 26.2 us  [swap(): lax.ppermute(array, 'expert', [(i, i ^ (odd if i & 1 else even)) for i in...]
    pallas_call x0 -> x5, Pallas kernels: none -> 18 us  [the longest x4 15.5 us: expert_rows(): pl.pallas_call(functools.partial(expert_kernel, chosen, blocks, len(parts...]
    dot_general x11 -> x0, matrix products: 15.3 us -> none  [the longest x8 6.59 us: shards(): jnp.dot(energy[:, block_idx][None, :], onehot, precision=lax.Precision.HI...]
    all_to_all x3 -> x0, starting transfers between devices: 13.9 us -> none  [the longest x1 7.3 us: shards(): lax.all_to_all(out_bins.reshape(groups, capacity, block_count), 'expert',...]
    unnamed x7 -> x16, local copies, waits for them, and re-layouts: 1.85 us -> 3.97 us
    concatenate x0 -> x3, other arithmetic: none -> 1.92 us  [the longest x1 0.93 us: boxed(): half = jnp.concatenate([rows, first, second, third], axis=0)]
  transfers between devices with their start and end apart: 3 -> 25, of which waited for: 3 -> 11; matrix products, arithmetic and copies ran while one was open for 12% -> 1% of each run, Pallas kernels for 0% -> 17%
where the time goes in v1:
time: 81.9 us; the launch traced here: 81.5 us
  starting transfers between devices  27.6 us (34%)
  waiting for transfers between devices  26.2 us (32%)
  Pallas kernels  18 us (22%)
  other arithmetic  4.58 us (6%)
  local copies, waits for them, and re-layouts  4.23 us (5%)
  between operations  0.91 us (1%)
    ppermute x25, starting transfers between devices, swap(): lax.ppermute(array, 'expert', [(i, i ^ (odd if i & 1 else even)) for i in...  27.6 us
    ppermute x25, waiting for transfers between devices, swap(): lax.ppermute(array, 'expert', [(i, i ^ (odd if i & 1 else even)) for i in...  26.2 us
    pallas_call x4, Pallas kernels, expert_rows(): pl.pallas_call(functools.partial(expert_kernel, chosen, blocks, len(parts...  15.5 us
    unnamed x16, local copies, waits for them, and re-layouts  3.97 us
    pallas_call x1, Pallas kernels, expert_histogram(): pl.pallas_call(functools.partial(histogram_kernel, blocks, len(codes)), o...  2.51 us
  transfers between devices with their start and end apart: 25, of which 11 were waited for; matrix products, arithmetic and copies ran while one was open for 1% of the time, Pallas kernels for 17%

profile of v1, /device:TPU:0, one launch (start us, length us, event | category | flops | bytes accessed | tf_op | source)
XLA Modules:
  0.0 81.5 jit_solution(4481972998373394020)
XLA Ops:
  0.6 0.8 copy.23
  1.4 0.1 fusion.12
  1.5 0.1 divide_convert_fusion
  1.6 0.8 fusion.6
  2.4 0.1 copy.27
  2.4 0.7 convert_element_type.59
  3.1 0.1 copy.26
  3.2 0.1 fusion.11
  3.3 0.9 %pad_maximum_fusion.2 = bf16[16,3712]{1,0:T(8,128)(2,1)S(1)} fusion(bf16[16,128]{1,0:T(8,128)(2,1)S(1)} %fusion.11, bf16[16,3584]{1,0:T(8,128)(2,1)} %param.5), kind=kLoop, calls=%fused_computation.9 | loop fusion | flops 237568 | bytes 237568 | tf_op jit(solution)/shard_map/concatenate | solution.py:28
  4.2 3.1 %collective-permute-start.4 = (bf16[16,3712]{1,0:T(8,128)(2,1)S(1)}, bf16[16,3712]{1,0:T(8,128)(2,1)S(1)}, u32[]{:S(2)}, u32[]{:S(2)}) collective-permute-start(bf16[16,3712]{1,0:T(8,128)(2,1)S(1)} %pad_maximum_fusion.2), channel_id=1, source_target_pairs={{0,8},{1,9},{2,10},{3,11},{4,12},{5,13},{6,14},{7,15},{8,0},{9,1},... | collective-permute-start | bytes 356360 | tf_op jit(solution)/shard_map/ppermute | solution.py:166
  7.3 2.6 %collective-permute-start.9 = (bf16[16,3712]{1,0:T(8,128)(2,1)S(1)}, bf16[16,3712]{1,0:T(8,128)(2,1)S(1)}, u32[]{:S(2)}, u32[]{:S(2)}) collective-permute-start(bf16[16,3712]{1,0:T(8,128)(2,1)S(1)} %pad_maximum_fusion.2), channel_id=1, source_target_pairs={{0,16},{1,17},{2,18},{3,19},{4,20},{5,21},{6,22},{7,23},{8,24},{9,... | collective-permute-start | bytes 356360 | tf_op jit(solution)/shard_map/ppermute | solution.py:166
  9.9 0.0 collective-permute-start.14
  9.9 1.7 %collective-permute-start = (bf16[16,3712]{1,0:T(8,128)(2,1)S(1)}, bf16[16,3712]{1,0:T(8,128)(2,1)S(1)}, u32[]{:S(2)}, u32[]{:S(2)}) collective-permute-start(bf16[16,3712]{1,0:T(8,128)(2,1)S(1)} %pad_maximum_fusion.2), channel_id=1, source_target_pairs={{0,2},{1,5},{2,0},{3,7},{4,6},{5,1},{6,4},{7,3},{8,10},{9,13},{10,... | collective-permute-start | bytes 356360 | tf_op jit(solution)/shard_map/ppermute | solution.py:166
  11.6 1.5 %collective-permute-start.1 = (bf16[16,3712]{1,0:T(8,128)(2,1)S(1)}, bf16[16,3712]{1,0:T(8,128)(2,1)S(1)}, u32[]{:S(2)}, u32[]{:S(2)}) collective-permute-start(bf16[16,3712]{1,0:T(8,128)(2,1)S(1)} %pad_maximum_fusion.2), channel_id=1, source_target_pairs={{0,4},{1,3},{2,6},{3,1},{4,0},{5,7},{6,2},{7,5},{8,12},{9,11},{10,... | collective-permute-start | bytes 356360 | tf_op jit(solution)/shard_map/ppermute | solution.py:166
  13.1 0.0 collective-permute-done.4
  13.1 0.5 collective-permute-start.5
  13.7 5.6 %collective-permute-done.9 = bf16[16,3712]{1,0:T(8,128)(2,1)S(1)} collective-permute-done((bf16[16,3712]{1,0:T(8,128)(2,1)S(1)}, bf16[16,3712]{1,0:T(8,128)(2,1)S(1)}, u32[]{:S(2)}, u32[]{:S(2)}) %collective-permute-start.9) | collective-permute-done | bytes 118816 | tf_op jit(solution)/shard_map/ppermute | solution.py:166
  19.3 1.5 %collective-permute-start.6 = (bf16[16,3712]{1,0:T(8,128)(2,1)S(1)}, bf16[16,3712]{1,0:T(8,128)(2,1)S(1)}, u32[]{:S(2)}, u32[]{:S(2)}) collective-permute-start(bf16[16,3712]{1,0:T(8,128)(2,1)S(1)} %collective-permute-done.4), channel_id=1, source_target_pairs={{0,4},{1,3},{2,6},{3,1},{4,0},{5,7},{6,2},{7,5},{8,12},{9,11},{10,... | collective-permute-start | bytes 356360 | tf_op jit(solution)/shard_map/ppermute | solution.py:166
  20.8 0.0 collective-permute-done.14
  20.9 1.6 %collective-permute-start.10 = (bf16[16,3712]{1,0:T(8,128)(2,1)S(1)}, bf16[16,3712]{1,0:T(8,128)(2,1)S(1)}, u32[]{:S(2)}, u32[]{:S(2)}) collective-permute-start(bf16[16,3712]{1,0:T(8,128)(2,1)S(1)} %collective-permute-done.9), channel_id=1, source_target_pairs={{0,2},{1,5},{2,0},{3,7},{4,6},{5,1},{6,4},{7,3},{8,10},{9,13},{10,... | collective-permute-start | bytes 356360 | tf_op jit(solution)/shard_map/ppermute | solution.py:166
  22.4 0.5 collective-permute-start.2
  22.9 0.0 collective-permute-done.1
  22.9 1.6 %collective-permute-start.11 = (bf16[16,3712]{1,0:T(8,128)(2,1)S(1)}, bf16[16,3712]{1,0:T(8,128)(2,1)S(1)}, u32[]{:S(2)}, u32[]{:S(2)}) collective-permute-start(bf16[16,3712]{1,0:T(8,128)(2,1)S(1)} %collective-permute-done.9), channel_id=1, source_target_pairs={{0,4},{1,3},{2,6},{3,1},{4,0},{5,7},{6,2},{7,5},{8,12},{9,11},{10,... | collective-permute-start | bytes 356360 | tf_op jit(solution)/shard_map/ppermute | solution.py:166
  24.5 2.7 %collective-permute-done.2 = bf16[16,3712]{1,0:T(8,128)(2,1)S(1)} collective-permute-done((bf16[16,3712]{1,0:T(8,128)(2,1)S(1)}, bf16[16,3712]{1,0:T(8,128)(2,1)S(1)}, u32[]{:S(2)}, u32[]{:S(2)}) %collective-permute-start.2) | collective-permute-done | bytes 118816 | tf_op jit(solution)/shard_map/ppermute | solution.py:166
  27.3 1.1 %collective-permute-start.15 = (bf16[16,3712]{1,0:T(8,128)(2,1)S(1)}, bf16[16,3712]{1,0:T(8,128)(2,1)S(1)}, u32[]{:S(2)}, u32[]{:S(2)}) collective-permute-start(bf16[16,3712]{1,0:T(8,128)(2,1)S(1)} %collective-permute-done.14), channel_id=1, source_target_pairs={{0,2},{1,5},{2,0},{3,7},{4,6},{5,1},{6,4},{7,3},{8,10},{9,13},{10,... | collective-permute-start | bytes 356360 | tf_op jit(solution)/shard_map/ppermute | solution.py:166
  28.4 0.9 %pad_maximum_fusion.1.refs_0_ = bf16[64,3712]{1,0:T(8,128)(2,1)S(1)} fusion(bf16[16,3712]{1,0:T(8,128)(2,1)S(1)} %collective-permute-done.2, bf16[16,3712]{1,0:T(8,128)(2,1)S(1)} %collective-permute-done.1, bf16[16,3712]{1,0:T(8,128)(2,1)S(1)} %collective-permute-done, bf16[16,128]{1,0:T(8,128)(2,1)S(1)} %fusion.11, bf16[16,3584]{1,0:T(8,128)(2,1)} %param.5), kind=kLoop, calls=%fused_computation.4 | loop fusion | flops 2375680 | bytes 950272 | tf_op jit(solution)/shard_map/concatenate | solution.py:180
  29.3 0.0 collective-permute-done.5
  29.3 1.4 %collective-permute-start.16 = (bf16[16,3712]{1,0:T(8,128)(2,1)S(1)}, bf16[16,3712]{1,0:T(8,128)(2,1)S(1)}, u32[]{:S(2)}, u32[]{:S(2)}) collective-permute-start(bf16[16,3712]{1,0:T(8,128)(2,1)S(1)} %collective-permute-done.14), channel_id=1, source_target_pairs={{0,4},{1,3},{2,6},{3,1},{4,0},{5,7},{6,2},{7,5},{8,12},{9,11},{10,... | collective-permute-start | bytes 356360 | tf_op jit(solution)/shard_map/ppermute | solution.py:166
  30.7 0.0 collective-permute-done.6
  30.7 0.1 collective-permute-start.3
  30.9 0.8 collective-permute-start.7
  31.6 0.4 collective-permute-done.15
  32.1 1.0 %collective-permute-start.12 = (bf16[16,3712]{1,0:T(8,128)(2,1)S(1)}, bf16[16,3712]{1,0:T(8,128)(2,1)S(1)}, u32[]{:S(2)}, u32[]{:S(2)}) collective-permute-start(bf16[16,3712]{1,0:T(8,128)(2,1)S(1)} %collective-permute-done.10), channel_id=1, source_target_pairs={{0,4},{1,3},{2,6},{3,1},{4,0},{5,7},{6,2},{7,5},{8,12},{9,11},{10,... | collective-permute-start | bytes 356360 | tf_op jit(solution)/shard_map/ppermute | solution.py:166
  33.1 1.1 %collective-permute-start.17 = (bf16[16,3712]{1,0:T(8,128)(2,1)S(1)}, bf16[16,3712]{1,0:T(8,128)(2,1)S(1)}, u32[]{:S(2)}, u32[]{:S(2)}) collective-permute-start(bf16[16,3712]{1,0:T(8,128)(2,1)S(1)} %collective-permute-done.15), channel_id=1, source_target_pairs={{0,4},{1,3},{2,6},{3,1},{4,0},{5,7},{6,2},{7,5},{8,12},{9,11},{10,... | collective-permute-start | bytes 356360 | tf_op jit(solution)/shard_map/ppermute | solution.py:166
  34.2 0.0 collective-permute-done.16
  34.3 1.5 %collective-permute-done.7 = bf16[16,3712]{1,0:T(8,128)(2,1)S(1)} collective-permute-done((bf16[16,3712]{1,0:T(8,128)(2,1)S(1)}, bf16[16,3712]{1,0:T(8,128)(2,1)S(1)}, u32[]{:S(2)}, u32[]{:S(2)}) %collective-permute-start.7) | collective-permute-done | bytes 118816 | tf_op jit(solution)/shard_map/ppermute | solution.py:166
  35.8 0.1 collective-permute-start.8
  35.8 1.2 %collective-permute-done.12 = bf16[16,3712]{1,0:T(8,128)(2,1)S(1)} collective-permute-done((bf16[16,3712]{1,0:T(8,128)(2,1)S(1)}, bf16[16,3712]{1,0:T(8,128)(2,1)S(1)}, u32[]{:S(2)}, u32[]{:S(2)}) %collective-permute-start.12) | collective-permute-done | bytes 118816 | tf_op jit(solution)/shard_map/ppermute | solution.py:166
  37.0 0.1 collective-permute-start.13
  37.1 1.2 %collective-permute-done.17 = bf16[16,3712]{1,0:T(8,128)(2,1)S(1)} collective-permute-done((bf16[16,3712]{1,0:T(8,128)(2,1)S(1)}, bf16[16,3712]{1,0:T(8,128)(2,1)S(1)}, u32[]{:S(2)}, u32[]{:S(2)}) %collective-permute-start.17) | collective-permute-done | bytes 118816 | tf_op jit(solution)/shard_map/ppermute | solution.py:166
  38.3 0.1 collective-permute-start.18
  38.4 0.0 copy-start
  38.4 3.1 %copy-done = bf16[1,3584,1024]{2,1,0:T(8,128)(2,1)S(1)} copy-done((bf16[1,3584,1024]{2,1,0:T(8,128)(2,1)S(1)}, bf16[1,3584,1024]{2,1,0:T(8,128)(2,1)}, u32[]{:S(2)}) %copy-start) | copy-done | bytes 7340056
  41.5 3.7 %expert_rows.4 = (bf16[64,1024]{1,0:T(8,128)(2,1)S(1)}, bf16[64,1024]{1,0:T(8,128)(2,1)S(1)}, f32[128,128]{1,0:T(8,128)S(1)}, f32[128,128]{1,0:T(8,128)S(1)}) custom-call(s32[1]{0:T(128)} %bitcast.me_ref, bf16[64,3712]{1,0:T(8,128)(2,1)S(1)} %pad_maximum_fusion.1.refs_0_, bf16[64,3712]{1,0:T(8,128)(2,1)S(1)} %collective-permute-done.3.refs_1_, ...), custom_call_target="tpu_custom_call" | custom-call | flops 939524096 | bytes 7340032 | tf_op jit(solution)/shard_map/expert_rows/pallas_call | solution.py:84
  45.2 0.0 slice-start.1
  45.2 3.7 %expert_rows.5 = (bf16[64,1024]{1,0:T(8,128)(2,1)S(1)}, bf16[64,1024]{1,0:T(8,128)(2,1)S(1)}, f32[128,128]{1,0:T(8,128)S(1)}, f32[128,128]{1,0:T(8,128)S(1)}) custom-call(s32[1]{0:T(128)} %bitcast.me_ref, bf16[64,3712]{1,0:T(8,128)(2,1)S(1)} %constant_dynamic-update-slice_fusion.refs_0_, bf16[64,3712]{1,0:T(8,128)(2,1)S(1)} %collective-permute-done.8.refs_1_, ...), custom_call_target="tpu_custom_call" | custom-call | flops 939524096 | bytes 7340032 | tf_op jit(solution)/shard_map/expert_rows/pallas_call | solution.py:84
  48.9 3.7 %expert_rows.6 = (bf16[64,1024]{1,0:T(8,128)(2,1)S(1)}, bf16[64,1024]{1,0:T(8,128)(2,1)S(1)}, f32[128,128]{1,0:T(8,128)S(1)}, f32[128,128]{1,0:T(8,128)S(1)}) custom-call(s32[1]{0:T(128)} %bitcast.me_ref, bf16[64,3712]{1,0:T(8,128)(2,1)S(1)} %constant_dynamic-update-slice_fusion.4.refs_0_, bf16[64,3712]{1,0:T(8,128)(2,1)S(1)} %collective-permute-done.13.refs_1_, ...), custom_call_target="tpu_custom_call" | custom-call | flops 939524096 | bytes 7340032 | tf_op jit(solution)/shard_map/expert_rows/pallas_call | solution.py:84
  52.6 4.5 %expert_rows.7 = (bf16[64,1024]{1,0:T(8,128)(2,1)S(1)}, bf16[64,1024]{1,0:T(8,128)(2,1)S(1)}, f32[128,128]{1,0:T(8,128)S(1)}, f32[128,128]{1,0:T(8,128)S(1)}) custom-call(s32[1]{0:T(128)} %bitcast.me_ref, bf16[64,3712]{1,0:T(8,128)(2,1)S(1)} %constant_dynamic-update-slice_fusion.8.refs_0_, bf16[64,3712]{1,0:T(8,128)(2,1)} %collective-permute-done.18.refs_1_, ...), custom_call_target="tpu_custom_call" | custom-call | flops 939524096 | bytes 7340032 | tf_op jit(solution)/shard_map/expert_rows/pallas_call | solution.py:84
  57.1 0.1 pad_maximum_fusion
  57.1 0.6 collective-permute-start.19
  57.7 1.5 %collective-permute-done.19 = bf16[4,64,1024]{2,1,0:T(8,128)(2,1)S(1)} collective-permute-done((bf16[4,64,1024]{2,1,0:T(8,128)(2,1)S(1)}, bf16[4,64,1024]{2,1,0:T(8,128)(2,1)S(1)}, u32[]{:S(2)}, u32[]{:S(2)}) %collective-permute-start.19) | collective-permute-done | bytes 524320 | tf_op jit(solution)/shard_map/ppermute | solution.py:166
  59.2 0.2 copy_add_fusion
  59.5 1.1 %collective-permute-start.20 = (bf16[4,2,16,1024]{3,2,0,1:T(8,128)(2,1)S(1)}, bf16[4,2,16,1024]{3,2,0,1:T(8,128)(2,1)S(1)}, u32[]{:S(2)}, u32[]{:S(2)}) collective-permute-start(bf16[4,2,16,1024]{3,2,0,1:T(8,128)(2,1)S(1)} %slice.65), channel_id=1, source_target_pairs={{0,4},{1,3},{2,6},{3,1},{4,0},{5,7},{6,2},{7,5},{8,12},{9,11},{10,... | collective-permute-start | bytes 786440 | tf_op jit(solution)/shard_map/ppermute | solution.py:166
  60.6 5.3 %collective-permute-done.20 = bf16[4,2,16,1024]{3,2,0,1:T(8,128)(2,1)S(1)} collective-permute-done((bf16[4,2,16,1024]{3,2,0,1:T(8,128)(2,1)S(1)}, bf16[4,2,16,1024]{3,2,0,1:T(8,128)(2,1)S(1)}, u32[]{:S(2)}, u32[]{:S(2)}) %collective-permute-start.20) | collective-permute-done | bytes 262176 | tf_op jit(solution)/shard_map/ppermute | solution.py:166
  65.9 0.1 slice_add_fusion
  66.0 1.2 %collective-permute-start.21 = (bf16[4,16,1024]{2,1,0:T(8,128)(2,1)S(1)}, bf16[4,16,1024]{2,1,0:T(8,128)(2,1)S(1)}, u32[]{:S(2)}, u32[]{:S(2)}) collective-permute-start(bf16[4,16,1024]{2,1,0:T(8,128)(2,1)S(1)} %fusion.1), channel_id=1, source_target_pairs={{0,2},{1,5},{2,0},{3,7},{4,6},{5,1},{6,4},{7,3},{8,10},{9,13},{10,... | collective-permute-start | bytes 393224 | tf_op jit(solution)/shard_map/ppermute | solution.py:166
  67.2 3.8 %collective-permute-done.21 = bf16[4,16,1024]{2,1,0:T(8,128)(2,1)S(1)} collective-permute-done((bf16[4,16,1024]{2,1,0:T(8,128)(2,1)S(1)}, bf16[4,16,1024]{2,1,0:T(8,128)(2,1)S(1)}, u32[]{:S(2)}, u32[]{:S(2)}) %collective-permute-start.21) | collective-permute-done | bytes 131104 | tf_op jit(solution)/shard_map/ppermute | solution.py:166
  71.1 1.6 %collective-permute-start.22 = (bf16[16,1024]{1,0:T(8,128)(2,1)S(1)}, bf16[16,1024]{1,0:T(8,128)(2,1)S(1)}, u32[]{:S(2)}, u32[]{:S(2)}) collective-permute-start(bf16[16,1024]{1,0:T(8,128)(2,1)S(1)} %get-tuple-element.36), channel_id=1, source_target_pairs={{0,8},{1,9},{2,10},{3,11},{4,12},{5,13},{6,14},{7,15},{8,0},{9,1},... | collective-permute-start | bytes 98312 | tf_op jit(solution)/shard_map/ppermute | solution.py:166
  72.6 2.5 %collective-permute-start.23 = (bf16[16,1024]{1,0:T(8,128)(2,1)S(1)}, bf16[16,1024]{1,0:T(8,128)(2,1)S(1)}, u32[]{:S(2)}, u32[]{:S(2)}) collective-permute-start(bf16[16,1024]{1,0:T(8,128)(2,1)S(1)} %get-tuple-element.38), channel_id=1, source_target_pairs={{0,16},{1,17},{2,18},{3,19},{4,20},{5,21},{6,22},{7,23},{8,24},{9,... | collective-permute-start | bytes 98312 | tf_op jit(solution)/shard_map/ppermute | solution.py:166
  75.2 0.3 collective-permute-start.24
  75.5 2.5 %expert_histogram.1 = f32[8,2048]{1,0:T(8,128)} custom-call(f32[128,128]{1,0:T(8,128)S(1)} %get-tuple-element.26.refs_0_, f32[128,128]{1,0:T(8,128)S(1)} %get-tuple-element.27.refs_1_, f32[128,128]{1,0:T(8,128)S(1)} %get-tuple-element.28.refs_2_, f32[128,128]{1,0:T(8,128)S(1)} %get-tuple-element.29.refs_3_, f32[128,128]{1,0:T(8,128)S(1)} %get-tuple-element.30.refs_4_, ...), custom_call_target="tpu_custom_call" | custom-call | flops 268435456 | bytes 524288 | tf_op jit(solution)/shard_map/expert_histogram/pallas_call | solution.py:150
  78.0 0.1 collective-permute-done.23
  78.1 2.8 %collective-permute-done.24 = bf16[16,1024]{1,0:T(8,128)(2,1)S(1)} collective-permute-done((bf16[16,1024]{1,0:T(8,128)(2,1)S(1)}, bf16[16,1024]{1,0:T(8,128)(2,1)S(1)}, u32[]{:S(2)}, u32[]{:S(2)}) %collective-permute-start.24) | collective-permute-done | bytes 32800 | tf_op jit(solution)/shard_map/ppermute | solution.py:166
  80.9 0.6 fusion.5
  (28 shorter events, 0.3 us)
Async XLA Ops:
  4.2 8.9 %collective-permute-start.4 = (bf16[16,3712]{1,0:T(8,128)(2,1)S(1)}, bf16[16,3712]{1,0:T(8,128)(2,1)S(1)}, u32[]{:S(2)}, u32[]{:S(2)}) collective-permute-start(bf16[16,3712]{1,0:T(8,128)(2,1)S(1)} %pad_maximum_fusion.2), channel_id=1, source_target_pairs={{0,8},{1,9},{2,10},{3,11},{4,12},{5,13},{6,14},{7,15},{8,0},{9,1},... | collective-permute-start | bytes 356360 | tf_op jit(solution)/shard_map/ppermute | solution.py:166
  7.3 12.0 %collective-permute-start.9 = (bf16[16,3712]{1,0:T(8,128)(2,1)S(1)}, bf16[16,3712]{1,0:T(8,128)(2,1)S(1)}, u32[]{:S(2)}, u32[]{:S(2)}) collective-permute-start(bf16[16,3712]{1,0:T(8,128)(2,1)S(1)} %pad_maximum_fusion.2), channel_id=1, source_target_pairs={{0,16},{1,17},{2,18},{3,19},{4,20},{5,21},{6,22},{7,23},{8,24},{9,... | collective-permute-start | bytes 356360 | tf_op jit(solution)/shard_map/ppermute | solution.py:166
  9.9 10.9 %collective-permute-start.14 = (bf16[16,3712]{1,0:T(8,128)(2,1)S(1)}, bf16[16,3712]{1,0:T(8,128)(2,1)S(1)}, u32[]{:S(2)}, u32[]{:S(2)}) collective-permute-start(bf16[16,3712]{1,0:T(8,128)(2,1)S(1)} %pad_maximum_fusion.2), channel_id=1, source_target_pairs={{0,24},{1,25},{2,26},{3,27},{4,28},{5,29},{6,30},{7,31},{8,16},{9,... | collective-permute-start | bytes 356360 | tf_op jit(solution)/shard_map/ppermute | solution.py:166
  9.9 12.5 %collective-permute-start = (bf16[16,3712]{1,0:T(8,128)(2,1)S(1)}, bf16[16,3712]{1,0:T(8,128)(2,1)S(1)}, u32[]{:S(2)}, u32[]{:S(2)}) collective-permute-start(bf16[16,3712]{1,0:T(8,128)(2,1)S(1)} %pad_maximum_fusion.2), channel_id=1, source_target_pairs={{0,2},{1,5},{2,0},{3,7},{4,6},{5,1},{6,4},{7,3},{8,10},{9,13},{10,... | collective-permute-start | bytes 356360 | tf_op jit(solution)/shard_map/ppermute | solution.py:166
  11.6 11.3 %collective-permute-start.1 = (bf16[16,3712]{1,0:T(8,128)(2,1)S(1)}, bf16[16,3712]{1,0:T(8,128)(2,1)S(1)}, u32[]{:S(2)}, u32[]{:S(2)}) collective-permute-start(bf16[16,3712]{1,0:T(8,128)(2,1)S(1)} %pad_maximum_fusion.2), channel_id=1, source_target_pairs={{0,4},{1,3},{2,6},{3,1},{4,0},{5,7},{6,2},{7,5},{8,12},{9,11},{10,... | collective-permute-start | bytes 356360 | tf_op jit(solution)/shard_map/ppermute | solution.py:166
  13.1 16.2 %collective-permute-start.5 = (bf16[16,3712]{1,0:T(8,128)(2,1)S(1)}, bf16[16,3712]{1,0:T(8,128)(2,1)S(1)}, u32[]{:S(2)}, u32[]{:S(2)}) collective-permute-start(bf16[16,3712]{1,0:T(8,128)(2,1)S(1)} %collective-permute-done.4), channel_id=1, source_target_pairs={{0,2},{1,5},{2,0},{3,7},{4,6},{5,1},{6,4},{7,3},{8,10},{9,13},{10,... | collective-permute-start | bytes 356360 | tf_op jit(solution)/shard_map/ppermute | solution.py:166
  19.3 11.4 %collective-permute-start.6 = (bf16[16,3712]{1,0:T(8,128)(2,1)S(1)}, bf16[16,3712]{1,0:T(8,128)(2,1)S(1)}, u32[]{:S(2)}, u32[]{:S(2)}) collective-permute-start(bf16[16,3712]{1,0:T(8,128)(2,1)S(1)} %collective-permute-done.4), channel_id=1, source_target_pairs={{0,4},{1,3},{2,6},{3,1},{4,0},{5,7},{6,2},{7,5},{8,12},{9,11},{10,... | collective-permute-start | bytes 356360 | tf_op jit(solution)/shard_map/ppermute | solution.py:166
  20.9 10.0 %collective-permute-start.10 = (bf16[16,3712]{1,0:T(8,128)(2,1)S(1)}, bf16[16,3712]{1,0:T(8,128)(2,1)S(1)}, u32[]{:S(2)}, u32[]{:S(2)}) collective-permute-start(bf16[16,3712]{1,0:T(8,128)(2,1)S(1)} %collective-permute-done.9), channel_id=1, source_target_pairs={{0,2},{1,5},{2,0},{3,7},{4,6},{5,1},{6,4},{7,3},{8,10},{9,13},{10,... | collective-permute-start | bytes 356360 | tf_op jit(solution)/shard_map/ppermute | solution.py:166
  22.4 4.8 %collective-permute-start.2 = (bf16[16,3712]{1,0:T(8,128)(2,1)S(1)}, bf16[16,3712]{1,0:T(8,128)(2,1)S(1)}, u32[]{:S(2)}, u32[]{:S(2)}) collective-permute-start(bf16[16,3712]{1,0:T(8,128)(2,1)S(1)} %collective-permute-done), channel_id=1, source_target_pairs={{0,4},{1,3},{2,6},{3,1},{4,0},{5,7},{6,2},{7,5},{8,12},{9,11},{10,... | collective-permute-start | bytes 356360 | tf_op jit(solution)/shard_map/ppermute | solution.py:166
  22.9 10.1 %collective-permute-start.11 = (bf16[16,3712]{1,0:T(8,128)(2,1)S(1)}, bf16[16,3712]{1,0:T(8,128)(2,1)S(1)}, u32[]{:S(2)}, u32[]{:S(2)}) collective-permute-start(bf16[16,3712]{1,0:T(8,128)(2,1)S(1)} %collective-permute-done.9), channel_id=1, source_target_pairs={{0,4},{1,3},{2,6},{3,1},{4,0},{5,7},{6,2},{7,5},{8,12},{9,11},{10,... | collective-permute-start | bytes 356360 | tf_op jit(solution)/shard_map/ppermute | solution.py:166
  27.3 4.8 %collective-permute-start.15 = (bf16[16,3712]{1,0:T(8,128)(2,1)S(1)}, bf16[16,3712]{1,0:T(8,128)(2,1)S(1)}, u32[]{:S(2)}, u32[]{:S(2)}) collective-permute-start(bf16[16,3712]{1,0:T(8,128)(2,1)S(1)} %collective-permute-done.14), channel_id=1, source_target_pairs={{0,2},{1,5},{2,0},{3,7},{4,6},{5,1},{6,4},{7,3},{8,10},{9,13},{10,... | collective-permute-start | bytes 356360 | tf_op jit(solution)/shard_map/ppermute | solution.py:166
  29.3 4.9 %collective-permute-start.16 = (bf16[16,3712]{1,0:T(8,128)(2,1)S(1)}, bf16[16,3712]{1,0:T(8,128)(2,1)S(1)}, u32[]{:S(2)}, u32[]{:S(2)}) collective-permute-start(bf16[16,3712]{1,0:T(8,128)(2,1)S(1)} %collective-permute-done.14), channel_id=1, source_target_pairs={{0,4},{1,3},{2,6},{3,1},{4,0},{5,7},{6,2},{7,5},{8,12},{9,11},{10,... | collective-permute-start | bytes 356360 | tf_op jit(solution)/shard_map/ppermute | solution.py:166
  30.7 7.7 %collective-permute-start.3 = (bf16[64,3712]{1,0:T(8,128)(2,1)S(1)}, bf16[64,3712]{1,0:T(8,128)(2,1)S(1)}, u32[]{:S(2)}, u32[]{:S(2)}) collective-permute-start(bf16[64,3712]{1,0:T(8,128)(2,1)S(1)} %pad_maximum_fusion.1.refs_0_), channel_id=1, source_target_pairs={{0,1},{1,0},{2,3},{3,2},{4,5},{5,4},{6,7},{7,6},{8,9},{9,8},{10,11... | collective-permute-start | bytes 1425416 | tf_op jit(solution)/shard_map/ppermute | solution.py:166
  30.9 4.9 %collective-permute-start.7 = (bf16[16,3712]{1,0:T(8,128)(2,1)S(1)}, bf16[16,3712]{1,0:T(8,128)(2,1)S(1)}, u32[]{:S(2)}, u32[]{:S(2)}) collective-permute-start(bf16[16,3712]{1,0:T(8,128)(2,1)S(1)} %collective-permute-done.5), channel_id=1, source_target_pairs={{0,4},{1,3},{2,6},{3,1},{4,0},{5,7},{6,2},{7,5},{8,12},{9,11},{10,... | collective-permute-start | bytes 356360 | tf_op jit(solution)/shard_map/ppermute | solution.py:166
  32.1 4.9 %collective-permute-start.12 = (bf16[16,3712]{1,0:T(8,128)(2,1)S(1)}, bf16[16,3712]{1,0:T(8,128)(2,1)S(1)}, u32[]{:S(2)}, u32[]{:S(2)}) collective-permute-start(bf16[16,3712]{1,0:T(8,128)(2,1)S(1)} %collective-permute-done.10), channel_id=1, source_target_pairs={{0,4},{1,3},{2,6},{3,1},{4,0},{5,7},{6,2},{7,5},{8,12},{9,11},{10,... | collective-permute-start | bytes 356360 | tf_op jit(solution)/shard_map/ppermute | solution.py:166
  33.1 5.2 %collective-permute-start.17 = (bf16[16,3712]{1,0:T(8,128)(2,1)S(1)}, bf16[16,3712]{1,0:T(8,128)(2,1)S(1)}, u32[]{:S(2)}, u32[]{:S(2)}) collective-permute-start(bf16[16,3712]{1,0:T(8,128)(2,1)S(1)} %collective-permute-done.15), channel_id=1, source_target_pairs={{0,4},{1,3},{2,6},{3,1},{4,0},{5,7},{6,2},{7,5},{8,12},{9,11},{10,... | collective-permute-start | bytes 356360 | tf_op jit(solution)/shard_map/ppermute | solution.py:166
  35.8 9.4 %collective-permute-start.8 = (bf16[64,3712]{1,0:T(8,128)(2,1)S(1)}, bf16[64,3712]{1,0:T(8,128)(2,1)S(1)}, u32[]{:S(2)}, u32[]{:S(2)}) collective-permute-start(bf16[64,3712]{1,0:T(8,128)(2,1)S(1)} %constant_dynamic-update-slice_fusion.refs_0_), channel_id=1, source_target_pairs={{0,1},{1,0},{2,3},{3,2},{4,5},{5,4},{6,7},{7,6},{8,9},{9,8},{10,11... | collective-permute-start | bytes 1425416 | tf_op jit(solution)/shard_map/ppermute | solution.py:166
  37.0 11.8 %collective-permute-start.13 = (bf16[64,3712]{1,0:T(8,128)(2,1)S(1)}, bf16[64,3712]{1,0:T(8,128)(2,1)S(1)}, u32[]{:S(2)}, u32[]{:S(2)}) collective-permute-start(bf16[64,3712]{1,0:T(8,128)(2,1)S(1)} %constant_dynamic-update-slice_fusion.4.refs_0_), channel_id=1, source_target_pairs={{0,1},{1,0},{2,3},{3,2},{4,5},{5,4},{6,7},{7,6},{8,9},{9,8},{10,11... | collective-permute-start | bytes 1425416 | tf_op jit(solution)/shard_map/ppermute | solution.py:166
  38.3 14.2 %collective-permute-start.18 = (bf16[64,3712]{1,0:T(8,128)(2,1)S(1)}, bf16[64,3712]{1,0:T(8,128)(2,1)}, u32[]{:S(2)}, u32[]{:S(2)}) collective-permute-start(bf16[64,3712]{1,0:T(8,128)(2,1)S(1)} %constant_dynamic-update-slice_fusion.8.refs_0_), channel_id=1, source_target_pairs={{0,1},{1,0},{2,3},{3,2},{4,5},{5,4},{6,7},{7,6},{8,9},{9,8},{10,11... | collective-permute-start | bytes 1425416 | tf_op jit(solution)/shard_map/ppermute | solution.py:166
  38.4 3.1 %copy-start = (bf16[1,3584,1024]{2,1,0:T(8,128)(2,1)S(1)}, bf16[1,3584,1024]{2,1,0:T(8,128)(2,1)}, u32[]{:S(2)}) copy-start(bf16[1,3584,1024]{2,1,0:T(8,128)(2,1)} %param.9) | copy-start | bytes 22020100
  41.5 11.1 %slice-start = ((s8[7340032]{0:T(1024)(128)(4,1)}), s8[4194304]{0:T(1024)(128)(4,1)S(1)}, s32[]{:S(2)}) async-start(s8[7340032]{0:T(1024)(128)(4,1)} %bitcast.49), calls=%async_computation | async-start | bytes 8388608
  45.2 7.4 %slice-start.1 = ((s8[7340032]{0:T(1024)(128)(4,1)}), s8[3145728]{0:T(1024)(128)(4,1)S(1)}, s32[]{:S(2)}) async-start(s8[7340032]{0:T(1024)(128)(4,1)} %bitcast.49), calls=%async_computation.1 | async-start | bytes 6291456
  57.1 2.1 %collective-permute-start.19 = (bf16[4,64,1024]{2,1,0:T(8,128)(2,1)S(1)}, bf16[4,64,1024]{2,1,0:T(8,128)(2,1)S(1)}, u32[]{:S(2)}, u32[]{:S(2)}) collective-permute-start(bf16[4,64,1024]{2,1,0:T(8,128)(2,1)S(1)} %pad_maximum_fusion), channel_id=1, source_target_pairs={{0,1},{1,0},{2,3},{3,2},{4,5},{5,4},{6,7},{7,6},{8,9},{9,8},{10,11... | collective-permute-start | bytes 1572872 | tf_op jit(solution)/shard_map/ppermute | solution.py:166
  59.5 6.4 %collective-permute-start.20 = (bf16[4,2,16,1024]{3,2,0,1:T(8,128)(2,1)S(1)}, bf16[4,2,16,1024]{3,2,0,1:T(8,128)(2,1)S(1)}, u32[]{:S(2)}, u32[]{:S(2)}) collective-permute-start(bf16[4,2,16,1024]{3,2,0,1:T(8,128)(2,1)S(1)} %slice.65), channel_id=1, source_target_pairs={{0,4},{1,3},{2,6},{3,1},{4,0},{5,7},{6,2},{7,5},{8,12},{9,11},{10,... | collective-permute-start | bytes 786440 | tf_op jit(solution)/shard_map/ppermute | solution.py:166
  66.0 5.0 %collective-permute-start.21 = (bf16[4,16,1024]{2,1,0:T(8,128)(2,1)S(1)}, bf16[4,16,1024]{2,1,0:T(8,128)(2,1)S(1)}, u32[]{:S(2)}, u32[]{:S(2)}) collective-permute-start(bf16[4,16,1024]{2,1,0:T(8,128)(2,1)S(1)} %fusion.1), channel_id=1, source_target_pairs={{0,2},{1,5},{2,0},{3,7},{4,6},{5,1},{6,4},{7,3},{8,10},{9,13},{10,... | collective-permute-start | bytes 393224 | tf_op jit(solution)/shard_map/ppermute | solution.py:166
  71.1 7.0 %collective-permute-start.22 = (bf16[16,1024]{1,0:T(8,128)(2,1)S(1)}, bf16[16,1024]{1,0:T(8,128)(2,1)S(1)}, u32[]{:S(2)}, u32[]{:S(2)}) collective-permute-start(bf16[16,1024]{1,0:T(8,128)(2,1)S(1)} %get-tuple-element.36), channel_id=1, source_target_pairs={{0,8},{1,9},{2,10},{3,11},{4,12},{5,13},{6,14},{7,15},{8,0},{9,1},... | collective-permute-start | bytes 98312 | tf_op jit(solution)/shard_map/ppermute | solution.py:166
  72.6 5.5 %collective-permute-start.23 = (bf16[16,1024]{1,0:T(8,128)(2,1)S(1)}, bf16[16,1024]{1,0:T(8,128)(2,1)S(1)}, u32[]{:S(2)}, u32[]{:S(2)}) collective-permute-start(bf16[16,1024]{1,0:T(8,128)(2,1)S(1)} %get-tuple-element.38), channel_id=1, source_target_pairs={{0,16},{1,17},{2,18},{3,19},{4,20},{5,21},{6,22},{7,23},{8,24},{9,... | collective-permute-start | bytes 98312 | tf_op jit(solution)/shard_map/ppermute | solution.py:166
  75.2 5.7 %collective-permute-start.24 = (bf16[16,1024]{1,0:T(8,128)(2,1)S(1)}, bf16[16,1024]{1,0:T(8,128)(2,1)S(1)}, u32[]{:S(2)}, u32[]{:S(2)}) collective-permute-start(bf16[16,1024]{1,0:T(8,128)(2,1)S(1)} %get-tuple-element.37), channel_id=1, source_target_pairs={{0,24},{1,25},{2,26},{3,27},{4,28},{5,29},{6,30},{7,31},{8,16},{9,... | collective-permute-start | bytes 98312 | tf_op jit(solution)/shard_map/ppermute | solution.py:166

commit v2 on v1

--- a/solution.py
+++ b/solution.py
@@ -11,89 +11,133 @@
 NBINS = 2048
 LANES = 128
 TILE_N = 256
+K_SLICES = 7
 
 route_scale = 2.827
 
 
+def pack_kernel(tokens_ref, ids_ref, logits_ref, bins_ref, out_ref):
+    tok_rows, width = tokens_ref.shape
+    scores = jax.nn.sigmoid(logits_ref[...])
+    route_weight = route_scale * scores / jnp.sum(scores, axis=0, keepdims=True)
+    bins = bins_ref[...]
+    code = ((128 + (bins & 127)) << (bins >> 7)).astype(jnp.float32)
+    used = 2 * ids_ref.shape[0] + bins.shape[0]
+    tail = jnp.concatenate(
+        [
+            ids_ref[...].astype(jnp.float32),
+            route_weight,
+            code,
+            jnp.zeros((LANES - used, tok_rows), jnp.float32),
+        ],
+        axis=0,
+    ).astype(jnp.bfloat16)
+    row = lax.broadcasted_iota(jnp.int32, (LANES, LANES), 0)
+    col = lax.broadcasted_iota(jnp.int32, (LANES, LANES), 1)
+    unit = jnp.where(row == col, 1.0, 0.0).astype(jnp.bfloat16)
+    turned = lax.dot_general(
+        tail, unit, (((0,), (0,)), ((), ())), preferred_element_type=jnp.float32
+    )
+    out_ref[:, :width] = tokens_ref[...]
+    out_ref[:, width:] = turned.astype(jnp.bfloat16)
+
+
 def pack_rows(tokens, expert_ids, gate_logits, bin_ids):
-    tok_rows, chosen = expert_ids.shape
-    scores = jax.nn.sigmoid(gate_logits)
-    route_weight = (route_scale * scores / jnp.sum(scores, axis=1, keepdims=True)).astype(
-        jnp.bfloat16
-    )
-    bins = bin_ids.reshape(tok_rows, -1)
-    code = ((128 + (bins & 127)) << (bins >> 7)).astype(jnp.float32).astype(jnp.bfloat16)
-    tail = jnp.concatenate([expert_ids.astype(jnp.bfloat16), route_weight, code], axis=1)
-    tail = jnp.pad(tail, ((0, 0), (0, LANES - tail.shape[1])))
-    return jnp.concatenate([tokens, tail], axis=1)
+    tok_rows, width = tokens.shape
+    return pl.pallas_call(
+        pack_kernel,
+        out_shape=jax.ShapeDtypeStruct((tok_rows, width + LANES), jnp.bfloat16),
+        name="pack_rows",
+    )(
+        tokens,
+        expert_ids.T,
+        gate_logits.T,
+        jnp.transpose(bin_ids, (1, 2, 0)).reshape(-1, tok_rows),
+    )
 
 
 def expert_kernel(chosen, blocks, n_parts, me_ref, *refs):
     parts = refs[:n_parts]
     w_ref = refs[n_parts]
     outs = refs[n_parts + 1 : 2 * n_parts + 1]
-    code_ref, energy_ref = refs[2 * n_parts + 1 : 2 * n_parts + 3]
-    step = pl.program_id(0)
-    width, tile = w_ref.shape
-
-    @pl.when(step == 0)
-    def _():
-        tail = jnp.concatenate([p[:, width:] for p in parts], axis=0)
-        row = lax.broadcasted_iota(jnp.int32, (LANES, LANES), 0)
-        col = lax.broadcasted_iota(jnp.int32, (LANES, LANES), 1)
-        bins_at = 2 * chosen
-        bins_end = bins_at + chosen * blocks
-        choice = jnp.where(col < bins_at, col - chosen, (col - bins_at) // blocks)
-        carries = (col >= chosen) & (col < bins_end)
-        spread = jnp.where((row == choice) & carries, 1.0, 0.0).astype(jnp.bfloat16)
-        ids = jnp.dot(tail, spread, preferred_element_type=jnp.float32)
-        lane = lax.broadcasted_iota(jnp.int32, tail.shape, 1)
-        mine = (
-            (ids == me_ref[0].astype(jnp.float32)) & (lane >= chosen) & (lane < bins_end)
+    code_ref, energy_ref, held, up_ref, sems = refs[2 * n_parts + 1 :]
+    width, hidden = w_ref.shape
+    tile = min(TILE_N, hidden)
+    slices = sems.shape[0]
+    depth = width // slices
+    copies = [
+        pltpu.make_async_copy(
+            w_ref.at[pl.ds(i * depth, depth)], held.at[pl.ds(i * depth, depth)], sems.at[i]
         )
-        picked = jnp.where(mine, tail, jnp.zeros_like(tail))
-        target = jnp.where(row < bins_at, blocks, (row - bins_at) % blocks)
-        usable = (row >= chosen) & (row < bins_end)
-        fold = jnp.where((col == target) & usable, 1.0, 0.0).astype(jnp.bfloat16)
-        code_ref[...] = jnp.dot(picked, fold, preferred_element_type=jnp.float32)
-        energy_ref[...] = jnp.zeros_like(energy_ref)
-
-    rows = jnp.concatenate([p[:, :width] for p in parts], axis=0)
-    up = jnp.dot(rows, w_ref[...], preferred_element_type=jnp.float32)
+        for i in range(slices)
+    ]
+    for copy in copies:
+        copy.start()
+
+    tail = jnp.concatenate([p[:, width:] for p in parts], axis=0)
+    row = lax.broadcasted_iota(jnp.int32, (LANES, LANES), 0)
+    col = lax.broadcasted_iota(jnp.int32, (LANES, LANES), 1)
+    bins_at = 2 * chosen
+    bins_end = bins_at + chosen * blocks
+    choice = jnp.where(col < bins_at, col - chosen, (col - bins_at) // blocks)
+    carries = (col >= chosen) & (col < bins_end)
+    spread = jnp.where((row == choice) & carries, 1.0, 0.0).astype(jnp.bfloat16)
+    ids = jnp.dot(tail, spread, preferred_element_type=jnp.float32)
+    lane = lax.broadcasted_iota(jnp.int32, tail.shape, 1)
+    mine = (ids == me_ref[0].astype(jnp.float32)) & (lane >= chosen) & (lane < bins_end)
+    picked = jnp.where(mine, tail.astype(jnp.float32), 0.0).astype(jnp.bfloat16)
+    target = jnp.where(row < bins_at, blocks, (row - bins_at) % blocks)
+    usable = (row >= chosen) & (row < bins_end)
+    fold = jnp.where((col == target) & usable, 1.0, 0.0).astype(jnp.bfloat16)
+    code = jnp.dot(picked, fold, preferred_element_type=jnp.float32)
+    code_ref[...] = code
+    weight = code[:, blocks : blocks + 1]
+
+    energy = jnp.zeros(energy_ref.shape, jnp.float32)
     unit = lax.broadcasted_iota(jnp.int32, (tile, LANES), 0)
-    lane = lax.broadcasted_iota(jnp.int32, (tile, LANES), 1)
-    mean = jnp.where(
-        (unit + step * tile) // BLOCK == lane % blocks, 1.0 / BLOCK, 0.0
-    ).astype(jnp.bfloat16)
-    energy_ref[...] += jnp.dot(
-        (up * up).astype(jnp.bfloat16), mean, preferred_element_type=jnp.float32
-    )
-    weight = code_ref[:, blocks : blocks + 1]
-    scaled = (weight * up.astype(jnp.bfloat16).astype(jnp.float32)).astype(jnp.bfloat16)
-    at = 0
-    for part, out in zip(parts, outs):
-        out[...] = scaled[at : at + part.shape[0]]
-        at += part.shape[0]
+    slot = lax.broadcasted_iota(jnp.int32, (tile, LANES), 1) % blocks
+    for i, copy in enumerate(copies):
+        copy.wait()
+        span = slice(i * depth, (i + 1) * depth)
+        rows = jnp.concatenate([p[:, span] for p in parts], axis=0)
+        for j in range(0, hidden, tile):
+            term = jnp.dot(rows, held[span, j : j + tile], preferred_element_type=jnp.float32)
+            up_ref[:, j : j + tile] = term if i == 0 else up_ref[:, j : j + tile] + term
+    for i in range(hidden // tile):
+        up = up_ref[:, i * tile : (i + 1) * tile]
+        mean = jnp.where((unit + i * tile) // BLOCK == slot, 1.0 / BLOCK, 0.0)
+        energy += jnp.dot(
+            (up * up).astype(jnp.bfloat16),
+            mean.astype(jnp.bfloat16),
+            preferred_element_type=jnp.float32,
+        )
+        scaled = (weight * up.astype(jnp.bfloat16).astype(jnp.float32)).astype(jnp.bfloat16)
+        at = 0
+        for part, out in zip(parts, outs):
+            out[:, i * tile : (i + 1) * tile] = scaled[at : at + part.shape[0]]
+            at += part.shape[0]
+    energy_ref[...] = energy
 
 
 def expert_rows(me, parts, weight, chosen, blocks):
     width, hidden = weight.shape
     total = sum(p.shape[0] for p in parts)
-    tile = min(TILE_N, hidden)
     small = jax.ShapeDtypeStruct((total, LANES), jnp.float32)
+    inside = pl.BlockSpec(memory_space=pltpu.VMEM)
     return pl.pallas_call(
         functools.partial(expert_kernel, chosen, blocks, len(parts)),
-        grid=(hidden // tile,),
         in_specs=[pl.BlockSpec(memory_space=pltpu.SMEM)]
-        + [pl.BlockSpec(p.shape, lambda j: (0, 0)) for p in parts]
-        + [pl.BlockSpec((width, tile), lambda j: (0, j))],
-        out_specs=[pl.BlockSpec((p.shape[0], tile), lambda j: (0, j)) for p in parts]
-        + [pl.BlockSpec((total, LANES), lambda j: (0, 0))] * 2,
+        + [inside] * len(parts)
+        + [pl.BlockSpec(memory_space=pltpu.HBM)],
+        out_specs=[inside] * (len(parts) + 2),
         out_shape=[jax.ShapeDtypeStruct((p.shape[0], hidden), jnp.bfloat16) for p in parts]
         + [small, small],
-        compiler_params=pltpu.CompilerParams(
-            dimension_semantics=("arbitrary",), vmem_limit_bytes=24 * 1024 * 1024
-        ),
+        scratch_shapes=[
+            pltpu.VMEM((width, hidden), weight.dtype),
+            pltpu.VMEM((total, hidden), jnp.float32),
+            pltpu.SemaphoreType.DMA((K_SLICES,)),
+        ],
+        compiler_params=pltpu.CompilerParams(vmem_limit_bytes=50 * 1024 * 1024),
         cost_estimate=pl.CostEstimate(
             flops=2 * total * width * hidden,
             bytes_accessed=2 * width * hidden,
@@ -171,23 +215,29 @@
 
 
 def boxed(packed, me, weight, chosen, blocks):
-    layers = [packed, swap(packed, 8), swap(packed, 16), swap(packed, 24)]
-    keeps, sends, codes, energies = [], [], [], []
-    for rows in layers:
+    far = swap(packed, 16)
+    near = swap(packed, 8)
+    layers = [packed, near, far, swap(far, 8)]
+    halves, others = [], []
+    for rows in [packed, near, jnp.concatenate([far, layers[3]], axis=0)]:
         first = swap(rows, 2, 4)
         second = swap(rows, 4, 2)
         third = swap(first, 4, 2)
         half = jnp.concatenate([rows, first, second, third], axis=0)
-        other = swap(half, 1)
-        keep, send, code, energy = expert_rows(me, [half, other], weight, chosen, blocks)
-        keeps.append(keep)
-        sends.append(send)
-        codes.append(code)
-        energies.append(energy)
+        halves.append(half)
+        others.append(swap(half, 1))
+    four = len(layers)
+    *scaled, code, energy = expert_rows(me, halves + others, weight, chosen, blocks)
     tok_rows = packed.shape[0]
-    four = len(layers)
-    keep = jnp.stack(keeps).reshape(four, 4, tok_rows, -1)
-    came = swap(jnp.stack(sends), 1).reshape(keep.shape)
+
+    def by_layer(parts):
+        near_two = jnp.stack(parts[:2]).reshape(2, 4, tok_rows, -1)
+        far_two = jnp.swapaxes(parts[2].reshape(4, 2, tok_rows, -1), 0, 1)
+        return jnp.concatenate([near_two, far_two], axis=0)
+
+    keep = by_layer(scaled[:3])
+    came = swap(jnp.concatenate(scaled[3:], axis=0), 1)
+    came = by_layer([came[: 4 * tok_rows], came[4 * tok_rows : 8 * tok_rows], came[8 * tok_rows :]])
     partial = add32(keep, came)
     crossed = swap(partial[:, 2:].astype(jnp.bfloat16), 4, 2)
     partial = add32(partial[:, :2], crossed)
@@ -195,7 +245,7 @@
     partial = add32(partial[:, 0], crossed)
     home = [swap(partial[i].astype(jnp.bfloat16), 8 * i) for i in range(1, four)]
     mixed = add32(partial[0], *home).astype(jnp.bfloat16)
-    return mixed, expert_histogram(codes, energies, blocks)
+    return mixed, expert_histogram([code], [energy], blocks)
 
 
 def plain(packed, me, weight, chosen, blocks):

time: 81.9 us -> 66.5 us (0.81)
  Pallas kernels: 18 us -> 11.4 us
  local copies, waits for them, and re-layouts: 4.23 us -> 0.27 us
  starting transfers between devices: 27.6 us -> 24.2 us
  other arithmetic: 4.58 us -> 1.87 us
  waiting for transfers between devices: 26.2 us -> 27.8 us
    pallas_call x4 -> x1, Pallas kernels: 15.5 us -> 7.6 us  [expert_rows(): pl.pallas_call(functools.partial(expert_kernel, chosen, blocks, len(parts...]
    unnamed x16 -> x8, local copies, waits for them, and re-layouts: 3.97 us -> 0.11 us
    ppermute x25 -> x21, starting transfers between devices: 27.6 us -> 24.2 us  [swap(): lax.ppermute(array, 'expert', [(i, i ^ (odd if i & 1 else even)) for i in...]
    pallas_call x0 -> x1, Pallas kernels: none -> 1.76 us  [pack_rows(): pl.pallas_call(pack_kernel, out_shape=jax.ShapeDtypeStruct((tok_rows, wid...]
    ppermute x25 -> x21, waiting for transfers between devices: 26.2 us -> 27.8 us  [swap(): lax.ppermute(array, 'expert', [(i, i ^ (odd if i & 1 else even)) for i in...]
    convert_element_type x3 -> x0, other arithmetic: 1.56 us -> none  [the longest x1 0.79 us: pack_rows(): (128 + (bins & 127) << (bins >> 7)).astype(jnp.float32).astype(jnp.bfloat16)]
    concatenate x2 -> x1, other arithmetic: 0.99 us -> 0.04 us  [boxed(): came = swap(jnp.concatenate(scaled[3:], axis=0), 1)]
  transfers between devices with their start and end apart: 25 -> 21, of which waited for: 11 -> 11; matrix products, arithmetic and copies ran while one was open for 1% -> 2% of each run, Pallas kernels for 17% -> 3%
where the time goes in v2:
time: 66.5 us; the launch traced here: 66.3 us
  waiting for transfers between devices  27.8 us (42%)
  starting transfers between devices  24.2 us (36%)
  Pallas kernels  11.4 us (17%)
  other arithmetic  1.87 us (3%)
  between operations  0.81 us (1%)
    ppermute x21, waiting for transfers between devices, swap(): lax.ppermute(array, 'expert', [(i, i ^ (odd if i & 1 else even)) for i in...  27.8 us
    ppermute x21, starting transfers between devices, swap(): lax.ppermute(array, 'expert', [(i, i ^ (odd if i & 1 else even)) for i in...  24.2 us
    pallas_call x1, Pallas kernels, expert_rows(): pl.pallas_call(functools.partial(expert_kernel, chosen, blocks, len(parts...  7.6 us
    pallas_call x1, Pallas kernels, expert_histogram(): pl.pallas_call(functools.partial(histogram_kernel, blocks, len(codes)), o...  2 us
    pallas_call x1, Pallas kernels, pack_rows(): pl.pallas_call(pack_kernel, out_shape=jax.ShapeDtypeStruct((tok_rows, wid...  1.76 us
  transfers between devices with their start and end apart: 21, of which 11 were waited for; matrix products, arithmetic and copies ran while one was open for 2% of the time, Pallas kernels for 3%

profile of v2, /device:TPU:0, one launch (start us, length us, event | category | flops | bytes accessed | tf_op | source)
XLA Modules:
  0.0 66.3 jit_solution(2938564491846311900)
XLA Ops:
  0.6 1.8 %pack_rows.1 = bf16[16,3712]{1,0:T(8,128)(2,1)} custom-call(bf16[16,3584]{1,0:T(8,128)(2,1)} %tokens_ref.1, s32[8,16]{1,0:T(8,128)} %bitcast.56, f32[8,16]{1,0:T(8,128)} %bitcast.57, s32[64,16]{1,0:T(8,128)} %bitcast.55), custom_call_target="tpu_custom_call" | custom-call | tf_op jit(solution)/shard_map/pack_rows/pallas_call | solution.py:47
  2.4 3.0 %collective-permute-start.3 = (bf16[16,3712]{1,0:T(8,128)(2,1)}, bf16[16,3712]{1,0:T(8,128)(2,1)S(1)}, u32[]{:S(2)}, u32[]{:S(2)}) collective-permute-start(bf16[16,3712]{1,0:T(8,128)(2,1)} %pack_rows.1), channel_id=1, source_target_pairs={{0,8},{1,9},{2,10},{3,11},{4,12},{5,13},{6,14},{7,15},{8,0},{9,1},... | collective-permute-start | bytes 356360 | tf_op jit(solution)/shard_map/ppermute | solution.py:210
  5.4 2.6 %collective-permute-start.7 = (bf16[16,3712]{1,0:T(8,128)(2,1)}, bf16[16,3712]{1,0:T(8,128)(2,1)S(1)}, u32[]{:S(2)}, u32[]{:S(2)}) collective-permute-start(bf16[16,3712]{1,0:T(8,128)(2,1)} %pack_rows.1), channel_id=1, source_target_pairs={{0,16},{1,17},{2,18},{3,19},{4,20},{5,21},{6,22},{7,23},{8,24},{9,... | collective-permute-start | bytes 356360 | tf_op jit(solution)/shard_map/ppermute | solution.py:210
  8.0 1.5 %collective-permute-start.1 = (bf16[16,3712]{1,0:T(8,128)(2,1)}, bf16[16,3712]{1,0:T(8,128)(2,1)S(1)}, u32[]{:S(2)}, u32[]{:S(2)}) collective-permute-start(bf16[16,3712]{1,0:T(8,128)(2,1)} %pack_rows.1), channel_id=1, source_target_pairs={{0,4},{1,3},{2,6},{3,1},{4,0},{5,7},{6,2},{7,5},{8,12},{9,11},{10,... | collective-permute-start | bytes 356360 | tf_op jit(solution)/shard_map/ppermute | solution.py:210
  9.5 1.5 %collective-permute-start = (bf16[16,3712]{1,0:T(8,128)(2,1)}, bf16[16,3712]{1,0:T(8,128)(2,1)S(1)}, u32[]{:S(2)}, u32[]{:S(2)}) collective-permute-start(bf16[16,3712]{1,0:T(8,128)(2,1)} %pack_rows.1), channel_id=1, source_target_pairs={{0,2},{1,5},{2,0},{3,7},{4,6},{5,1},{6,4},{7,3},{8,10},{9,13},{10,... | collective-permute-start | bytes 356360 | tf_op jit(solution)/shard_map/ppermute | solution.py:210
  11.0 0.0 collective-permute-done.3
  11.0 1.0 %collective-permute-start.5 = (bf16[16,3712]{1,0:T(8,128)(2,1)S(1)}, bf16[16,3712]{1,0:T(8,128)(2,1)S(1)}, u32[]{:S(2)}, u32[]{:S(2)}) collective-permute-start(bf16[16,3712]{1,0:T(8,128)(2,1)S(1)} %collective-permute-done.3), channel_id=1, source_target_pairs={{0,4},{1,3},{2,6},{3,1},{4,0},{5,7},{6,2},{7,5},{8,12},{9,11},{10,... | collective-permute-start | bytes 356360 | tf_op jit(solution)/shard_map/ppermute | solution.py:210
  12.0 1.5 %collective-permute-start.4 = (bf16[16,3712]{1,0:T(8,128)(2,1)S(1)}, bf16[16,3712]{1,0:T(8,128)(2,1)S(1)}, u32[]{:S(2)}, u32[]{:S(2)}) collective-permute-start(bf16[16,3712]{1,0:T(8,128)(2,1)S(1)} %collective-permute-done.3), channel_id=1, source_target_pairs={{0,2},{1,5},{2,0},{3,7},{4,6},{5,1},{6,4},{7,3},{8,10},{9,13},{10,... | collective-permute-start | bytes 356360 | tf_op jit(solution)/shard_map/ppermute | solution.py:210
  13.5 0.3 collective-permute-done.7
  13.8 0.4 collective-permute-start.8
  14.3 0.6 collective-permute-done
  14.9 1.0 %collective-permute-start.2 = (bf16[16,3712]{1,0:T(8,128)(2,1)S(1)}, bf16[16,3712]{1,0:T(8,128)(2,1)S(1)}, u32[]{:S(2)}, u32[]{:S(2)}) collective-permute-start(bf16[16,3712]{1,0:T(8,128)(2,1)S(1)} %collective-permute-done), channel_id=1, source_target_pairs={{0,4},{1,3},{2,6},{3,1},{4,0},{5,7},{6,2},{7,5},{8,12},{9,11},{10,... | collective-permute-start | bytes 356360 | tf_op jit(solution)/shard_map/ppermute | solution.py:210
  15.9 2.8 %collective-permute-done.8 = bf16[16,3712]{1,0:T(8,128)(2,1)S(1)} collective-permute-done((bf16[16,3712]{1,0:T(8,128)(2,1)S(1)}, bf16[16,3712]{1,0:T(8,128)(2,1)S(1)}, u32[]{:S(2)}, u32[]{:S(2)}) %collective-permute-start.8) | collective-permute-done | bytes 118816 | tf_op jit(solution)/shard_map/ppermute | solution.py:210
  18.7 1.6 %collective-permute-start.10 = (bf16[32,3712]{1,0:T(8,128)(2,1)S(1)}, bf16[32,3712]{1,0:T(8,128)(2,1)S(1)}, u32[]{:S(2)}, u32[]{:S(2)}) collective-permute-start(bf16[32,3712]{1,0:T(8,128)(2,1)S(1)} %get-tuple-element.25), channel_id=1, source_target_pairs={{0,4},{1,3},{2,6},{3,1},{4,0},{5,7},{6,2},{7,5},{8,12},{9,11},{10,... | collective-permute-start | bytes 712712 | tf_op jit(solution)/shard_map/ppermute | solution.py:210
  20.3 0.0 collective-permute-done.1
  20.3 1.5 %collective-permute-start.9 = (bf16[32,3712]{1,0:T(8,128)(2,1)S(1)}, bf16[32,3712]{1,0:T(8,128)(2,1)S(1)}, u32[]{:S(2)}, u32[]{:S(2)}) collective-permute-start(bf16[32,3712]{1,0:T(8,128)(2,1)S(1)} %get-tuple-element.25), channel_id=1, source_target_pairs={{0,2},{1,5},{2,0},{3,7},{4,6},{5,1},{6,4},{7,3},{8,10},{9,13},{10,... | collective-permute-start | bytes 712712 | tf_op jit(solution)/shard_map/ppermute | solution.py:210
  21.8 0.0 collective-permute-done.2
  21.8 0.9 %pad_maximum_fusion.1.refs_0_ = bf16[64,3712]{1,0:T(8,128)(2,1)S(1)} fusion(bf16[16,3712]{1,0:T(8,128)(2,1)S(1)} %collective-permute-done.2, bf16[16,3712]{1,0:T(8,128)(2,1)S(1)} %collective-permute-done.1, bf16[16,3712]{1,0:T(8,128)(2,1)S(1)} %collective-permute-done, bf16[16,3712]{1,0:T(8,128)(2,1)} %pack_rows.1), kind=kLoop, calls=%fused_computation.4 | loop fusion | flops 1900544 | bytes 950272 | tf_op jit(solution)/shard_map/concatenate | solution.py:226
  22.7 0.1 collective-permute-start.12
  22.8 0.0 collective-permute-done.4
  22.8 0.6 collective-permute-start.6
  23.4 3.5 %collective-permute-done.9 = bf16[32,3712]{1,0:T(8,128)(2,1)S(1)} collective-permute-done((bf16[32,3712]{1,0:T(8,128)(2,1)S(1)}, bf16[32,3712]{1,0:T(8,128)(2,1)S(1)}, u32[]{:S(2)}, u32[]{:S(2)}) %collective-permute-start.9) | collective-permute-done | bytes 237600 | tf_op jit(solution)/shard_map/ppermute | solution.py:210
  26.8 0.5 collective-permute-start.11
  27.3 0.0 collective-permute-done.10
  27.4 5.6 %collective-permute-done.11 = bf16[32,3712]{1,0:T(8,128)(2,1)S(1)} collective-permute-done((bf16[32,3712]{1,0:T(8,128)(2,1)S(1)}, bf16[32,3712]{1,0:T(8,128)(2,1)S(1)}, u32[]{:S(2)}, u32[]{:S(2)}) %collective-permute-start.11) | collective-permute-done | bytes 237600 | tf_op jit(solution)/shard_map/ppermute | solution.py:210
  33.0 0.0 copy-start
  33.0 0.1 collective-permute-start.14
  33.1 0.0 collective-permute-done.5
  33.1 0.0 collective-permute-done.6
  33.1 0.5 collective-permute-start.13
  33.7 0.0 collective-permute-done.12.refs_3_
  33.7 2.6 %collective-permute-done.13.refs_4_ = bf16[64,3712]{1,0:T(8,128)(2,1)S(1)} collective-permute-done((bf16[64,3712]{1,0:T(8,128)(2,1)S(1)}, bf16[64,3712]{1,0:T(8,128)(2,1)S(1)}, u32[]{:S(2)}, u32[]{:S(2)}) %collective-permute-start.13) | collective-permute-done | bytes 475168 | tf_op jit(solution)/shard_map/ppermute | solution.py:210
  36.3 0.0 collective-permute-done.14.refs_5_
  36.3 0.0 copy-done
  36.3 7.6 %expert_rows.1 = (bf16[64,1024]{1,0:T(8,128)(2,1)S(1)}, bf16[64,1024]{1,0:T(8,128)(2,1)S(1)}, bf16[128,1024]{1,0:T(8,128)(2,1)S(1)}, bf16[64,1024]{1,0:T(8,128)(...) custom-call(s32[1]{0:T(128)} %bitcast.me_ref, ...), custom_call_target="tpu_custom_call" | custom-call | flops 3758096384 | bytes 7340032 | tf_op jit(solution)/shard_map/expert_rows/pallas_call | solution.py:127
  43.9 0.2 collective-permute-start.15
  44.1 1.8 %collective-permute-done.15 = bf16[256,1024]{1,0:T(8,128)(2,1)S(1)} collective-permute-done((bf16[256,1024]{1,0:T(8,128)(2,1)S(1)}, bf16[256,1024]{1,0:T(8,128)(2,1)S(1)}, u32[]{:S(2)}, u32[]{:S(2)}) %collective-permute-start.15) | collective-permute-done | bytes 524320 | tf_op jit(solution)/shard_map/ppermute | solution.py:210
  45.9 0.2 convert_add_fusion
  46.1 0.5 collective-permute-start.16
  46.7 5.9 %collective-permute-done.16 = bf16[4,2,16,1024]{3,2,0,1:T(8,128)(2,1)S(1)} collective-permute-done((bf16[4,2,16,1024]{3,2,0,1:T(8,128)(2,1)S(1)}, bf16[4,2,16,1024]{3,2,0,1:T(8,128)(2,1)S(1)}, u32[]{:S(2)}, u32[]{:S(2)}) %collective-permute-start.16) | collective-permute-done | bytes 262176 | tf_op jit(solution)/shard_map/ppermute | solution.py:210
  52.6 0.1 slice_add_fusion
  52.7 2.5 %collective-permute-start.17 = (bf16[4,16,1024]{2,1,0:T(8,128)(2,1)S(1)}, bf16[4,16,1024]{2,1,0:T(8,128)(2,1)S(1)}, u32[]{:S(2)}, u32[]{:S(2)}) collective-permute-start(bf16[4,16,1024]{2,1,0:T(8,128)(2,1)S(1)} %fusion.1), channel_id=1, source_target_pairs={{0,2},{1,5},{2,0},{3,7},{4,6},{5,1},{6,4},{7,3},{8,10},{9,13},{10,... | collective-permute-start | bytes 393224 | tf_op jit(solution)/shard_map/ppermute | solution.py:210
  55.2 2.9 %collective-permute-done.17 = bf16[4,16,1024]{2,1,0:T(8,128)(2,1)S(1)} collective-permute-done((bf16[4,16,1024]{2,1,0:T(8,128)(2,1)S(1)}, bf16[4,16,1024]{2,1,0:T(8,128)(2,1)S(1)}, u32[]{:S(2)}, u32[]{:S(2)}) %collective-permute-start.17) | collective-permute-done | bytes 131104 | tf_op jit(solution)/shard_map/ppermute | solution.py:210
  58.2 0.1 collective-permute-start.18
  58.3 2.5 %collective-permute-start.20 = (bf16[16,1024]{1,0:T(8,128)(2,1)S(1)}, bf16[16,1024]{1,0:T(8,128)(2,1)S(1)}, u32[]{:S(2)}, u32[]{:S(2)}) collective-permute-start(bf16[16,1024]{1,0:T(8,128)(2,1)S(1)} %get-tuple-element.23), channel_id=1, source_target_pairs={{0,24},{1,25},{2,26},{3,27},{4,28},{5,29},{6,30},{7,31},{8,16},{9,... | collective-permute-start | bytes 98312 | tf_op jit(solution)/shard_map/ppermute | solution.py:210
  60.8 1.0 %collective-permute-start.19 = (bf16[16,1024]{1,0:T(8,128)(2,1)S(1)}, bf16[16,1024]{1,0:T(8,128)(2,1)S(1)}, u32[]{:S(2)}, u32[]{:S(2)}) collective-permute-start(bf16[16,1024]{1,0:T(8,128)(2,1)S(1)} %get-tuple-element.24), channel_id=1, source_target_pairs={{0,16},{1,17},{2,18},{3,19},{4,20},{5,21},{6,22},{7,23},{8,24},{9,... | collective-permute-start | bytes 98312 | tf_op jit(solution)/shard_map/ppermute | solution.py:210
  61.8 2.0 %expert_histogram.1 = f32[8,2048]{1,0:T(8,128)} custom-call(f32[512,128]{1,0:T(8,128)S(1)} %get-tuple-element.16.refs_0_, f32[512,128]{1,0:T(8,128)S(1)} %get-tuple-element.17.refs_1_), custom_call_target="tpu_custom_call" | custom-call | flops 268435456 | bytes 524288 | tf_op jit(solution)/shard_map/expert_histogram/pallas_call | solution.py:194
  63.8 0.0 collective-permute-done.18
  63.8 0.3 collective-permute-done.20
  64.1 1.6 %collective-permute-done.19 = bf16[16,1024]{1,0:T(8,128)(2,1)S(1)} collective-permute-done((bf16[16,1024]{1,0:T(8,128)(2,1)S(1)}, bf16[16,1024]{1,0:T(8,128)(2,1)S(1)}, u32[]{:S(2)}, u32[]{:S(2)}) %collective-permute-start.19) | collective-permute-done | bytes 32800 | tf_op jit(solution)/shard_map/ppermute | solution.py:210
  65.6 0.6 fusion.5
  (16 shorter events, 0.3 us)
Async XLA Ops:
  2.4 8.6 %collective-permute-start.3 = (bf16[16,3712]{1,0:T(8,128)(2,1)}, bf16[16,3712]{1,0:T(8,128)(2,1)S(1)}, u32[]{:S(2)}, u32[]{:S(2)}) collective-permute-start(bf16[16,3712]{1,0:T(8,128)(2,1)} %pack_rows.1), channel_id=1, source_target_pairs={{0,8},{1,9},{2,10},{3,11},{4,12},{5,13},{6,14},{7,15},{8,0},{9,1},... | collective-permute-start | bytes 356360 | tf_op jit(solution)/shard_map/ppermute | solution.py:210
  5.4 8.4 %collective-permute-start.7 = (bf16[16,3712]{1,0:T(8,128)(2,1)}, bf16[16,3712]{1,0:T(8,128)(2,1)S(1)}, u32[]{:S(2)}, u32[]{:S(2)}) collective-permute-start(bf16[16,3712]{1,0:T(8,128)(2,1)} %pack_rows.1), channel_id=1, source_target_pairs={{0,16},{1,17},{2,18},{3,19},{4,20},{5,21},{6,22},{7,23},{8,24},{9,... | collective-permute-start | bytes 356360 | tf_op jit(solution)/shard_map/ppermute | solution.py:210
  8.0 12.3 %collective-permute-start.1 = (bf16[16,3712]{1,0:T(8,128)(2,1)}, bf16[16,3712]{1,0:T(8,128)(2,1)S(1)}, u32[]{:S(2)}, u32[]{:S(2)}) collective-permute-start(bf16[16,3712]{1,0:T(8,128)(2,1)} %pack_rows.1), channel_id=1, source_target_pairs={{0,4},{1,3},{2,6},{3,1},{4,0},{5,7},{6,2},{7,5},{8,12},{9,11},{10,... | collective-permute-start | bytes 356360 | tf_op jit(solution)/shard_map/ppermute | solution.py:210
  9.5 5.3 %collective-permute-start = (bf16[16,3712]{1,0:T(8,128)(2,1)}, bf16[16,3712]{1,0:T(8,128)(2,1)S(1)}, u32[]{:S(2)}, u32[]{:S(2)}) collective-permute-start(bf16[16,3712]{1,0:T(8,128)(2,1)} %pack_rows.1), channel_id=1, source_target_pairs={{0,2},{1,5},{2,0},{3,7},{4,6},{5,1},{6,4},{7,3},{8,10},{9,13},{10,... | collective-permute-start | bytes 356360 | tf_op jit(solution)/shard_map/ppermute | solution.py:210
  11.0 22.0 %collective-permute-start.5 = (bf16[16,3712]{1,0:T(8,128)(2,1)S(1)}, bf16[16,3712]{1,0:T(8,128)(2,1)S(1)}, u32[]{:S(2)}, u32[]{:S(2)}) collective-permute-start(bf16[16,3712]{1,0:T(8,128)(2,1)S(1)} %collective-permute-done.3), channel_id=1, source_target_pairs={{0,4},{1,3},{2,6},{3,1},{4,0},{5,7},{6,2},{7,5},{8,12},{9,11},{10,... | collective-permute-start | bytes 356360 | tf_op jit(solution)/shard_map/ppermute | solution.py:210
  12.0 10.8 %collective-permute-start.4 = (bf16[16,3712]{1,0:T(8,128)(2,1)S(1)}, bf16[16,3712]{1,0:T(8,128)(2,1)S(1)}, u32[]{:S(2)}, u32[]{:S(2)}) collective-permute-start(bf16[16,3712]{1,0:T(8,128)(2,1)S(1)} %collective-permute-done.3), channel_id=1, source_target_pairs={{0,2},{1,5},{2,0},{3,7},{4,6},{5,1},{6,4},{7,3},{8,10},{9,13},{10,... | collective-permute-start | bytes 356360 | tf_op jit(solution)/shard_map/ppermute | solution.py:210
  13.8 4.8 %collective-permute-start.8 = (bf16[16,3712]{1,0:T(8,128)(2,1)S(1)}, bf16[16,3712]{1,0:T(8,128)(2,1)S(1)}, u32[]{:S(2)}, u32[]{:S(2)}) collective-permute-start(bf16[16,3712]{1,0:T(8,128)(2,1)S(1)} %collective-permute-done.7), channel_id=1, source_target_pairs={{0,8},{1,9},{2,10},{3,11},{4,12},{5,13},{6,14},{7,15},{8,0},{9,1},... | collective-permute-start | bytes 356360 | tf_op jit(solution)/shard_map/ppermute | solution.py:210
  14.9 6.9 %collective-permute-start.2 = (bf16[16,3712]{1,0:T(8,128)(2,1)S(1)}, bf16[16,3712]{1,0:T(8,128)(2,1)S(1)}, u32[]{:S(2)}, u32[]{:S(2)}) collective-permute-start(bf16[16,3712]{1,0:T(8,128)(2,1)S(1)} %collective-permute-done), channel_id=1, source_target_pairs={{0,4},{1,3},{2,6},{3,1},{4,0},{5,7},{6,2},{7,5},{8,12},{9,11},{10,... | collective-permute-start | bytes 356360 | tf_op jit(solution)/shard_map/ppermute | solution.py:210
  18.7 8.7 %collective-permute-start.10 = (bf16[32,3712]{1,0:T(8,128)(2,1)S(1)}, bf16[32,3712]{1,0:T(8,128)(2,1)S(1)}, u32[]{:S(2)}, u32[]{:S(2)}) collective-permute-start(bf16[32,3712]{1,0:T(8,128)(2,1)S(1)} %get-tuple-element.25), channel_id=1, source_target_pairs={{0,4},{1,3},{2,6},{3,1},{4,0},{5,7},{6,2},{7,5},{8,12},{9,11},{10,... | collective-permute-start | bytes 712712 | tf_op jit(solution)/shard_map/ppermute | solution.py:210
  20.3 6.6 %collective-permute-start.9 = (bf16[32,3712]{1,0:T(8,128)(2,1)S(1)}, bf16[32,3712]{1,0:T(8,128)(2,1)S(1)}, u32[]{:S(2)}, u32[]{:S(2)}) collective-permute-start(bf16[32,3712]{1,0:T(8,128)(2,1)S(1)} %get-tuple-element.25), channel_id=1, source_target_pairs={{0,2},{1,5},{2,0},{3,7},{4,6},{5,1},{6,4},{7,3},{8,10},{9,13},{10,... | collective-permute-start | bytes 712712 | tf_op jit(solution)/shard_map/ppermute | solution.py:210
  22.7 11.0 %collective-permute-start.12 = (bf16[64,3712]{1,0:T(8,128)(2,1)S(1)}, bf16[64,3712]{1,0:T(8,128)(2,1)S(1)}, u32[]{:S(2)}, u32[]{:S(2)}) collective-permute-start(bf16[64,3712]{1,0:T(8,128)(2,1)S(1)} %pad_maximum_fusion.1.refs_0_), channel_id=1, source_target_pairs={{0,1},{1,0},{2,3},{3,2},{4,5},{5,4},{6,7},{7,6},{8,9},{9,8},{10,11... | collective-permute-start | bytes 1425416 | tf_op jit(solution)/shard_map/ppermute | solution.py:210
  22.8 10.3 %collective-permute-start.6 = (bf16[16,3712]{1,0:T(8,128)(2,1)S(1)}, bf16[16,3712]{1,0:T(8,128)(2,1)S(1)}, u32[]{:S(2)}, u32[]{:S(2)}) collective-permute-start(bf16[16,3712]{1,0:T(8,128)(2,1)S(1)} %collective-permute-done.4), channel_id=1, source_target_pairs={{0,4},{1,3},{2,6},{3,1},{4,0},{5,7},{6,2},{7,5},{8,12},{9,11},{10,... | collective-permute-start | bytes 356360 | tf_op jit(solution)/shard_map/ppermute | solution.py:210
  26.8 6.1 %collective-permute-start.11 = (bf16[32,3712]{1,0:T(8,128)(2,1)S(1)}, bf16[32,3712]{1,0:T(8,128)(2,1)S(1)}, u32[]{:S(2)}, u32[]{:S(2)}) collective-permute-start(bf16[32,3712]{1,0:T(8,128)(2,1)S(1)} %collective-permute-done.9), channel_id=1, source_target_pairs={{0,4},{1,3},{2,6},{3,1},{4,0},{5,7},{6,2},{7,5},{8,12},{9,11},{10,... | collective-permute-start | bytes 712712 | tf_op jit(solution)/shard_map/ppermute | solution.py:210
  33.0 3.3 %copy-start = (bf16[128,3712]{1,0:T(8,128)(2,1)}, bf16[128,3712]{1,0:T(8,128)(2,1)S(1)}, u32[]{:S(2)}) copy-start(bf16[128,3712]{1,0:T(8,128)(2,1)S(1)} %constant_dynamic-update-slice_fusion.6.refs_2_) | copy-start | bytes 2850820
  33.0 3.3 %collective-permute-start.14 = (bf16[128,3712]{1,0:T(8,128)(2,1)S(1)}, bf16[128,3712]{1,0:T(8,128)(2,1)}, u32[]{:S(2)}, u32[]{:S(2)}) collective-permute-start(bf16[128,3712]{1,0:T(8,128)(2,1)S(1)} %constant_dynamic-update-slice_fusion.6.refs_2_), channel_id=1, source_target_pairs={{0,1},{1,0},{2,3},{3,2},{4,5},{5,4},{6,7},{7,6},{8,9},{9,8},{10,11... | collective-permute-start | bytes 2850824 | tf_op jit(solution)/shard_map/ppermute | solution.py:210
  33.1 3.1 %collective-permute-start.13 = (bf16[64,3712]{1,0:T(8,128)(2,1)S(1)}, bf16[64,3712]{1,0:T(8,128)(2,1)S(1)}, u32[]{:S(2)}, u32[]{:S(2)}) collective-permute-start(bf16[64,3712]{1,0:T(8,128)(2,1)S(1)} %constant_dynamic-update-slice_fusion.refs_1_), channel_id=1, source_target_pairs={{0,1},{1,0},{2,3},{3,2},{4,5},{5,4},{6,7},{7,6},{8,9},{9,8},{10,11... | collective-permute-start | bytes 1425416 | tf_op jit(solution)/shard_map/ppermute | solution.py:210
  43.9 2.0 %collective-permute-start.15 = (bf16[256,1024]{1,0:T(8,128)(2,1)S(1)}, bf16[256,1024]{1,0:T(8,128)(2,1)S(1)}, u32[]{:S(2)}, u32[]{:S(2)}) collective-permute-start(bf16[256,1024]{1,0:T(8,128)(2,1)S(1)} %pad_maximum_fusion), channel_id=1, source_target_pairs={{0,1},{1,0},{2,3},{3,2},{4,5},{5,4},{6,7},{7,6},{8,9},{9,8},{10,11... | collective-permute-start | bytes 1572872 | tf_op jit(solution)/shard_map/ppermute | solution.py:210
  46.1 6.4 %collective-permute-start.16 = (bf16[4,2,16,1024]{3,2,0,1:T(8,128)(2,1)S(1)}, bf16[4,2,16,1024]{3,2,0,1:T(8,128)(2,1)S(1)}, u32[]{:S(2)}, u32[]{:S(2)}) collective-permute-start(bf16[4,2,16,1024]{3,2,0,1:T(8,128)(2,1)S(1)} %slice.80), channel_id=1, source_target_pairs={{0,4},{1,3},{2,6},{3,1},{4,0},{5,7},{6,2},{7,5},{8,12},{9,11},{10,... | collective-permute-start | bytes 786440 | tf_op jit(solution)/shard_map/ppermute | solution.py:210
  52.7 5.5 %collective-permute-start.17 = (bf16[4,16,1024]{2,1,0:T(8,128)(2,1)S(1)}, bf16[4,16,1024]{2,1,0:T(8,128)(2,1)S(1)}, u32[]{:S(2)}, u32[]{:S(2)}) collective-permute-start(bf16[4,16,1024]{2,1,0:T(8,128)(2,1)S(1)} %fusion.1), channel_id=1, source_target_pairs={{0,2},{1,5},{2,0},{3,7},{4,6},{5,1},{6,4},{7,3},{8,10},{9,13},{10,... | collective-permute-start | bytes 393224 | tf_op jit(solution)/shard_map/ppermute | solution.py:210
  58.2 5.6 %collective-permute-start.18 = (bf16[16,1024]{1,0:T(8,128)(2,1)S(1)}, bf16[16,1024]{1,0:T(8,128)(2,1)S(1)}, u32[]{:S(2)}, u32[]{:S(2)}) collective-permute-start(bf16[16,1024]{1,0:T(8,128)(2,1)S(1)} %get-tuple-element.22), channel_id=1, source_target_pairs={{0,8},{1,9},{2,10},{3,11},{4,12},{5,13},{6,14},{7,15},{8,0},{9,1},... | collective-permute-start | bytes 98312 | tf_op jit(solution)/shard_map/ppermute | solution.py:210
  58.3 5.8 %collective-permute-start.20 = (bf16[16,1024]{1,0:T(8,128)(2,1)S(1)}, bf16[16,1024]{1,0:T(8,128)(2,1)S(1)}, u32[]{:S(2)}, u32[]{:S(2)}) collective-permute-start(bf16[16,1024]{1,0:T(8,128)(2,1)S(1)} %get-tuple-element.23), channel_id=1, source_target_pairs={{0,24},{1,25},{2,26},{3,27},{4,28},{5,29},{6,30},{7,31},{8,16},{9,... | collective-permute-start | bytes 98312 | tf_op jit(solution)/shard_map/ppermute | solution.py:210
  60.8 4.8 %collective-permute-start.19 = (bf16[16,1024]{1,0:T(8,128)(2,1)S(1)}, bf16[16,1024]{1,0:T(8,128)(2,1)S(1)}, u32[]{:S(2)}, u32[]{:S(2)}) collective-permute-start(bf16[16,1024]{1,0:T(8,128)(2,1)S(1)} %get-tuple-element.24), channel_id=1, source_target_pairs={{0,16},{1,17},{2,18},{3,19},{4,20},{5,21},{6,22},{7,23},{8,24},{9,... | collective-permute-start | bytes 98312 | tf_op jit(solution)/shard_map/ppermute | solution.py:210

commit v3 on v2

--- a/solution.py
+++ b/solution.py
@@ -239,10 +239,13 @@
     came = swap(jnp.concatenate(scaled[3:], axis=0), 1)
     came = by_layer([came[: 4 * tok_rows], came[4 * tok_rows : 8 * tok_rows], came[8 * tok_rows :]])
     partial = add32(keep, came)
-    crossed = swap(partial[:, 2:].astype(jnp.bfloat16), 4, 2)
-    partial = add32(partial[:, :2], crossed)
-    crossed = swap(partial[:, 1].astype(jnp.bfloat16), 2, 4)
-    partial = add32(partial[:, 0], crossed)
+    leaving = partial[:, 1:].astype(jnp.bfloat16)
+    partial = add32(
+        partial[:, 0],
+        swap(leaving[:, 2], 6),
+        swap(leaving[:, 0], 2, 4),
+        swap(leaving[:, 1], 4, 2),
+    )
     home = [swap(partial[i].astype(jnp.bfloat16), 8 * i) for i in range(1, four)]
     mixed = add32(partial[0], *home).astype(jnp.bfloat16)
     return mixed, expert_histogram([code], [energy], blocks)

time: 66.5 us -> 64.2 us (0.965)
  waiting for transfers between devices: 27.8 us -> 24.6 us
  starting transfers between devices: 24.2 us -> 25.1 us
    ppermute x21 -> x22, waiting for transfers between devices: 27.8 us -> 24.6 us  [swap(): lax.ppermute(array, 'expert', [(i, i ^ (odd if i & 1 else even)) for i in...]
    ppermute x21 -> x22, starting transfers between devices: 24.2 us -> 25.1 us  [swap(): lax.ppermute(array, 'expert', [(i, i ^ (odd if i & 1 else even)) for i in...]
  transfers between devices with their start and end apart: 21 -> 22, of which waited for: 11 -> 11; matrix products, arithmetic and copies ran while one was open for 2% -> 2% of each run, Pallas kernels for 3% -> 3%
where the time goes in v3:
time: 64.2 us; the launch traced here: 64 us
  starting transfers between devices  25.1 us (39%)
  waiting for transfers between devices  24.6 us (38%)
  Pallas kernels  11.4 us (18%)
  other arithmetic  1.85 us (3%)
  between operations  0.79 us (1%)
    ppermute x22, starting transfers between devices, swap(): lax.ppermute(array, 'expert', [(i, i ^ (odd if i & 1 else even)) for i in...  25.1 us
    ppermute x22, waiting for transfers between devices, swap(): lax.ppermute(array, 'expert', [(i, i ^ (odd if i & 1 else even)) for i in...  24.6 us
    pallas_call x1, Pallas kernels, expert_rows(): pl.pallas_call(functools.partial(expert_kernel, chosen, blocks, len(parts...  7.6 us
    pallas_call x1, Pallas kernels, expert_histogram(): pl.pallas_call(functools.partial(histogram_kernel, blocks, len(codes)), o...  2 us
    pallas_call x1, Pallas kernels, pack_rows(): pl.pallas_call(pack_kernel, out_shape=jax.ShapeDtypeStruct((tok_rows, wid...  1.76 us
  transfers between devices with their start and end apart: 22, of which 11 were waited for; matrix products, arithmetic and copies ran while one was open for 2% of the time, Pallas kernels for 3%

profile of v3, /device:TPU:0, one launch (start us, length us, event | category | flops | bytes accessed | tf_op | source)
XLA Modules:
  0.0 64.0 jit_solution(5283061768247281973)
XLA Ops:
  0.6 1.8 %pack_rows.1 = bf16[16,3712]{1,0:T(8,128)(2,1)} custom-call(bf16[16,3584]{1,0:T(8,128)(2,1)} %tokens_ref.1, s32[8,16]{1,0:T(8,128)} %bitcast.64, f32[8,16]{1,0:T(8,128)} %bitcast.65, s32[64,16]{1,0:T(8,128)} %bitcast.63), custom_call_target="tpu_custom_call" | custom-call | tf_op jit(solution)/shard_map/pack_rows/pallas_call | solution.py:47
  2.4 3.0 %collective-permute-start.3 = (bf16[16,3712]{1,0:T(8,128)(2,1)}, bf16[16,3712]{1,0:T(8,128)(2,1)S(1)}, u32[]{:S(2)}, u32[]{:S(2)}) collective-permute-start(bf16[16,3712]{1,0:T(8,128)(2,1)} %pack_rows.1), channel_id=1, source_target_pairs={{0,8},{1,9},{2,10},{3,11},{4,12},{5,13},{6,14},{7,15},{8,0},{9,1},... | collective-permute-start | bytes 356360 | tf_op jit(solution)/shard_map/ppermute | solution.py:210
  5.4 2.6 %collective-permute-start.7 = (bf16[16,3712]{1,0:T(8,128)(2,1)}, bf16[16,3712]{1,0:T(8,128)(2,1)S(1)}, u32[]{:S(2)}, u32[]{:S(2)}) collective-permute-start(bf16[16,3712]{1,0:T(8,128)(2,1)} %pack_rows.1), channel_id=1, source_target_pairs={{0,16},{1,17},{2,18},{3,19},{4,20},{5,21},{6,22},{7,23},{8,24},{9,... | collective-permute-start | bytes 356360 | tf_op jit(solution)/shard_map/ppermute | solution.py:210
  8.0 1.5 %collective-permute-start.1 = (bf16[16,3712]{1,0:T(8,128)(2,1)}, bf16[16,3712]{1,0:T(8,128)(2,1)S(1)}, u32[]{:S(2)}, u32[]{:S(2)}) collective-permute-start(bf16[16,3712]{1,0:T(8,128)(2,1)} %pack_rows.1), channel_id=1, source_target_pairs={{0,4},{1,3},{2,6},{3,1},{4,0},{5,7},{6,2},{7,5},{8,12},{9,11},{10,... | collective-permute-start | bytes 356360 | tf_op jit(solution)/shard_map/ppermute | solution.py:210
  9.5 1.5 %collective-permute-start = (bf16[16,3712]{1,0:T(8,128)(2,1)}, bf16[16,3712]{1,0:T(8,128)(2,1)S(1)}, u32[]{:S(2)}, u32[]{:S(2)}) collective-permute-start(bf16[16,3712]{1,0:T(8,128)(2,1)} %pack_rows.1), channel_id=1, source_target_pairs={{0,2},{1,5},{2,0},{3,7},{4,6},{5,1},{6,4},{7,3},{8,10},{9,13},{10,... | collective-permute-start | bytes 356360 | tf_op jit(solution)/shard_map/ppermute | solution.py:210
  11.0 0.0 collective-permute-done.3
  11.0 1.0 %collective-permute-start.5 = (bf16[16,3712]{1,0:T(8,128)(2,1)S(1)}, bf16[16,3712]{1,0:T(8,128)(2,1)S(1)}, u32[]{:S(2)}, u32[]{:S(2)}) collective-permute-start(bf16[16,3712]{1,0:T(8,128)(2,1)S(1)} %collective-permute-done.3), channel_id=1, source_target_pairs={{0,4},{1,3},{2,6},{3,1},{4,0},{5,7},{6,2},{7,5},{8,12},{9,11},{10,... | collective-permute-start | bytes 356360 | tf_op jit(solution)/shard_map/ppermute | solution.py:210
  12.0 1.5 %collective-permute-start.4 = (bf16[16,3712]{1,0:T(8,128)(2,1)S(1)}, bf16[16,3712]{1,0:T(8,128)(2,1)S(1)}, u32[]{:S(2)}, u32[]{:S(2)}) collective-permute-start(bf16[16,3712]{1,0:T(8,128)(2,1)S(1)} %collective-permute-done.3), channel_id=1, source_target_pairs={{0,2},{1,5},{2,0},{3,7},{4,6},{5,1},{6,4},{7,3},{8,10},{9,13},{10,... | collective-permute-start | bytes 356360 | tf_op jit(solution)/shard_map/ppermute | solution.py:210
  13.5 0.3 collective-permute-done.7
  13.8 0.4 collective-permute-start.8
  14.3 0.6 collective-permute-done
  14.9 1.0 %collective-permute-start.2 = (bf16[16,3712]{1,0:T(8,128)(2,1)S(1)}, bf16[16,3712]{1,0:T(8,128)(2,1)S(1)}, u32[]{:S(2)}, u32[]{:S(2)}) collective-permute-start(bf16[16,3712]{1,0:T(8,128)(2,1)S(1)} %collective-permute-done), channel_id=1, source_target_pairs={{0,4},{1,3},{2,6},{3,1},{4,0},{5,7},{6,2},{7,5},{8,12},{9,11},{10,... | collective-permute-start | bytes 356360 | tf_op jit(solution)/shard_map/ppermute | solution.py:210
  15.9 2.8 %collective-permute-done.8 = bf16[16,3712]{1,0:T(8,128)(2,1)S(1)} collective-permute-done((bf16[16,3712]{1,0:T(8,128)(2,1)S(1)}, bf16[16,3712]{1,0:T(8,128)(2,1)S(1)}, u32[]{:S(2)}, u32[]{:S(2)}) %collective-permute-start.8) | collective-permute-done | bytes 118816 | tf_op jit(solution)/shard_map/ppermute | solution.py:210
  18.7 1.6 %collective-permute-start.10 = (bf16[32,3712]{1,0:T(8,128)(2,1)S(1)}, bf16[32,3712]{1,0:T(8,128)(2,1)S(1)}, u32[]{:S(2)}, u32[]{:S(2)}) collective-permute-start(bf16[32,3712]{1,0:T(8,128)(2,1)S(1)} %get-tuple-element.30), channel_id=1, source_target_pairs={{0,4},{1,3},{2,6},{3,1},{4,0},{5,7},{6,2},{7,5},{8,12},{9,11},{10,... | collective-permute-start | bytes 712712 | tf_op jit(solution)/shard_map/ppermute | solution.py:210
  20.3 0.0 collective-permute-done.1
  20.3 1.5 %collective-permute-start.9 = (bf16[32,3712]{1,0:T(8,128)(2,1)S(1)}, bf16[32,3712]{1,0:T(8,128)(2,1)S(1)}, u32[]{:S(2)}, u32[]{:S(2)}) collective-permute-start(bf16[32,3712]{1,0:T(8,128)(2,1)S(1)} %get-tuple-element.30), channel_id=1, source_target_pairs={{0,2},{1,5},{2,0},{3,7},{4,6},{5,1},{6,4},{7,3},{8,10},{9,13},{10,... | collective-permute-start | bytes 712712 | tf_op jit(solution)/shard_map/ppermute | solution.py:210
  21.8 0.0 collective-permute-done.2
  21.8 0.9 %pad_maximum_fusion.1.refs_0_ = bf16[64,3712]{1,0:T(8,128)(2,1)S(1)} fusion(bf16[16,3712]{1,0:T(8,128)(2,1)S(1)} %collective-permute-done.2, bf16[16,3712]{1,0:T(8,128)(2,1)S(1)} %collective-permute-done.1, bf16[16,3712]{1,0:T(8,128)(2,1)S(1)} %collective-permute-done, bf16[16,3712]{1,0:T(8,128)(2,1)} %pack_rows.1), kind=kLoop, calls=%fused_computation.2 | loop fusion | flops 1900544 | bytes 950272 | tf_op jit(solution)/shard_map/concatenate | solution.py:226
  22.7 0.1 collective-permute-start.12
  22.8 0.0 collective-permute-done.4
  22.8 0.6 collective-permute-start.6
  23.4 3.5 %collective-permute-done.9 = bf16[32,3712]{1,0:T(8,128)(2,1)S(1)} collective-permute-done((bf16[32,3712]{1,0:T(8,128)(2,1)S(1)}, bf16[32,3712]{1,0:T(8,128)(2,1)S(1)}, u32[]{:S(2)}, u32[]{:S(2)}) %collective-permute-start.9) | collective-permute-done | bytes 237600 | tf_op jit(solution)/shard_map/ppermute | solution.py:210
  26.8 0.5 collective-permute-start.11
  27.3 0.0 collective-permute-done.10
  27.4 5.6 %collective-permute-done.11 = bf16[32,3712]{1,0:T(8,128)(2,1)S(1)} collective-permute-done((bf16[32,3712]{1,0:T(8,128)(2,1)S(1)}, bf16[32,3712]{1,0:T(8,128)(2,1)S(1)}, u32[]{:S(2)}, u32[]{:S(2)}) %collective-permute-start.11) | collective-permute-done | bytes 237600 | tf_op jit(solution)/shard_map/ppermute | solution.py:210
  33.0 0.0 copy-start
  33.0 0.1 collective-permute-start.14
  33.1 0.0 collective-permute-done.5
  33.1 0.0 collective-permute-done.6
  33.1 0.5 collective-permute-start.13
  33.7 0.0 collective-permute-done.12.refs_3_
  33.7 2.6 %collective-permute-done.13.refs_4_ = bf16[64,3712]{1,0:T(8,128)(2,1)S(1)} collective-permute-done((bf16[64,3712]{1,0:T(8,128)(2,1)S(1)}, bf16[64,3712]{1,0:T(8,128)(2,1)S(1)}, u32[]{:S(2)}, u32[]{:S(2)}) %collective-permute-start.13) | collective-permute-done | bytes 475168 | tf_op jit(solution)/shard_map/ppermute | solution.py:210
  36.2 0.0 collective-permute-done.14.refs_5_
  36.3 0.0 copy-done
  36.3 7.6 %expert_rows.1 = (bf16[64,1024]{1,0:T(8,128)(2,1)S(1)}, bf16[64,1024]{1,0:T(8,128)(2,1)S(1)}, bf16[128,1024]{1,0:T(8,128)(2,1)S(1)}, bf16[64,1024]{1,0:T(8,128)(...) custom-call(s32[1]{0:T(128)} %bitcast.me_ref, ...), custom_call_target="tpu_custom_call" | custom-call | flops 3758096384 | bytes 7340032 | tf_op jit(solution)/shard_map/expert_rows/pallas_call | solution.py:127
  43.9 0.2 collective-permute-start.15
  44.1 1.8 %collective-permute-done.15 = bf16[256,1024]{1,0:T(8,128)(2,1)S(1)} collective-permute-done((bf16[256,1024]{1,0:T(8,128)(2,1)S(1)}, bf16[256,1024]{1,0:T(8,128)(2,1)S(1)}, u32[]{:S(2)}, u32[]{:S(2)}) %collective-permute-start.15) | collective-permute-done | bytes 524320 | tf_op jit(solution)/shard_map/ppermute | solution.py:210
  45.9 0.2 convert_add_fusion
  46.2 2.0 %collective-permute-start.16 = (bf16[4,16,1024]{2,1,0:T(8,128)(2,1)S(1)}, bf16[4,16,1024]{2,1,0:T(8,128)(2,1)S(1)}, u32[]{:S(2)}, u32[]{:S(2)}) collective-permute-start(bf16[4,16,1024]{2,1,0:T(8,128)(2,1)S(1)} %get-tuple-element.22), channel_id=1, source_target_pairs={{0,6},{1,7},{2,4},{3,5},{4,2},{5,3},{6,0},{7,1},{8,14},{9,15},{10,... | collective-permute-start | bytes 393224 | tf_op jit(solution)/shard_map/ppermute | solution.py:210
  48.2 2.0 %collective-permute-start.18 = (bf16[4,16,1024]{2,1,0:T(8,128)(2,1)S(1)}, bf16[4,16,1024]{2,1,0:T(8,128)(2,1)S(1)}, u32[]{:S(2)}, u32[]{:S(2)}) collective-permute-start(bf16[4,16,1024]{2,1,0:T(8,128)(2,1)S(1)} %get-tuple-element.23), channel_id=1, source_target_pairs={{0,4},{1,3},{2,6},{3,1},{4,0},{5,7},{6,2},{7,5},{8,12},{9,11},{10,... | collective-permute-start | bytes 393224 | tf_op jit(solution)/shard_map/ppermute | solution.py:210
  50.2 0.0 collective-permute-start.17
  50.2 3.0 %collective-permute-done.16 = bf16[4,16,1024]{2,1,0:T(8,128)(2,1)S(1)} collective-permute-done((bf16[4,16,1024]{2,1,0:T(8,128)(2,1)S(1)}, bf16[4,16,1024]{2,1,0:T(8,128)(2,1)S(1)}, u32[]{:S(2)}, u32[]{:S(2)}) %collective-permute-start.16) | collective-permute-done | bytes 131104 | tf_op jit(solution)/shard_map/ppermute | solution.py:210
  53.2 2.3 %collective-permute-done.18 = bf16[4,16,1024]{2,1,0:T(8,128)(2,1)S(1)} collective-permute-done((bf16[4,16,1024]{2,1,0:T(8,128)(2,1)S(1)}, bf16[4,16,1024]{2,1,0:T(8,128)(2,1)S(1)}, u32[]{:S(2)}, u32[]{:S(2)}) %collective-permute-start.18) | collective-permute-done | bytes 131104 | tf_op jit(solution)/shard_map/ppermute | solution.py:210
  55.5 0.0 collective-permute-done.17
  55.5 0.1 fusion.8
  55.6 0.5 collective-permute-start.19
  56.0 2.5 %collective-permute-start.21 = (bf16[16,1024]{1,0:T(8,128)(2,1)S(1)}, bf16[16,1024]{1,0:T(8,128)(2,1)S(1)}, u32[]{:S(2)}, u32[]{:S(2)}) collective-permute-start(bf16[16,1024]{1,0:T(8,128)(2,1)S(1)} %get-tuple-element.28), channel_id=1, source_target_pairs={{0,24},{1,25},{2,26},{3,27},{4,28},{5,29},{6,30},{7,31},{8,16},{9,... | collective-permute-start | bytes 98312 | tf_op jit(solution)/shard_map/ppermute | solution.py:210
  58.5 0.6 collective-permute-start.20
  59.1 2.0 %expert_histogram.1 = f32[8,2048]{1,0:T(8,128)} custom-call(f32[512,128]{1,0:T(8,128)S(1)} %get-tuple-element.16.refs_0_, f32[512,128]{1,0:T(8,128)S(1)} %get-tuple-element.17.refs_1_), custom_call_target="tpu_custom_call" | custom-call | flops 268435456 | bytes 524288 | tf_op jit(solution)/shard_map/expert_histogram/pallas_call | solution.py:194
  61.1 0.0 collective-permute-done.19
  61.1 0.7 %collective-permute-done.21 = bf16[16,1024]{1,0:T(8,128)(2,1)S(1)} collective-permute-done((bf16[16,1024]{1,0:T(8,128)(2,1)S(1)}, bf16[16,1024]{1,0:T(8,128)(2,1)S(1)}, u32[]{:S(2)}, u32[]{:S(2)}) %collective-permute-start.21) | collective-permute-done | bytes 32800 | tf_op jit(solution)/shard_map/ppermute | solution.py:210
  61.8 1.5 %collective-permute-done.20 = bf16[16,1024]{1,0:T(8,128)(2,1)S(1)} collective-permute-done((bf16[16,1024]{1,0:T(8,128)(2,1)S(1)}, bf16[16,1024]{1,0:T(8,128)(2,1)S(1)}, u32[]{:S(2)}, u32[]{:S(2)}) %collective-permute-start.20) | collective-permute-done | bytes 32800 | tf_op jit(solution)/shard_map/ppermute | solution.py:210
  63.3 0.6 fusion.6
  (14 shorter events, 0.3 us)
Async XLA Ops:
  2.4 8.6 %collective-permute-start.3 = (bf16[16,3712]{1,0:T(8,128)(2,1)}, bf16[16,3712]{1,0:T(8,128)(2,1)S(1)}, u32[]{:S(2)}, u32[]{:S(2)}) collective-permute-start(bf16[16,3712]{1,0:T(8,128)(2,1)} %pack_rows.1), channel_id=1, source_target_pairs={{0,8},{1,9},{2,10},{3,11},{4,12},{5,13},{6,14},{7,15},{8,0},{9,1},... | collective-permute-start | bytes 356360 | tf_op jit(solution)/shard_map/ppermute | solution.py:210
  5.4 8.4 %collective-permute-start.7 = (bf16[16,3712]{1,0:T(8,128)(2,1)}, bf16[16,3712]{1,0:T(8,128)(2,1)S(1)}, u32[]{:S(2)}, u32[]{:S(2)}) collective-permute-start(bf16[16,3712]{1,0:T(8,128)(2,1)} %pack_rows.1), channel_id=1, source_target_pairs={{0,16},{1,17},{2,18},{3,19},{4,20},{5,21},{6,22},{7,23},{8,24},{9,... | collective-permute-start | bytes 356360 | tf_op jit(solution)/shard_map/ppermute | solution.py:210
  8.0 12.3 %collective-permute-start.1 = (bf16[16,3712]{1,0:T(8,128)(2,1)}, bf16[16,3712]{1,0:T(8,128)(2,1)S(1)}, u32[]{:S(2)}, u32[]{:S(2)}) collective-permute-start(bf16[16,3712]{1,0:T(8,128)(2,1)} %pack_rows.1), channel_id=1, source_target_pairs={{0,4},{1,3},{2,6},{3,1},{4,0},{5,7},{6,2},{7,5},{8,12},{9,11},{10,... | collective-permute-start | bytes 356360 | tf_op jit(solution)/shard_map/ppermute | solution.py:210
  9.5 5.3 %collective-permute-start = (bf16[16,3712]{1,0:T(8,128)(2,1)}, bf16[16,3712]{1,0:T(8,128)(2,1)S(1)}, u32[]{:S(2)}, u32[]{:S(2)}) collective-permute-start(bf16[16,3712]{1,0:T(8,128)(2,1)} %pack_rows.1), channel_id=1, source_target_pairs={{0,2},{1,5},{2,0},{3,7},{4,6},{5,1},{6,4},{7,3},{8,10},{9,13},{10,... | collective-permute-start | bytes 356360 | tf_op jit(solution)/shard_map/ppermute | solution.py:210
  11.0 22.0 %collective-permute-start.5 = (bf16[16,3712]{1,0:T(8,128)(2,1)S(1)}, bf16[16,3712]{1,0:T(8,128)(2,1)S(1)}, u32[]{:S(2)}, u32[]{:S(2)}) collective-permute-start(bf16[16,3712]{1,0:T(8,128)(2,1)S(1)} %collective-permute-done.3), channel_id=1, source_target_pairs={{0,4},{1,3},{2,6},{3,1},{4,0},{5,7},{6,2},{7,5},{8,12},{9,11},{10,... | collective-permute-start | bytes 356360 | tf_op jit(solution)/shard_map/ppermute | solution.py:210
  12.0 10.8 %collective-permute-start.4 = (bf16[16,3712]{1,0:T(8,128)(2,1)S(1)}, bf16[16,3712]{1,0:T(8,128)(2,1)S(1)}, u32[]{:S(2)}, u32[]{:S(2)}) collective-permute-start(bf16[16,3712]{1,0:T(8,128)(2,1)S(1)} %collective-permute-done.3), channel_id=1, source_target_pairs={{0,2},{1,5},{2,0},{3,7},{4,6},{5,1},{6,4},{7,3},{8,10},{9,13},{10,... | collective-permute-start | bytes 356360 | tf_op jit(solution)/shard_map/ppermute | solution.py:210
  13.8 4.8 %collective-permute-start.8 = (bf16[16,3712]{1,0:T(8,128)(2,1)S(1)}, bf16[16,3712]{1,0:T(8,128)(2,1)S(1)}, u32[]{:S(2)}, u32[]{:S(2)}) collective-permute-start(bf16[16,3712]{1,0:T(8,128)(2,1)S(1)} %collective-permute-done.7), channel_id=1, source_target_pairs={{0,8},{1,9},{2,10},{3,11},{4,12},{5,13},{6,14},{7,15},{8,0},{9,1},... | collective-permute-start | bytes 356360 | tf_op jit(solution)/shard_map/ppermute | solution.py:210
  14.9 6.9 %collective-permute-start.2 = (bf16[16,3712]{1,0:T(8,128)(2,1)S(1)}, bf16[16,3712]{1,0:T(8,128)(2,1)S(1)}, u32[]{:S(2)}, u32[]{:S(2)}) collective-permute-start(bf16[16,3712]{1,0:T(8,128)(2,1)S(1)} %collective-permute-done), channel_id=1, source_target_pairs={{0,4},{1,3},{2,6},{3,1},{4,0},{5,7},{6,2},{7,5},{8,12},{9,11},{10,... | collective-permute-start | bytes 356360 | tf_op jit(solution)/shard_map/ppermute | solution.py:210
  18.7 8.7 %collective-permute-start.10 = (bf16[32,3712]{1,0:T(8,128)(2,1)S(1)}, bf16[32,3712]{1,0:T(8,128)(2,1)S(1)}, u32[]{:S(2)}, u32[]{:S(2)}) collective-permute-start(bf16[32,3712]{1,0:T(8,128)(2,1)S(1)} %get-tuple-element.30), channel_id=1, source_target_pairs={{0,4},{1,3},{2,6},{3,1},{4,0},{5,7},{6,2},{7,5},{8,12},{9,11},{10,... | collective-permute-start | bytes 712712 | tf_op jit(solution)/shard_map/ppermute | solution.py:210
  20.3 6.6 %collective-permute-start.9 = (bf16[32,3712]{1,0:T(8,128)(2,1)S(1)}, bf16[32,3712]{1,0:T(8,128)(2,1)S(1)}, u32[]{:S(2)}, u32[]{:S(2)}) collective-permute-start(bf16[32,3712]{1,0:T(8,128)(2,1)S(1)} %get-tuple-element.30), channel_id=1, source_target_pairs={{0,2},{1,5},{2,0},{3,7},{4,6},{5,1},{6,4},{7,3},{8,10},{9,13},{10,... | collective-permute-start | bytes 712712 | tf_op jit(solution)/shard_map/ppermute | solution.py:210
  22.7 11.0 %collective-permute-start.12 = (bf16[64,3712]{1,0:T(8,128)(2,1)S(1)}, bf16[64,3712]{1,0:T(8,128)(2,1)S(1)}, u32[]{:S(2)}, u32[]{:S(2)}) collective-permute-start(bf16[64,3712]{1,0:T(8,128)(2,1)S(1)} %pad_maximum_fusion.1.refs_0_), channel_id=1, source_target_pairs={{0,1},{1,0},{2,3},{3,2},{4,5},{5,4},{6,7},{7,6},{8,9},{9,8},{10,11... | collective-permute-start | bytes 1425416 | tf_op jit(solution)/shard_map/ppermute | solution.py:210
  22.8 10.3 %collective-permute-start.6 = (bf16[16,3712]{1,0:T(8,128)(2,1)S(1)}, bf16[16,3712]{1,0:T(8,128)(2,1)S(1)}, u32[]{:S(2)}, u32[]{:S(2)}) collective-permute-start(bf16[16,3712]{1,0:T(8,128)(2,1)S(1)} %collective-permute-done.4), channel_id=1, source_target_pairs={{0,4},{1,3},{2,6},{3,1},{4,0},{5,7},{6,2},{7,5},{8,12},{9,11},{10,... | collective-permute-start | bytes 356360 | tf_op jit(solution)/shard_map/ppermute | solution.py:210
  26.8 6.1 %collective-permute-start.11 = (bf16[32,3712]{1,0:T(8,128)(2,1)S(1)}, bf16[32,3712]{1,0:T(8,128)(2,1)S(1)}, u32[]{:S(2)}, u32[]{:S(2)}) collective-permute-start(bf16[32,3712]{1,0:T(8,128)(2,1)S(1)} %collective-permute-done.9), channel_id=1, source_target_pairs={{0,4},{1,3},{2,6},{3,1},{4,0},{5,7},{6,2},{7,5},{8,12},{9,11},{10,... | collective-permute-start | bytes 712712 | tf_op jit(solution)/shard_map/ppermute | solution.py:210
  33.0 3.3 %copy-start = (bf16[128,3712]{1,0:T(8,128)(2,1)}, bf16[128,3712]{1,0:T(8,128)(2,1)S(1)}, u32[]{:S(2)}) copy-start(bf16[128,3712]{1,0:T(8,128)(2,1)S(1)} %constant_dynamic-update-slice_fusion.6.refs_2_) | copy-start | bytes 2850820
  33.0 3.3 %collective-permute-start.14 = (bf16[128,3712]{1,0:T(8,128)(2,1)S(1)}, bf16[128,3712]{1,0:T(8,128)(2,1)}, u32[]{:S(2)}, u32[]{:S(2)}) collective-permute-start(bf16[128,3712]{1,0:T(8,128)(2,1)S(1)} %constant_dynamic-update-slice_fusion.6.refs_2_), channel_id=1, source_target_pairs={{0,1},{1,0},{2,3},{3,2},{4,5},{5,4},{6,7},{7,6},{8,9},{9,8},{10,11... | collective-permute-start | bytes 2850824 | tf_op jit(solution)/shard_map/ppermute | solution.py:210
  33.1 3.1 %collective-permute-start.13 = (bf16[64,3712]{1,0:T(8,128)(2,1)S(1)}, bf16[64,3712]{1,0:T(8,128)(2,1)S(1)}, u32[]{:S(2)}, u32[]{:S(2)}) collective-permute-start(bf16[64,3712]{1,0:T(8,128)(2,1)S(1)} %constant_dynamic-update-slice_fusion.refs_1_), channel_id=1, source_target_pairs={{0,1},{1,0},{2,3},{3,2},{4,5},{5,4},{6,7},{7,6},{8,9},{9,8},{10,11... | collective-permute-start | bytes 1425416 | tf_op jit(solution)/shard_map/ppermute | solution.py:210
  43.9 2.0 %collective-permute-start.15 = (bf16[256,1024]{1,0:T(8,128)(2,1)S(1)}, bf16[256,1024]{1,0:T(8,128)(2,1)S(1)}, u32[]{:S(2)}, u32[]{:S(2)}) collective-permute-start(bf16[256,1024]{1,0:T(8,128)(2,1)S(1)} %pad_maximum_fusion), channel_id=1, source_target_pairs={{0,1},{1,0},{2,3},{3,2},{4,5},{5,4},{6,7},{7,6},{8,9},{9,8},{10,11... | collective-permute-start | bytes 1572872 | tf_op jit(solution)/shard_map/ppermute | solution.py:210
  46.2 7.1 %collective-permute-start.16 = (bf16[4,16,1024]{2,1,0:T(8,128)(2,1)S(1)}, bf16[4,16,1024]{2,1,0:T(8,128)(2,1)S(1)}, u32[]{:S(2)}, u32[]{:S(2)}) collective-permute-start(bf16[4,16,1024]{2,1,0:T(8,128)(2,1)S(1)} %get-tuple-element.22), channel_id=1, source_target_pairs={{0,6},{1,7},{2,4},{3,5},{4,2},{5,3},{6,0},{7,1},{8,14},{9,15},{10,... | collective-permute-start | bytes 393224 | tf_op jit(solution)/shard_map/ppermute | solution.py:210
  48.2 7.3 %collective-permute-start.18 = (bf16[4,16,1024]{2,1,0:T(8,128)(2,1)S(1)}, bf16[4,16,1024]{2,1,0:T(8,128)(2,1)S(1)}, u32[]{:S(2)}, u32[]{:S(2)}) collective-permute-start(bf16[4,16,1024]{2,1,0:T(8,128)(2,1)S(1)} %get-tuple-element.23), channel_id=1, source_target_pairs={{0,4},{1,3},{2,6},{3,1},{4,0},{5,7},{6,2},{7,5},{8,12},{9,11},{10,... | collective-permute-start | bytes 393224 | tf_op jit(solution)/shard_map/ppermute | solution.py:210
  50.2 5.3 %collective-permute-start.17 = (bf16[4,16,1024]{2,1,0:T(8,128)(2,1)S(1)}, bf16[4,16,1024]{2,1,0:T(8,128)(2,1)S(1)}, u32[]{:S(2)}, u32[]{:S(2)}) collective-permute-start(bf16[4,16,1024]{2,1,0:T(8,128)(2,1)S(1)} %get-tuple-element.24), channel_id=1, source_target_pairs={{0,2},{1,5},{2,0},{3,7},{4,6},{5,1},{6,4},{7,3},{8,10},{9,13},{10,... | collective-permute-start | bytes 393224 | tf_op jit(solution)/shard_map/ppermute | solution.py:210
  55.6 5.6 %collective-permute-start.19 = (bf16[16,1024]{1,0:T(8,128)(2,1)S(1)}, bf16[16,1024]{1,0:T(8,128)(2,1)S(1)}, u32[]{:S(2)}, u32[]{:S(2)}) collective-permute-start(bf16[16,1024]{1,0:T(8,128)(2,1)S(1)} %get-tuple-element.27), channel_id=1, source_target_pairs={{0,8},{1,9},{2,10},{3,11},{4,12},{5,13},{6,14},{7,15},{8,0},{9,1},... | collective-permute-start | bytes 98312 | tf_op jit(solution)/shard_map/ppermute | solution.py:210
  56.0 5.8 %collective-permute-start.21 = (bf16[16,1024]{1,0:T(8,128)(2,1)S(1)}, bf16[16,1024]{1,0:T(8,128)(2,1)S(1)}, u32[]{:S(2)}, u32[]{:S(2)}) collective-permute-start(bf16[16,1024]{1,0:T(8,128)(2,1)S(1)} %get-tuple-element.28), channel_id=1, source_target_pairs={{0,24},{1,25},{2,26},{3,27},{4,28},{5,29},{6,30},{7,31},{8,16},{9,... | collective-permute-start | bytes 98312 | tf_op jit(solution)/shard_map/ppermute | solution.py:210
  58.5 4.8 %collective-permute-start.20 = (bf16[16,1024]{1,0:T(8,128)(2,1)S(1)}, bf16[16,1024]{1,0:T(8,128)(2,1)S(1)}, u32[]{:S(2)}, u32[]{:S(2)}) collective-permute-start(bf16[16,1024]{1,0:T(8,128)(2,1)S(1)} %get-tuple-element.29), channel_id=1, source_target_pairs={{0,16},{1,17},{2,18},{3,19},{4,20},{5,21},{6,22},{7,23},{8,24},{9,... | collective-permute-start | bytes 98312 | tf_op jit(solution)/shard_map/ppermute | solution.py:210

commit v4 on v3

--- a/solution.py
+++ b/solution.py
@@ -214,20 +214,40 @@
     return functools.reduce(lambda a, b: a + b, [a.astype(jnp.float32) for a in arrays])
 
 
+def after(array, *others):
+    return lax.optimization_barrier((array, *others))[0]
+
+
 def boxed(packed, me, weight, chosen, blocks):
     far = swap(packed, 16)
     near = swap(packed, 8)
     layers = [packed, near, far, swap(far, 8)]
     halves, others = [], []
-    for rows in [packed, near, jnp.concatenate([far, layers[3]], axis=0)]:
+    for rows in [packed, near]:
         first = swap(rows, 2, 4)
         second = swap(rows, 4, 2)
         third = swap(first, 4, 2)
         half = jnp.concatenate([rows, first, second, third], axis=0)
         halves.append(half)
         others.append(swap(half, 1))
+    fars = jnp.concatenate([far, layers[3]], axis=0)
+    first = swap(fars, 2, 4)
+    second = swap(fars, 4, 2)
+    early = jnp.concatenate([fars, first, second], axis=0)
+    early = after(early, others[0])
+    early_other = swap(early, 1)
+    third = swap(first, 4, 2)
+    third_other = swap(third, 1)
     four = len(layers)
-    *scaled, code, energy = expert_rows(me, halves + others, weight, chosen, blocks)
+    *scaled, code, energy = expert_rows(
+        me, halves + [early, third] + others + [early_other, third_other], weight, chosen, blocks
+    )
+    scaled = [
+        *scaled[:2],
+        jnp.concatenate(scaled[2:4], axis=0),
+        *scaled[4:6],
+        jnp.concatenate(scaled[6:8], axis=0),
+    ]
     tok_rows = packed.shape[0]
 
     def by_layer(parts):

time: 64.2 us -> 63.1 us (0.983)
  starting transfers between devices: 25.1 us -> 24.3 us
    ppermute x22 -> x23, starting transfers between devices: 25.1 us -> 24.3 us  [swap(): lax.ppermute(array, 'expert', [(i, i ^ (odd if i & 1 else even)) for i in...]
    ppermute x22 -> x23, waiting for transfers between devices: 24.6 us -> 24.6 us  [swap(): lax.ppermute(array, 'expert', [(i, i ^ (odd if i & 1 else even)) for i in...]
  transfers between devices with their start and end apart: 22 -> 23, of which waited for: 11 -> 13; matrix products, arithmetic and copies ran while one was open for 2% -> 2% of each run, Pallas kernels for 3% -> 3%
where the time goes in v4:
time: 63.1 us; the launch traced here: 62.9 us
  waiting for transfers between devices  24.6 us (39%)
  starting transfers between devices  24.3 us (39%)
  Pallas kernels  11.2 us (18%)
  other arithmetic  1.92 us (3%)
  between operations  0.78 us (1%)
    ppermute x23, waiting for transfers between devices, swap(): lax.ppermute(array, 'expert', [(i, i ^ (odd if i & 1 else even)) for i in...  24.6 us
    ppermute x23, starting transfers between devices, swap(): lax.ppermute(array, 'expert', [(i, i ^ (odd if i & 1 else even)) for i in...  24.3 us
    pallas_call x1, Pallas kernels, expert_rows(): pl.pallas_call(functools.partial(expert_kernel, chosen, blocks, len(parts...  7.45 us
    pallas_call x1, Pallas kernels, expert_histogram(): pl.pallas_call(functools.partial(histogram_kernel, blocks, len(codes)), o...  2 us
    pallas_call x1, Pallas kernels, pack_rows(): pl.pallas_call(pack_kernel, out_shape=jax.ShapeDtypeStruct((tok_rows, wid...  1.76 us
  transfers between devices with their start and end apart: 23, of which 13 were waited for; matrix products, arithmetic and copies ran while one was open for 2% of the time, Pallas kernels for 3%

profile of v4, /device:TPU:0, one launch (start us, length us, event | category | flops | bytes accessed | tf_op | source)
XLA Modules:
  0.0 62.9 jit_solution(12599722478262056056)
XLA Ops:
  0.6 1.8 %pack_rows.1 = bf16[16,3712]{1,0:T(8,128)(2,1)} custom-call(bf16[16,3584]{1,0:T(8,128)(2,1)} %tokens_ref.1, s32[8,16]{1,0:T(8,128)} %bitcast.64, f32[8,16]{1,0:T(8,128)} %bitcast.65, s32[64,16]{1,0:T(8,128)} %bitcast.63), custom_call_target="tpu_custom_call" | custom-call | tf_op jit(solution)/shard_map/pack_rows/pallas_call | solution.py:47
  2.4 3.0 %collective-permute-start.3 = (bf16[16,3712]{1,0:T(8,128)(2,1)}, bf16[16,3712]{1,0:T(8,128)(2,1)S(1)}, u32[]{:S(2)}, u32[]{:S(2)}) collective-permute-start(bf16[16,3712]{1,0:T(8,128)(2,1)} %pack_rows.1), channel_id=1, source_target_pairs={{0,8},{1,9},{2,10},{3,11},{4,12},{5,13},{6,14},{7,15},{8,0},{9,1},... | collective-permute-start | bytes 356360 | tf_op jit(solution)/shard_map/ppermute | solution.py:210
  5.4 2.6 %collective-permute-start.7 = (bf16[16,3712]{1,0:T(8,128)(2,1)}, bf16[16,3712]{1,0:T(8,128)(2,1)S(1)}, u32[]{:S(2)}, u32[]{:S(2)}) collective-permute-start(bf16[16,3712]{1,0:T(8,128)(2,1)} %pack_rows.1), channel_id=1, source_target_pairs={{0,16},{1,17},{2,18},{3,19},{4,20},{5,21},{6,22},{7,23},{8,24},{9,... | collective-permute-start | bytes 356360 | tf_op jit(solution)/shard_map/ppermute | solution.py:210
  8.0 1.5 %collective-permute-start.1 = (bf16[16,3712]{1,0:T(8,128)(2,1)}, bf16[16,3712]{1,0:T(8,128)(2,1)S(1)}, u32[]{:S(2)}, u32[]{:S(2)}) collective-permute-start(bf16[16,3712]{1,0:T(8,128)(2,1)} %pack_rows.1), channel_id=1, source_target_pairs={{0,4},{1,3},{2,6},{3,1},{4,0},{5,7},{6,2},{7,5},{8,12},{9,11},{10,... | collective-permute-start | bytes 356360 | tf_op jit(solution)/shard_map/ppermute | solution.py:210
  9.5 1.5 %collective-permute-start = (bf16[16,3712]{1,0:T(8,128)(2,1)}, bf16[16,3712]{1,0:T(8,128)(2,1)S(1)}, u32[]{:S(2)}, u32[]{:S(2)}) collective-permute-start(bf16[16,3712]{1,0:T(8,128)(2,1)} %pack_rows.1), channel_id=1, source_target_pairs={{0,2},{1,5},{2,0},{3,7},{4,6},{5,1},{6,4},{7,3},{8,10},{9,13},{10,... | collective-permute-start | bytes 356360 | tf_op jit(solution)/shard_map/ppermute | solution.py:210
  11.0 0.0 collective-permute-done.3
  11.0 1.0 %collective-permute-start.5 = (bf16[16,3712]{1,0:T(8,128)(2,1)S(1)}, bf16[16,3712]{1,0:T(8,128)(2,1)S(1)}, u32[]{:S(2)}, u32[]{:S(2)}) collective-permute-start(bf16[16,3712]{1,0:T(8,128)(2,1)S(1)} %collective-permute-done.3), channel_id=1, source_target_pairs={{0,4},{1,3},{2,6},{3,1},{4,0},{5,7},{6,2},{7,5},{8,12},{9,11},{10,... | collective-permute-start | bytes 356360 | tf_op jit(solution)/shard_map/ppermute | solution.py:210
  12.0 1.5 %collective-permute-start.4 = (bf16[16,3712]{1,0:T(8,128)(2,1)S(1)}, bf16[16,3712]{1,0:T(8,128)(2,1)S(1)}, u32[]{:S(2)}, u32[]{:S(2)}) collective-permute-start(bf16[16,3712]{1,0:T(8,128)(2,1)S(1)} %collective-permute-done.3), channel_id=1, source_target_pairs={{0,2},{1,5},{2,0},{3,7},{4,6},{5,1},{6,4},{7,3},{8,10},{9,13},{10,... | collective-permute-start | bytes 356360 | tf_op jit(solution)/shard_map/ppermute | solution.py:210
  13.5 0.3 collective-permute-done.7
  13.8 0.4 collective-permute-start.8
  14.3 0.6 collective-permute-done
  14.9 1.0 %collective-permute-start.2 = (bf16[16,3712]{1,0:T(8,128)(2,1)S(1)}, bf16[16,3712]{1,0:T(8,128)(2,1)S(1)}, u32[]{:S(2)}, u32[]{:S(2)}) collective-permute-start(bf16[16,3712]{1,0:T(8,128)(2,1)S(1)} %collective-permute-done), channel_id=1, source_target_pairs={{0,4},{1,3},{2,6},{3,1},{4,0},{5,7},{6,2},{7,5},{8,12},{9,11},{10,... | collective-permute-start | bytes 356360 | tf_op jit(solution)/shard_map/ppermute | solution.py:210
  15.9 2.8 %collective-permute-done.8 = bf16[16,3712]{1,0:T(8,128)(2,1)S(1)} collective-permute-done((bf16[16,3712]{1,0:T(8,128)(2,1)S(1)}, bf16[16,3712]{1,0:T(8,128)(2,1)S(1)}, u32[]{:S(2)}, u32[]{:S(2)}) %collective-permute-start.8) | collective-permute-done | bytes 118816 | tf_op jit(solution)/shard_map/ppermute | solution.py:210
  18.7 1.6 %collective-permute-start.10 = (bf16[32,3712]{1,0:T(8,128)(2,1)S(1)}, bf16[32,3712]{1,0:T(8,128)(2,1)S(1)}, u32[]{:S(2)}, u32[]{:S(2)}) collective-permute-start(bf16[32,3712]{1,0:T(8,128)(2,1)S(1)} %constant_dynamic-update-slice_fusion.4), channel_id=1, source_target_pairs={{0,4},{1,3},{2,6},{3,1},{4,0},{5,7},{6,2},{7,5},{8,12},{9,11},{10,... | collective-permute-start | bytes 712712 | tf_op jit(solution)/shard_map/ppermute | solution.py:210
  20.3 0.0 collective-permute-done.1
  20.3 1.5 %collective-permute-start.9 = (bf16[32,3712]{1,0:T(8,128)(2,1)S(1)}, bf16[32,3712]{1,0:T(8,128)(2,1)S(1)}, u32[]{:S(2)}, u32[]{:S(2)}) collective-permute-start(bf16[32,3712]{1,0:T(8,128)(2,1)S(1)} %constant_dynamic-update-slice_fusion.4), channel_id=1, source_target_pairs={{0,2},{1,5},{2,0},{3,7},{4,6},{5,1},{6,4},{7,3},{8,10},{9,13},{10,... | collective-permute-start | bytes 712712 | tf_op jit(solution)/shard_map/ppermute | solution.py:210
  21.8 0.0 collective-permute-done.2
  21.8 0.9 %pad_maximum_fusion.2.refs_0_ = bf16[64,3712]{1,0:T(8,128)(2,1)S(1)} fusion(bf16[16,3712]{1,0:T(8,128)(2,1)S(1)} %collective-permute-done.2, bf16[16,3712]{1,0:T(8,128)(2,1)S(1)} %collective-permute-done.1, bf16[16,3712]{1,0:T(8,128)(2,1)S(1)} %collective-permute-done, bf16[16,3712]{1,0:T(8,128)(2,1)} %pack_rows.1), kind=kLoop, calls=%fused_computation.3 | loop fusion | flops 1900544 | bytes 950272 | tf_op jit(solution)/shard_map/concatenate | solution.py:230
  22.7 0.1 collective-permute-start.11
  22.8 0.0 collective-permute-done.4
  22.8 0.6 collective-permute-start.6
  23.4 0.0 collective-permute-done.5
  23.4 1.4 %collective-permute-done.10 = bf16[32,3712]{1,0:T(8,128)(2,1)S(1)} collective-permute-done((bf16[32,3712]{1,0:T(8,128)(2,1)S(1)}, bf16[32,3712]{1,0:T(8,128)(2,1)S(1)}, u32[]{:S(2)}, u32[]{:S(2)}) %collective-permute-start.10) | collective-permute-done | bytes 237600 | tf_op jit(solution)/shard_map/ppermute | solution.py:210
  24.9 2.0 %collective-permute-done.9 = bf16[32,3712]{1,0:T(8,128)(2,1)S(1)} collective-permute-done((bf16[32,3712]{1,0:T(8,128)(2,1)S(1)}, bf16[32,3712]{1,0:T(8,128)(2,1)S(1)}, u32[]{:S(2)}, u32[]{:S(2)}) %collective-permute-start.9) | collective-permute-done | bytes 237600 | tf_op jit(solution)/shard_map/ppermute | solution.py:210
  26.8 0.1 pad_maximum_fusion.refs_2_
  26.9 0.0 copy-start
  26.9 0.0 collective-permute-done.11.refs_4_
  26.9 0.1 collective-permute-start.14
  27.0 0.7 %collective-permute-done.6 = bf16[16,3712]{1,0:T(8,128)(2,1)S(1)} collective-permute-done((bf16[16,3712]{1,0:T(8,128)(2,1)S(1)}, bf16[16,3712]{1,0:T(8,128)(2,1)S(1)}, u32[]{:S(2)}, u32[]{:S(2)}) %collective-permute-start.6) | collective-permute-done | bytes 118816 | tf_op jit(solution)/shard_map/ppermute | solution.py:210
  27.7 0.1 collective-permute-start.13
  27.8 0.5 collective-permute-start.12
  28.4 5.6 %collective-permute-done.12.refs_3_ = bf16[32,3712]{1,0:T(8,128)(2,1)S(1)} collective-permute-done((bf16[32,3712]{1,0:T(8,128)(2,1)S(1)}, bf16[32,3712]{1,0:T(8,128)(2,1)S(1)}, u32[]{:S(2)}, u32[]{:S(2)}) %collective-permute-start.12) | collective-permute-done | bytes 237600 | tf_op jit(solution)/shard_map/ppermute | solution.py:210
  34.0 0.0 collective-permute-start.15
  34.0 0.0 collective-permute-done.13.refs_5_
  34.0 1.5 %collective-permute-done.15.refs_7_ = bf16[32,3712]{1,0:T(8,128)(2,1)S(1)} collective-permute-done((bf16[32,3712]{1,0:T(8,128)(2,1)S(1)}, bf16[32,3712]{1,0:T(8,128)(2,1)S(1)}, u32[]{:S(2)}, u32[]{:S(2)}) %collective-permute-start.15) | collective-permute-done | bytes 237600 | tf_op jit(solution)/shard_map/ppermute | solution.py:210
  35.5 0.0 collective-permute-done.14.refs_6_
  35.5 0.0 copy-done
  35.5 7.5 %expert_rows.1 = (bf16[64,1024]{1,0:T(8,128)(2,1)S(1)}, bf16[64,1024]{1,0:T(8,128)(2,1)S(1)}, bf16[96,1024]{1,0:T(8,128)(2,1)S(1)}, bf16[32,1024]{1,0:T(8,128)(2...) custom-call(s32[1]{0:T(128)} %bitcast.me_ref, ...), custom_call_target="tpu_custom_call" | custom-call | flops 3758096384 | bytes 7340032 | tf_op jit(solution)/shard_map/expert_rows/pallas_call | solution.py:127
  43.0 0.2 collective-permute-start.16
  43.2 1.7 %collective-permute-done.16 = bf16[256,1024]{1,0:T(8,128)(2,1)S(1)} collective-permute-done((bf16[256,1024]{1,0:T(8,128)(2,1)S(1)}, bf16[256,1024]{1,0:T(8,128)(2,1)S(1)}, u32[]{:S(2)}, u32[]{:S(2)}) %collective-permute-start.16) | collective-permute-done | bytes 524320 | tf_op jit(solution)/shard_map/ppermute | solution.py:210
  45.0 0.2 convert_add_fusion
  45.2 1.7 %collective-permute-start.17 = (bf16[4,16,1024]{2,1,0:T(8,128)(2,1)S(1)}, bf16[4,16,1024]{2,1,0:T(8,128)(2,1)S(1)}, u32[]{:S(2)}, u32[]{:S(2)}) collective-permute-start(bf16[4,16,1024]{2,1,0:T(8,128)(2,1)S(1)} %get-tuple-element.28), channel_id=1, source_target_pairs={{0,6},{1,7},{2,4},{3,5},{4,2},{5,3},{6,0},{7,1},{8,14},{9,15},{10,... | collective-permute-start | bytes 393224 | tf_op jit(solution)/shard_map/ppermute | solution.py:210
  47.0 1.8 %collective-permute-start.19 = (bf16[4,16,1024]{2,1,0:T(8,128)(2,1)S(1)}, bf16[4,16,1024]{2,1,0:T(8,128)(2,1)S(1)}, u32[]{:S(2)}, u32[]{:S(2)}) collective-permute-start(bf16[4,16,1024]{2,1,0:T(8,128)(2,1)S(1)} %get-tuple-element.29), channel_id=1, source_target_pairs={{0,4},{1,3},{2,6},{3,1},{4,0},{5,7},{6,2},{7,5},{8,12},{9,11},{10,... | collective-permute-start | bytes 393224 | tf_op jit(solution)/shard_map/ppermute | solution.py:210
  48.8 0.0 collective-permute-start.18
  48.8 3.7 %collective-permute-done.17 = bf16[4,16,1024]{2,1,0:T(8,128)(2,1)S(1)} collective-permute-done((bf16[4,16,1024]{2,1,0:T(8,128)(2,1)S(1)}, bf16[4,16,1024]{2,1,0:T(8,128)(2,1)S(1)}, u32[]{:S(2)}, u32[]{:S(2)}) %collective-permute-start.17) | collective-permute-done | bytes 131104 | tf_op jit(solution)/shard_map/ppermute | solution.py:210
  52.5 2.0 %collective-permute-done.19 = bf16[4,16,1024]{2,1,0:T(8,128)(2,1)S(1)} collective-permute-done((bf16[4,16,1024]{2,1,0:T(8,128)(2,1)S(1)}, bf16[4,16,1024]{2,1,0:T(8,128)(2,1)S(1)}, u32[]{:S(2)}, u32[]{:S(2)}) %collective-permute-start.19) | collective-permute-done | bytes 131104 | tf_op jit(solution)/shard_map/ppermute | solution.py:210
  54.5 0.0 collective-permute-done.18
  54.5 0.1 fusion.8
  54.6 0.5 collective-permute-start.20
  55.1 2.4 %collective-permute-start.22 = (bf16[16,1024]{1,0:T(8,128)(2,1)S(1)}, bf16[16,1024]{1,0:T(8,128)(2,1)S(1)}, u32[]{:S(2)}, u32[]{:S(2)}) collective-permute-start(bf16[16,1024]{1,0:T(8,128)(2,1)S(1)} %get-tuple-element.34), channel_id=1, source_target_pairs={{0,24},{1,25},{2,26},{3,27},{4,28},{5,29},{6,30},{7,31},{8,16},{9,... | collective-permute-start | bytes 98312 | tf_op jit(solution)/shard_map/ppermute | solution.py:210
  57.5 0.7 %collective-permute-start.21 = (bf16[16,1024]{1,0:T(8,128)(2,1)S(1)}, bf16[16,1024]{1,0:T(8,128)(2,1)S(1)}, u32[]{:S(2)}, u32[]{:S(2)}) collective-permute-start(bf16[16,1024]{1,0:T(8,128)(2,1)S(1)} %get-tuple-element.35), channel_id=1, source_target_pairs={{0,16},{1,17},{2,18},{3,19},{4,20},{5,21},{6,22},{7,23},{8,24},{9,... | collective-permute-start | bytes 98312 | tf_op jit(solution)/shard_map/ppermute | solution.py:210
  58.2 2.0 %expert_histogram.1 = f32[8,2048]{1,0:T(8,128)} custom-call(f32[512,128]{1,0:T(8,128)S(1)} %get-tuple-element.22.refs_0_, f32[512,128]{1,0:T(8,128)S(1)} %get-tuple-element.23.refs_1_), custom_call_target="tpu_custom_call" | custom-call | flops 268435456 | bytes 524288 | tf_op jit(solution)/shard_map/expert_histogram/pallas_call | solution.py:194
  60.2 0.0 collective-permute-done.20
  60.2 0.7 %collective-permute-done.22 = bf16[16,1024]{1,0:T(8,128)(2,1)S(1)} collective-permute-done((bf16[16,1024]{1,0:T(8,128)(2,1)S(1)}, bf16[16,1024]{1,0:T(8,128)(2,1)S(1)}, u32[]{:S(2)}, u32[]{:S(2)}) %collective-permute-start.22) | collective-permute-done | bytes 32800 | tf_op jit(solution)/shard_map/ppermute | solution.py:210
  60.9 1.4 %collective-permute-done.21 = bf16[16,1024]{1,0:T(8,128)(2,1)S(1)} collective-permute-done((bf16[16,1024]{1,0:T(8,128)(2,1)S(1)}, bf16[16,1024]{1,0:T(8,128)(2,1)S(1)}, u32[]{:S(2)}, u32[]{:S(2)}) %collective-permute-start.21) | collective-permute-done | bytes 32800 | tf_op jit(solution)/shard_map/ppermute | solution.py:210
  62.3 0.6 %fusion.6 = bf16[16,1024]{1,0:T(8,128)(2,1)} fusion(f32[4,16,1024]{2,1,0:T(8,128)S(1)} %get-tuple-element.25, bf16[16,1024]{1,0:T(8,128)(2,1)S(1)} %collective-permute-done.22, bf16[16,1024]{1,0:T(8,128)(2,1)S(1)} %collective-permute-done.21, bf16[16,1024]{1,0:T(8,128)(2,1)S(1)} %collective-permute-done.20), kind=kLoop, calls=%fused_computation.16 | loop fusion | flops 114688 | bytes 196608 | tf_op jit(solution)/shard_map/convert_element_type | solution.py:270
  (12 shorter events, 0.2 us)
Async XLA Ops:
  2.4 8.6 %collective-permute-start.3 = (bf16[16,3712]{1,0:T(8,128)(2,1)}, bf16[16,3712]{1,0:T(8,128)(2,1)S(1)}, u32[]{:S(2)}, u32[]{:S(2)}) collective-permute-start(bf16[16,3712]{1,0:T(8,128)(2,1)} %pack_rows.1), channel_id=1, source_target_pairs={{0,8},{1,9},{2,10},{3,11},{4,12},{5,13},{6,14},{7,15},{8,0},{9,1},... | collective-permute-start | bytes 356360 | tf_op jit(solution)/shard_map/ppermute | solution.py:210
  5.4 8.4 %collective-permute-start.7 = (bf16[16,3712]{1,0:T(8,128)(2,1)}, bf16[16,3712]{1,0:T(8,128)(2,1)S(1)}, u32[]{:S(2)}, u32[]{:S(2)}) collective-permute-start(bf16[16,3712]{1,0:T(8,128)(2,1)} %pack_rows.1), channel_id=1, source_target_pairs={{0,16},{1,17},{2,18},{3,19},{4,20},{5,21},{6,22},{7,23},{8,24},{9,... | collective-permute-start | bytes 356360 | tf_op jit(solution)/shard_map/ppermute | solution.py:210
  8.0 12.3 %collective-permute-start.1 = (bf16[16,3712]{1,0:T(8,128)(2,1)}, bf16[16,3712]{1,0:T(8,128)(2,1)S(1)}, u32[]{:S(2)}, u32[]{:S(2)}) collective-permute-start(bf16[16,3712]{1,0:T(8,128)(2,1)} %pack_rows.1), channel_id=1, source_target_pairs={{0,4},{1,3},{2,6},{3,1},{4,0},{5,7},{6,2},{7,5},{8,12},{9,11},{10,... | collective-permute-start | bytes 356360 | tf_op jit(solution)/shard_map/ppermute | solution.py:210
  9.5 5.3 %collective-permute-start = (bf16[16,3712]{1,0:T(8,128)(2,1)}, bf16[16,3712]{1,0:T(8,128)(2,1)S(1)}, u32[]{:S(2)}, u32[]{:S(2)}) collective-permute-start(bf16[16,3712]{1,0:T(8,128)(2,1)} %pack_rows.1), channel_id=1, source_target_pairs={{0,2},{1,5},{2,0},{3,7},{4,6},{5,1},{6,4},{7,3},{8,10},{9,13},{10,... | collective-permute-start | bytes 356360 | tf_op jit(solution)/shard_map/ppermute | solution.py:210
  11.0 12.4 %collective-permute-start.5 = (bf16[16,3712]{1,0:T(8,128)(2,1)S(1)}, bf16[16,3712]{1,0:T(8,128)(2,1)S(1)}, u32[]{:S(2)}, u32[]{:S(2)}) collective-permute-start(bf16[16,3712]{1,0:T(8,128)(2,1)S(1)} %collective-permute-done.3), channel_id=1, source_target_pairs={{0,4},{1,3},{2,6},{3,1},{4,0},{5,7},{6,2},{7,5},{8,12},{9,11},{10,... | collective-permute-start | bytes 356360 | tf_op jit(solution)/shard_map/ppermute | solution.py:210
  12.0 10.8 %collective-permute-start.4 = (bf16[16,3712]{1,0:T(8,128)(2,1)S(1)}, bf16[16,3712]{1,0:T(8,128)(2,1)S(1)}, u32[]{:S(2)}, u32[]{:S(2)}) collective-permute-start(bf16[16,3712]{1,0:T(8,128)(2,1)S(1)} %collective-permute-done.3), channel_id=1, source_target_pairs={{0,2},{1,5},{2,0},{3,7},{4,6},{5,1},{6,4},{7,3},{8,10},{9,13},{10,... | collective-permute-start | bytes 356360 | tf_op jit(solution)/shard_map/ppermute | solution.py:210
  13.8 4.8 %collective-permute-start.8 = (bf16[16,3712]{1,0:T(8,128)(2,1)S(1)}, bf16[16,3712]{1,0:T(8,128)(2,1)S(1)}, u32[]{:S(2)}, u32[]{:S(2)}) collective-permute-start(bf16[16,3712]{1,0:T(8,128)(2,1)S(1)} %collective-permute-done.7), channel_id=1, source_target_pairs={{0,8},{1,9},{2,10},{3,11},{4,12},{5,13},{6,14},{7,15},{8,0},{9,1},... | collective-permute-start | bytes 356360 | tf_op jit(solution)/shard_map/ppermute | solution.py:210
  14.9 6.9 %collective-permute-start.2 = (bf16[16,3712]{1,0:T(8,128)(2,1)S(1)}, bf16[16,3712]{1,0:T(8,128)(2,1)S(1)}, u32[]{:S(2)}, u32[]{:S(2)}) collective-permute-start(bf16[16,3712]{1,0:T(8,128)(2,1)S(1)} %collective-permute-done), channel_id=1, source_target_pairs={{0,4},{1,3},{2,6},{3,1},{4,0},{5,7},{6,2},{7,5},{8,12},{9,11},{10,... | collective-permute-start | bytes 356360 | tf_op jit(solution)/shard_map/ppermute | solution.py:210
  18.7 6.2 %collective-permute-start.10 = (bf16[32,3712]{1,0:T(8,128)(2,1)S(1)}, bf16[32,3712]{1,0:T(8,128)(2,1)S(1)}, u32[]{:S(2)}, u32[]{:S(2)}) collective-permute-start(bf16[32,3712]{1,0:T(8,128)(2,1)S(1)} %constant_dynamic-update-slice_fusion.4), channel_id=1, source_target_pairs={{0,4},{1,3},{2,6},{3,1},{4,0},{5,7},{6,2},{7,5},{8,12},{9,11},{10,... | collective-permute-start | bytes 712712 | tf_op jit(solution)/shard_map/ppermute | solution.py:210
  20.3 6.5 %collective-permute-start.9 = (bf16[32,3712]{1,0:T(8,128)(2,1)S(1)}, bf16[32,3712]{1,0:T(8,128)(2,1)S(1)}, u32[]{:S(2)}, u32[]{:S(2)}) collective-permute-start(bf16[32,3712]{1,0:T(8,128)(2,1)S(1)} %constant_dynamic-update-slice_fusion.4), channel_id=1, source_target_pairs={{0,2},{1,5},{2,0},{3,7},{4,6},{5,1},{6,4},{7,3},{8,10},{9,13},{10,... | collective-permute-start | bytes 712712 | tf_op jit(solution)/shard_map/ppermute | solution.py:210
  22.7 4.2 %collective-permute-start.11 = (bf16[64,3712]{1,0:T(8,128)(2,1)S(1)}, bf16[64,3712]{1,0:T(8,128)(2,1)S(1)}, u32[]{:S(2)}, u32[]{:S(2)}) collective-permute-start(bf16[64,3712]{1,0:T(8,128)(2,1)S(1)} %pad_maximum_fusion.2.refs_0_), channel_id=1, source_target_pairs={{0,1},{1,0},{2,3},{3,2},{4,5},{5,4},{6,7},{7,6},{8,9},{9,8},{10,11... | collective-permute-start | bytes 1425416 | tf_op jit(solution)/shard_map/ppermute | solution.py:210
  22.8 4.9 %collective-permute-start.6 = (bf16[16,3712]{1,0:T(8,128)(2,1)S(1)}, bf16[16,3712]{1,0:T(8,128)(2,1)S(1)}, u32[]{:S(2)}, u32[]{:S(2)}) collective-permute-start(bf16[16,3712]{1,0:T(8,128)(2,1)S(1)} %collective-permute-done.4), channel_id=1, source_target_pairs={{0,4},{1,3},{2,6},{3,1},{4,0},{5,7},{6,2},{7,5},{8,12},{9,11},{10,... | collective-permute-start | bytes 356360 | tf_op jit(solution)/shard_map/ppermute | solution.py:210
  26.9 8.6 %copy-start = (bf16[96,3712]{1,0:T(8,128)(2,1)}, bf16[96,3712]{1,0:T(8,128)(2,1)S(1)}, u32[]{:S(2)}) copy-start(bf16[96,3712]{1,0:T(8,128)(2,1)S(1)} %pad_maximum_fusion.refs_2_) | copy-start | bytes 2138116
  26.9 8.6 %collective-permute-start.14 = (bf16[96,3712]{1,0:T(8,128)(2,1)S(1)}, bf16[96,3712]{1,0:T(8,128)(2,1)}, u32[]{:S(2)}, u32[]{:S(2)}) collective-permute-start(bf16[96,3712]{1,0:T(8,128)(2,1)S(1)} %pad_maximum_fusion.refs_2_), channel_id=1, source_target_pairs={{0,1},{1,0},{2,3},{3,2},{4,5},{5,4},{6,7},{7,6},{8,9},{9,8},{10,11... | collective-permute-start | bytes 2138120 | tf_op jit(solution)/shard_map/ppermute | solution.py:210
  27.7 6.3 %collective-permute-start.13 = (bf16[64,3712]{1,0:T(8,128)(2,1)S(1)}, bf16[64,3712]{1,0:T(8,128)(2,1)S(1)}, u32[]{:S(2)}, u32[]{:S(2)}) collective-permute-start(bf16[64,3712]{1,0:T(8,128)(2,1)S(1)} %constant_dynamic-update-slice_fusion.refs_1_), channel_id=1, source_target_pairs={{0,1},{1,0},{2,3},{3,2},{4,5},{5,4},{6,7},{7,6},{8,9},{9,8},{10,11... | collective-permute-start | bytes 1425416 | tf_op jit(solution)/shard_map/ppermute | solution.py:210
  27.8 6.1 %collective-permute-start.12 = (bf16[32,3712]{1,0:T(8,128)(2,1)S(1)}, bf16[32,3712]{1,0:T(8,128)(2,1)S(1)}, u32[]{:S(2)}, u32[]{:S(2)}) collective-permute-start(bf16[32,3712]{1,0:T(8,128)(2,1)S(1)} %collective-permute-done.9), channel_id=1, source_target_pairs={{0,4},{1,3},{2,6},{3,1},{4,0},{5,7},{6,2},{7,5},{8,12},{9,11},{10,... | collective-permute-start | bytes 712712 | tf_op jit(solution)/shard_map/ppermute | solution.py:210
  34.0 1.5 %collective-permute-start.15 = (bf16[32,3712]{1,0:T(8,128)(2,1)S(1)}, bf16[32,3712]{1,0:T(8,128)(2,1)S(1)}, u32[]{:S(2)}, u32[]{:S(2)}) collective-permute-start(bf16[32,3712]{1,0:T(8,128)(2,1)S(1)} %collective-permute-done.12.refs_3_), channel_id=1, source_target_pairs={{0,1},{1,0},{2,3},{3,2},{4,5},{5,4},{6,7},{7,6},{8,9},{9,8},{10,11... | collective-permute-start | bytes 712712 | tf_op jit(solution)/shard_map/ppermute | solution.py:210
  43.0 2.0 %collective-permute-start.16 = (bf16[256,1024]{1,0:T(8,128)(2,1)S(1)}, bf16[256,1024]{1,0:T(8,128)(2,1)S(1)}, u32[]{:S(2)}, u32[]{:S(2)}) collective-permute-start(bf16[256,1024]{1,0:T(8,128)(2,1)S(1)} %pad_maximum_fusion.1), channel_id=1, source_target_pairs={{0,1},{1,0},{2,3},{3,2},{4,5},{5,4},{6,7},{7,6},{8,9},{9,8},{10,11... | collective-permute-start | bytes 1572872 | tf_op jit(solution)/shard_map/ppermute | solution.py:210
  45.2 7.3 %collective-permute-start.17 = (bf16[4,16,1024]{2,1,0:T(8,128)(2,1)S(1)}, bf16[4,16,1024]{2,1,0:T(8,128)(2,1)S(1)}, u32[]{:S(2)}, u32[]{:S(2)}) collective-permute-start(bf16[4,16,1024]{2,1,0:T(8,128)(2,1)S(1)} %get-tuple-element.28), channel_id=1, source_target_pairs={{0,6},{1,7},{2,4},{3,5},{4,2},{5,3},{6,0},{7,1},{8,14},{9,15},{10,... | collective-permute-start | bytes 393224 | tf_op jit(solution)/shard_map/ppermute | solution.py:210
  47.0 7.6 %collective-permute-start.19 = (bf16[4,16,1024]{2,1,0:T(8,128)(2,1)S(1)}, bf16[4,16,1024]{2,1,0:T(8,128)(2,1)S(1)}, u32[]{:S(2)}, u32[]{:S(2)}) collective-permute-start(bf16[4,16,1024]{2,1,0:T(8,128)(2,1)S(1)} %get-tuple-element.29), channel_id=1, source_target_pairs={{0,4},{1,3},{2,6},{3,1},{4,0},{5,7},{6,2},{7,5},{8,12},{9,11},{10,... | collective-permute-start | bytes 393224 | tf_op jit(solution)/shard_map/ppermute | solution.py:210
  48.8 5.8 %collective-permute-start.18 = (bf16[4,16,1024]{2,1,0:T(8,128)(2,1)S(1)}, bf16[4,16,1024]{2,1,0:T(8,128)(2,1)S(1)}, u32[]{:S(2)}, u32[]{:S(2)}) collective-permute-start(bf16[4,16,1024]{2,1,0:T(8,128)(2,1)S(1)} %get-tuple-element.30), channel_id=1, source_target_pairs={{0,2},{1,5},{2,0},{3,7},{4,6},{5,1},{6,4},{7,3},{8,10},{9,13},{10,... | collective-permute-start | bytes 393224 | tf_op jit(solution)/shard_map/ppermute | solution.py:210
  54.6 5.6 %collective-permute-start.20 = (bf16[16,1024]{1,0:T(8,128)(2,1)S(1)}, bf16[16,1024]{1,0:T(8,128)(2,1)S(1)}, u32[]{:S(2)}, u32[]{:S(2)}) collective-permute-start(bf16[16,1024]{1,0:T(8,128)(2,1)S(1)} %get-tuple-element.33), channel_id=1, source_target_pairs={{0,8},{1,9},{2,10},{3,11},{4,12},{5,13},{6,14},{7,15},{8,0},{9,1},... | collective-permute-start | bytes 98312 | tf_op jit(solution)/shard_map/ppermute | solution.py:210
  55.1 5.8 %collective-permute-start.22 = (bf16[16,1024]{1,0:T(8,128)(2,1)S(1)}, bf16[16,1024]{1,0:T(8,128)(2,1)S(1)}, u32[]{:S(2)}, u32[]{:S(2)}) collective-permute-start(bf16[16,1024]{1,0:T(8,128)(2,1)S(1)} %get-tuple-element.34), channel_id=1, source_target_pairs={{0,24},{1,25},{2,26},{3,27},{4,28},{5,29},{6,30},{7,31},{8,16},{9,... | collective-permute-start | bytes 98312 | tf_op jit(solution)/shard_map/ppermute | solution.py:210
  57.5 4.8 %collective-permute-start.21 = (bf16[16,1024]{1,0:T(8,128)(2,1)S(1)}, bf16[16,1024]{1,0:T(8,128)(2,1)S(1)}, u32[]{:S(2)}, u32[]{:S(2)}) collective-permute-start(bf16[16,1024]{1,0:T(8,128)(2,1)S(1)} %get-tuple-element.35), channel_id=1, source_target_pairs={{0,16},{1,17},{2,18},{3,19},{4,20},{5,21},{6,22},{7,23},{8,24},{9,... | collective-permute-start | bytes 98312 | tf_op jit(solution)/shard_map/ppermute | solution.py:210

commit v5 on v4

--- a/solution.py
+++ b/solution.py
@@ -11,7 +11,6 @@
 NBINS = 2048
 LANES = 128
 TILE_N = 256
-K_SLICES = 7
 
 route_scale = 2.827
 
@@ -56,6 +55,13 @@
     )
 
 
+def weight_spans(width):
+    unit = width // 14
+    depths = [unit * n for n in (1, 2, 3, 4)]
+    depths.append(width - sum(depths))
+    return [(sum(depths[:i]), depth) for i, depth in enumerate(depths)]
+
+
 def expert_kernel(chosen, blocks, n_parts, me_ref, *refs):
     parts = refs[:n_parts]
     w_ref = refs[n_parts]
@@ -64,12 +70,12 @@
     width, hidden = w_ref.shape
     tile = min(TILE_N, hidden)
     slices = sems.shape[0]
-    depth = width // slices
+    spans = weight_spans(width)
     copies = [
         pltpu.make_async_copy(
-            w_ref.at[pl.ds(i * depth, depth)], held.at[pl.ds(i * depth, depth)], sems.at[i]
+            w_ref.at[pl.ds(start, depth)], held.at[pl.ds(start, depth)], sems.at[i]
         )
-        for i in range(slices)
+        for i, (start, depth) in enumerate(spans)
     ]
     for copy in copies:
         copy.start()
@@ -98,24 +104,26 @@
     slot = lax.broadcasted_iota(jnp.int32, (tile, LANES), 1) % blocks
     for i, copy in enumerate(copies):
         copy.wait()
-        span = slice(i * depth, (i + 1) * depth)
+        span = slice(spans[i][0], sum(spans[i]))
         rows = jnp.concatenate([p[:, span] for p in parts], axis=0)
         for j in range(0, hidden, tile):
-            term = jnp.dot(rows, held[span, j : j + tile], preferred_element_type=jnp.float32)
-            up_ref[:, j : j + tile] = term if i == 0 else up_ref[:, j : j + tile] + term
-    for i in range(hidden // tile):
-        up = up_ref[:, i * tile : (i + 1) * tile]
-        mean = jnp.where((unit + i * tile) // BLOCK == slot, 1.0 / BLOCK, 0.0)
-        energy += jnp.dot(
-            (up * up).astype(jnp.bfloat16),
-            mean.astype(jnp.bfloat16),
-            preferred_element_type=jnp.float32,
-        )
-        scaled = (weight * up.astype(jnp.bfloat16).astype(jnp.float32)).astype(jnp.bfloat16)
-        at = 0
-        for part, out in zip(parts, outs):
-            out[:, i * tile : (i + 1) * tile] = scaled[at : at + part.shape[0]]
-            at += part.shape[0]
+            up = jnp.dot(rows, held[span, j : j + tile], preferred_element_type=jnp.float32)
+            if i > 0:
+                up += up_ref[:, j : j + tile]
+            if i < slices - 1:
+                up_ref[:, j : j + tile] = up
+                continue
+            mean = jnp.where((unit + j) // BLOCK == slot, 1.0 / BLOCK, 0.0)
+            energy += jnp.dot(
+                (up * up).astype(jnp.bfloat16),
+                mean.astype(jnp.bfloat16),
+                preferred_element_type=jnp.float32,
+            )
+            scaled = (weight * up.astype(jnp.bfloat16).astype(jnp.float32)).astype(jnp.bfloat16)
+            at = 0
+            for part, out in zip(parts, outs):
+                out[:, j : j + tile] = scaled[at : at + part.shape[0]]
+                at += part.shape[0]
     energy_ref[...] = energy
 
 
@@ -135,7 +143,7 @@
         scratch_shapes=[
             pltpu.VMEM((width, hidden), weight.dtype),
             pltpu.VMEM((total, hidden), jnp.float32),
-            pltpu.SemaphoreType.DMA((K_SLICES,)),
+            pltpu.SemaphoreType.DMA((len(weight_spans(width)),)),
         ],
         compiler_params=pltpu.CompilerParams(vmem_limit_bytes=50 * 1024 * 1024),
         cost_estimate=pl.CostEstimate(
@@ -266,9 +274,11 @@
         swap(leaving[:, 0], 2, 4),
         swap(leaving[:, 1], 4, 2),
     )
+    histogram = expert_histogram([code], [energy], blocks)
+    partial = after(partial, histogram)
     home = [swap(partial[i].astype(jnp.bfloat16), 8 * i) for i in range(1, four)]
     mixed = add32(partial[0], *home).astype(jnp.bfloat16)
-    return mixed, expert_histogram([code], [energy], blocks)
+    return mixed, histogram
 
 
 def plain(packed, me, weight, chosen, blocks):

time: 63.1 us -> 62.9 us (level)
  transfers between devices with their start and end apart: 23 -> 23, of which waited for: 13 -> 14; matrix products, arithmetic and copies ran while one was open for 2% -> 2% of each run, Pallas kernels for 3% -> 3%
where the time goes in v5:
time: 62.9 us; the launch traced here: 62.7 us
  waiting for transfers between devices  24.6 us (39%)
  starting transfers between devices  24.3 us (39%)
  Pallas kernels  11 us (17%)
  other arithmetic  1.93 us (3%)
  between operations  0.79 us (1%)
    ppermute x23, waiting for transfers between devices, swap(): lax.ppermute(array, 'expert', [(i, i ^ (odd if i & 1 else even)) for i in...  24.6 us
    ppermute x23, starting transfers between devices, swap(): lax.ppermute(array, 'expert', [(i, i ^ (odd if i & 1 else even)) for i in...  24.3 us
    pallas_call x1, Pallas kernels, expert_rows(): pl.pallas_call(functools.partial(expert_kernel, chosen, blocks, len(parts...  7.19 us
    pallas_call x1, Pallas kernels, expert_histogram(): pl.pallas_call(functools.partial(histogram_kernel, blocks, len(codes)), o...  2 us
    pallas_call x1, Pallas kernels, pack_rows(): pl.pallas_call(pack_kernel, out_shape=jax.ShapeDtypeStruct((tok_rows, wid...  1.76 us
  transfers between devices with their start and end apart: 23, of which 14 were waited for; matrix products, arithmetic and copies ran while one was open for 2% of the time, Pallas kernels for 3%

profile of v5, /device:TPU:0, one launch (start us, length us, event | category | flops | bytes accessed | tf_op | source)
XLA Modules:
  0.0 62.7 jit_solution(18278449788148763858)
XLA Ops:
  0.6 1.8 %pack_rows.1 = bf16[16,3712]{1,0:T(8,128)(2,1)} custom-call(bf16[16,3584]{1,0:T(8,128)(2,1)} %tokens_ref.1, s32[8,16]{1,0:T(8,128)} %bitcast.61, f32[8,16]{1,0:T(8,128)} %bitcast.62, s32[64,16]{1,0:T(8,128)} %bitcast.60), custom_call_target="tpu_custom_call" | custom-call | tf_op jit(solution)/shard_map/pack_rows/pallas_call | solution.py:46
  2.4 3.0 %collective-permute-start.3 = (bf16[16,3712]{1,0:T(8,128)(2,1)}, bf16[16,3712]{1,0:T(8,128)(2,1)S(1)}, u32[]{:S(2)}, u32[]{:S(2)}) collective-permute-start(bf16[16,3712]{1,0:T(8,128)(2,1)} %pack_rows.1), channel_id=1, source_target_pairs={{0,8},{1,9},{2,10},{3,11},{4,12},{5,13},{6,14},{7,15},{8,0},{9,1},... | collective-permute-start | bytes 356360 | tf_op jit(solution)/shard_map/ppermute | solution.py:218
  5.4 2.6 %collective-permute-start.7 = (bf16[16,3712]{1,0:T(8,128)(2,1)}, bf16[16,3712]{1,0:T(8,128)(2,1)S(1)}, u32[]{:S(2)}, u32[]{:S(2)}) collective-permute-start(bf16[16,3712]{1,0:T(8,128)(2,1)} %pack_rows.1), channel_id=1, source_target_pairs={{0,16},{1,17},{2,18},{3,19},{4,20},{5,21},{6,22},{7,23},{8,24},{9,... | collective-permute-start | bytes 356360 | tf_op jit(solution)/shard_map/ppermute | solution.py:218
  8.0 1.5 %collective-permute-start.1 = (bf16[16,3712]{1,0:T(8,128)(2,1)}, bf16[16,3712]{1,0:T(8,128)(2,1)S(1)}, u32[]{:S(2)}, u32[]{:S(2)}) collective-permute-start(bf16[16,3712]{1,0:T(8,128)(2,1)} %pack_rows.1), channel_id=1, source_target_pairs={{0,4},{1,3},{2,6},{3,1},{4,0},{5,7},{6,2},{7,5},{8,12},{9,11},{10,... | collective-permute-start | bytes 356360 | tf_op jit(solution)/shard_map/ppermute | solution.py:218
  9.5 1.5 %collective-permute-start = (bf16[16,3712]{1,0:T(8,128)(2,1)}, bf16[16,3712]{1,0:T(8,128)(2,1)S(1)}, u32[]{:S(2)}, u32[]{:S(2)}) collective-permute-start(bf16[16,3712]{1,0:T(8,128)(2,1)} %pack_rows.1), channel_id=1, source_target_pairs={{0,2},{1,5},{2,0},{3,7},{4,6},{5,1},{6,4},{7,3},{8,10},{9,13},{10,... | collective-permute-start | bytes 356360 | tf_op jit(solution)/shard_map/ppermute | solution.py:218
  11.0 0.0 collective-permute-done.3
  11.0 1.0 %collective-permute-start.5 = (bf16[16,3712]{1,0:T(8,128)(2,1)S(1)}, bf16[16,3712]{1,0:T(8,128)(2,1)S(1)}, u32[]{:S(2)}, u32[]{:S(2)}) collective-permute-start(bf16[16,3712]{1,0:T(8,128)(2,1)S(1)} %collective-permute-done.3), channel_id=1, source_target_pairs={{0,4},{1,3},{2,6},{3,1},{4,0},{5,7},{6,2},{7,5},{8,12},{9,11},{10,... | collective-permute-start | bytes 356360 | tf_op jit(solution)/shard_map/ppermute | solution.py:218
  12.0 1.5 %collective-permute-start.4 = (bf16[16,3712]{1,0:T(8,128)(2,1)S(1)}, bf16[16,3712]{1,0:T(8,128)(2,1)S(1)}, u32[]{:S(2)}, u32[]{:S(2)}) collective-permute-start(bf16[16,3712]{1,0:T(8,128)(2,1)S(1)} %collective-permute-done.3), channel_id=1, source_target_pairs={{0,2},{1,5},{2,0},{3,7},{4,6},{5,1},{6,4},{7,3},{8,10},{9,13},{10,... | collective-permute-start | bytes 356360 | tf_op jit(solution)/shard_map/ppermute | solution.py:218
  13.5 0.3 collective-permute-done.7
  13.8 0.4 collective-permute-start.8
  14.3 0.6 collective-permute-done
  14.9 1.0 %collective-permute-start.2 = (bf16[16,3712]{1,0:T(8,128)(2,1)S(1)}, bf16[16,3712]{1,0:T(8,128)(2,1)S(1)}, u32[]{:S(2)}, u32[]{:S(2)}) collective-permute-start(bf16[16,3712]{1,0:T(8,128)(2,1)S(1)} %collective-permute-done), channel_id=1, source_target_pairs={{0,4},{1,3},{2,6},{3,1},{4,0},{5,7},{6,2},{7,5},{8,12},{9,11},{10,... | collective-permute-start | bytes 356360 | tf_op jit(solution)/shard_map/ppermute | solution.py:218
  15.9 2.8 %collective-permute-done.8 = bf16[16,3712]{1,0:T(8,128)(2,1)S(1)} collective-permute-done((bf16[16,3712]{1,0:T(8,128)(2,1)S(1)}, bf16[16,3712]{1,0:T(8,128)(2,1)S(1)}, u32[]{:S(2)}, u32[]{:S(2)}) %collective-permute-start.8) | collective-permute-done | bytes 118816 | tf_op jit(solution)/shard_map/ppermute | solution.py:218
  18.7 1.6 %collective-permute-start.10 = (bf16[32,3712]{1,0:T(8,128)(2,1)S(1)}, bf16[32,3712]{1,0:T(8,128)(2,1)S(1)}, u32[]{:S(2)}, u32[]{:S(2)}) collective-permute-start(bf16[32,3712]{1,0:T(8,128)(2,1)S(1)} %constant_dynamic-update-slice_fusion.4), channel_id=1, source_target_pairs={{0,4},{1,3},{2,6},{3,1},{4,0},{5,7},{6,2},{7,5},{8,12},{9,11},{10,... | collective-permute-start | bytes 712712 | tf_op jit(solution)/shard_map/ppermute | solution.py:218
  20.3 0.0 collective-permute-done.1
  20.3 1.5 %collective-permute-start.9 = (bf16[32,3712]{1,0:T(8,128)(2,1)S(1)}, bf16[32,3712]{1,0:T(8,128)(2,1)S(1)}, u32[]{:S(2)}, u32[]{:S(2)}) collective-permute-start(bf16[32,3712]{1,0:T(8,128)(2,1)S(1)} %constant_dynamic-update-slice_fusion.4), channel_id=1, source_target_pairs={{0,2},{1,5},{2,0},{3,7},{4,6},{5,1},{6,4},{7,3},{8,10},{9,13},{10,... | collective-permute-start | bytes 712712 | tf_op jit(solution)/shard_map/ppermute | solution.py:218
  21.8 0.0 collective-permute-done.2
  21.8 0.9 %pad_maximum_fusion.2.refs_0_ = bf16[64,3712]{1,0:T(8,128)(2,1)S(1)} fusion(bf16[16,3712]{1,0:T(8,128)(2,1)S(1)} %collective-permute-done.2, bf16[16,3712]{1,0:T(8,128)(2,1)S(1)} %collective-permute-done.1, bf16[16,3712]{1,0:T(8,128)(2,1)S(1)} %collective-permute-done, bf16[16,3712]{1,0:T(8,128)(2,1)} %pack_rows.1), kind=kLoop, calls=%fused_computation.3 | loop fusion | flops 1900544 | bytes 950272 | tf_op jit(solution)/shard_map/concatenate | solution.py:238
  22.7 0.1 collective-permute-start.11
  22.8 0.0 collective-permute-done.4
  22.8 0.6 collective-permute-start.6
  23.4 0.0 collective-permute-done.5
  23.4 1.4 %collective-permute-done.10 = bf16[32,3712]{1,0:T(8,128)(2,1)S(1)} collective-permute-done((bf16[32,3712]{1,0:T(8,128)(2,1)S(1)}, bf16[32,3712]{1,0:T(8,128)(2,1)S(1)}, u32[]{:S(2)}, u32[]{:S(2)}) %collective-permute-start.10) | collective-permute-done | bytes 237600 | tf_op jit(solution)/shard_map/ppermute | solution.py:218
  24.9 2.0 %collective-permute-done.9 = bf16[32,3712]{1,0:T(8,128)(2,1)S(1)} collective-permute-done((bf16[32,3712]{1,0:T(8,128)(2,1)S(1)}, bf16[32,3712]{1,0:T(8,128)(2,1)S(1)}, u32[]{:S(2)}, u32[]{:S(2)}) %collective-permute-start.9) | collective-permute-done | bytes 237600 | tf_op jit(solution)/shard_map/ppermute | solution.py:218
  26.8 0.1 pad_maximum_fusion.refs_2_
  26.9 0.0 copy-start
  26.9 0.0 collective-permute-done.11.refs_4_
  26.9 0.1 collective-permute-start.14
  27.0 0.7 %collective-permute-done.6 = bf16[16,3712]{1,0:T(8,128)(2,1)S(1)} collective-permute-done((bf16[16,3712]{1,0:T(8,128)(2,1)S(1)}, bf16[16,3712]{1,0:T(8,128)(2,1)S(1)}, u32[]{:S(2)}, u32[]{:S(2)}) %collective-permute-start.6) | collective-permute-done | bytes 118816 | tf_op jit(solution)/shard_map/ppermute | solution.py:218
  27.7 0.1 collective-permute-start.13
  27.8 0.5 collective-permute-start.12
  28.4 5.6 %collective-permute-done.12.refs_3_ = bf16[32,3712]{1,0:T(8,128)(2,1)S(1)} collective-permute-done((bf16[32,3712]{1,0:T(8,128)(2,1)S(1)}, bf16[32,3712]{1,0:T(8,128)(2,1)S(1)}, u32[]{:S(2)}, u32[]{:S(2)}) %collective-permute-start.12) | collective-permute-done | bytes 237600 | tf_op jit(solution)/shard_map/ppermute | solution.py:218
  34.0 0.0 collective-permute-start.15
  34.0 0.0 collective-permute-done.13.refs_5_
  34.0 1.5 %collective-permute-done.15.refs_7_ = bf16[32,3712]{1,0:T(8,128)(2,1)S(1)} collective-permute-done((bf16[32,3712]{1,0:T(8,128)(2,1)S(1)}, bf16[32,3712]{1,0:T(8,128)(2,1)S(1)}, u32[]{:S(2)}, u32[]{:S(2)}) %collective-permute-start.15) | collective-permute-done | bytes 237600 | tf_op jit(solution)/shard_map/ppermute | solution.py:218
  35.5 0.0 collective-permute-done.14.refs_6_
  35.5 0.0 copy-done
  35.5 7.2 %expert_rows.1 = (bf16[64,1024]{1,0:T(8,128)(2,1)S(1)}, bf16[64,1024]{1,0:T(8,128)(2,1)S(1)}, bf16[96,1024]{1,0:T(8,128)(2,1)S(1)}, bf16[32,1024]{1,0:T(8,128)(2...) custom-call(s32[1]{0:T(128)} %bitcast.me_ref, ...), custom_call_target="tpu_custom_call" | custom-call | flops 3758096384 | bytes 7340032 | tf_op jit(solution)/shard_map/expert_rows/pallas_call | solution.py:135
  42.7 0.2 collective-permute-start.16
  42.9 1.8 %collective-permute-done.16 = bf16[256,1024]{1,0:T(8,128)(2,1)S(1)} collective-permute-done((bf16[256,1024]{1,0:T(8,128)(2,1)S(1)}, bf16[256,1024]{1,0:T(8,128)(2,1)S(1)}, u32[]{:S(2)}, u32[]{:S(2)}) %collective-permute-start.16) | collective-permute-done | bytes 524320 | tf_op jit(solution)/shard_map/ppermute | solution.py:218
  44.7 0.2 fusion.6
  45.0 1.7 %collective-permute-start.17 = (bf16[4,16,1024]{2,1,0:T(8,128)(2,1)S(1)}, bf16[4,16,1024]{2,1,0:T(8,128)(2,1)S(1)}, u32[]{:S(2)}, u32[]{:S(2)}) collective-permute-start(bf16[4,16,1024]{2,1,0:T(8,128)(2,1)S(1)} %get-tuple-element.28), channel_id=1, source_target_pairs={{0,6},{1,7},{2,4},{3,5},{4,2},{5,3},{6,0},{7,1},{8,14},{9,15},{10,... | collective-permute-start | bytes 393224 | tf_op jit(solution)/shard_map/ppermute | solution.py:218
  46.7 1.8 %collective-permute-start.19 = (bf16[4,16,1024]{2,1,0:T(8,128)(2,1)S(1)}, bf16[4,16,1024]{2,1,0:T(8,128)(2,1)S(1)}, u32[]{:S(2)}, u32[]{:S(2)}) collective-permute-start(bf16[4,16,1024]{2,1,0:T(8,128)(2,1)S(1)} %get-tuple-element.29), channel_id=1, source_target_pairs={{0,4},{1,3},{2,6},{3,1},{4,0},{5,7},{6,2},{7,5},{8,12},{9,11},{10,... | collective-permute-start | bytes 393224 | tf_op jit(solution)/shard_map/ppermute | solution.py:218
  48.5 0.0 collective-permute-start.18
  48.5 2.0 %expert_histogram.1 = f32[8,2048]{1,0:T(8,128)} custom-call(f32[512,128]{1,0:T(8,128)S(1)} %get-tuple-element.23.refs_0_, f32[512,128]{1,0:T(8,128)S(1)} %get-tuple-element.24.refs_1_), custom_call_target="tpu_custom_call" | custom-call | flops 268435456 | bytes 524288 | tf_op jit(solution)/shard_map/expert_histogram/pallas_call | solution.py:202
  50.5 1.7 %collective-permute-done.17 = bf16[4,16,1024]{2,1,0:T(8,128)(2,1)S(1)} collective-permute-done((bf16[4,16,1024]{2,1,0:T(8,128)(2,1)S(1)}, bf16[4,16,1024]{2,1,0:T(8,128)(2,1)S(1)}, u32[]{:S(2)}, u32[]{:S(2)}) %collective-permute-start.17) | collective-permute-done | bytes 131104 | tf_op jit(solution)/shard_map/ppermute | solution.py:218
  52.3 2.0 %collective-permute-done.19 = bf16[4,16,1024]{2,1,0:T(8,128)(2,1)S(1)} collective-permute-done((bf16[4,16,1024]{2,1,0:T(8,128)(2,1)S(1)}, bf16[4,16,1024]{2,1,0:T(8,128)(2,1)S(1)}, u32[]{:S(2)}, u32[]{:S(2)}) %collective-permute-start.19) | collective-permute-done | bytes 131104 | tf_op jit(solution)/shard_map/ppermute | solution.py:218
  54.3 0.0 collective-permute-done.18
  54.3 0.1 fusion.2
  54.4 0.5 collective-permute-start.20
  54.9 2.4 %collective-permute-start.22 = (bf16[16,1024]{1,0:T(8,128)(2,1)S(1)}, bf16[16,1024]{1,0:T(8,128)(2,1)S(1)}, u32[]{:S(2)}, u32[]{:S(2)}) collective-permute-start(bf16[16,1024]{1,0:T(8,128)(2,1)S(1)} %get-tuple-element.34), channel_id=1, source_target_pairs={{0,24},{1,25},{2,26},{3,27},{4,28},{5,29},{6,30},{7,31},{8,16},{9,... | collective-permute-start | bytes 98312 | tf_op jit(solution)/shard_map/ppermute | solution.py:218
  57.2 0.7 %collective-permute-start.21 = (bf16[16,1024]{1,0:T(8,128)(2,1)S(1)}, bf16[16,1024]{1,0:T(8,128)(2,1)S(1)}, u32[]{:S(2)}, u32[]{:S(2)}) collective-permute-start(bf16[16,1024]{1,0:T(8,128)(2,1)S(1)} %get-tuple-element.35), channel_id=1, source_target_pairs={{0,16},{1,17},{2,18},{3,19},{4,20},{5,21},{6,22},{7,23},{8,24},{9,... | collective-permute-start | bytes 98312 | tf_op jit(solution)/shard_map/ppermute | solution.py:218
  57.9 0.4 collective-permute-done.20
  58.4 2.3 %collective-permute-done.22 = bf16[16,1024]{1,0:T(8,128)(2,1)S(1)} collective-permute-done((bf16[16,1024]{1,0:T(8,128)(2,1)S(1)}, bf16[16,1024]{1,0:T(8,128)(2,1)S(1)}, u32[]{:S(2)}, u32[]{:S(2)}) %collective-permute-start.22) | collective-permute-done | bytes 32800 | tf_op jit(solution)/shard_map/ppermute | solution.py:218
  60.7 1.4 %collective-permute-done.21 = bf16[16,1024]{1,0:T(8,128)(2,1)S(1)} collective-permute-done((bf16[16,1024]{1,0:T(8,128)(2,1)S(1)}, bf16[16,1024]{1,0:T(8,128)(2,1)S(1)}, u32[]{:S(2)}, u32[]{:S(2)}) %collective-permute-start.21) | collective-permute-done | bytes 32800 | tf_op jit(solution)/shard_map/ppermute | solution.py:218
  62.1 0.6 %fusion.5 = bf16[16,1024]{1,0:T(8,128)(2,1)} fusion(bf16[16,1024]{1,0:T(8,128)(2,1)S(1)} %collective-permute-done.22, bf16[16,1024]{1,0:T(8,128)(2,1)S(1)} %collective-permute-done.21, bf16[16,1024]{1,0:T(8,128)(2,1)S(1)} %collective-permute-done.20, f32[4,16,1024]{2,1,0:T(8,128)S(1)} %fusion.2), kind=kLoop, calls=%fused_computation.15 | loop fusion | flops 114688 | bytes 196608 | tf_op jit(solution)/shard_map/convert_element_type | solution.py:280
  (13 shorter events, 0.2 us)
Async XLA Ops:
  2.4 8.6 %collective-permute-start.3 = (bf16[16,3712]{1,0:T(8,128)(2,1)}, bf16[16,3712]{1,0:T(8,128)(2,1)S(1)}, u32[]{:S(2)}, u32[]{:S(2)}) collective-permute-start(bf16[16,3712]{1,0:T(8,128)(2,1)} %pack_rows.1), channel_id=1, source_target_pairs={{0,8},{1,9},{2,10},{3,11},{4,12},{5,13},{6,14},{7,15},{8,0},{9,1},... | collective-permute-start | bytes 356360 | tf_op jit(solution)/shard_map/ppermute | solution.py:218
  5.4 8.4 %collective-permute-start.7 = (bf16[16,3712]{1,0:T(8,128)(2,1)}, bf16[16,3712]{1,0:T(8,128)(2,1)S(1)}, u32[]{:S(2)}, u32[]{:S(2)}) collective-permute-start(bf16[16,3712]{1,0:T(8,128)(2,1)} %pack_rows.1), channel_id=1, source_target_pairs={{0,16},{1,17},{2,18},{3,19},{4,20},{5,21},{6,22},{7,23},{8,24},{9,... | collective-permute-start | bytes 356360 | tf_op jit(solution)/shard_map/ppermute | solution.py:218
  8.0 12.3 %collective-permute-start.1 = (bf16[16,3712]{1,0:T(8,128)(2,1)}, bf16[16,3712]{1,0:T(8,128)(2,1)S(1)}, u32[]{:S(2)}, u32[]{:S(2)}) collective-permute-start(bf16[16,3712]{1,0:T(8,128)(2,1)} %pack_rows.1), channel_id=1, source_target_pairs={{0,4},{1,3},{2,6},{3,1},{4,0},{5,7},{6,2},{7,5},{8,12},{9,11},{10,... | collective-permute-start | bytes 356360 | tf_op jit(solution)/shard_map/ppermute | solution.py:218
  9.5 5.3 %collective-permute-start = (bf16[16,3712]{1,0:T(8,128)(2,1)}, bf16[16,3712]{1,0:T(8,128)(2,1)S(1)}, u32[]{:S(2)}, u32[]{:S(2)}) collective-permute-start(bf16[16,3712]{1,0:T(8,128)(2,1)} %pack_rows.1), channel_id=1, source_target_pairs={{0,2},{1,5},{2,0},{3,7},{4,6},{5,1},{6,4},{7,3},{8,10},{9,13},{10,... | collective-permute-start | bytes 356360 | tf_op jit(solution)/shard_map/ppermute | solution.py:218
  11.0 12.4 %collective-permute-start.5 = (bf16[16,3712]{1,0:T(8,128)(2,1)S(1)}, bf16[16,3712]{1,0:T(8,128)(2,1)S(1)}, u32[]{:S(2)}, u32[]{:S(2)}) collective-permute-start(bf16[16,3712]{1,0:T(8,128)(2,1)S(1)} %collective-permute-done.3), channel_id=1, source_target_pairs={{0,4},{1,3},{2,6},{3,1},{4,0},{5,7},{6,2},{7,5},{8,12},{9,11},{10,... | collective-permute-start | bytes 356360 | tf_op jit(solution)/shard_map/ppermute | solution.py:218
  12.0 10.8 %collective-permute-start.4 = (bf16[16,3712]{1,0:T(8,128)(2,1)S(1)}, bf16[16,3712]{1,0:T(8,128)(2,1)S(1)}, u32[]{:S(2)}, u32[]{:S(2)}) collective-permute-start(bf16[16,3712]{1,0:T(8,128)(2,1)S(1)} %collective-permute-done.3), channel_id=1, source_target_pairs={{0,2},{1,5},{2,0},{3,7},{4,6},{5,1},{6,4},{7,3},{8,10},{9,13},{10,... | collective-permute-start | bytes 356360 | tf_op jit(solution)/shard_map/ppermute | solution.py:218
  13.8 4.8 %collective-permute-start.8 = (bf16[16,3712]{1,0:T(8,128)(2,1)S(1)}, bf16[16,3712]{1,0:T(8,128)(2,1)S(1)}, u32[]{:S(2)}, u32[]{:S(2)}) collective-permute-start(bf16[16,3712]{1,0:T(8,128)(2,1)S(1)} %collective-permute-done.7), channel_id=1, source_target_pairs={{0,8},{1,9},{2,10},{3,11},{4,12},{5,13},{6,14},{7,15},{8,0},{9,1},... | collective-permute-start | bytes 356360 | tf_op jit(solution)/shard_map/ppermute | solution.py:218
  14.9 6.9 %collective-permute-start.2 = (bf16[16,3712]{1,0:T(8,128)(2,1)S(1)}, bf16[16,3712]{1,0:T(8,128)(2,1)S(1)}, u32[]{:S(2)}, u32[]{:S(2)}) collective-permute-start(bf16[16,3712]{1,0:T(8,128)(2,1)S(1)} %collective-permute-done), channel_id=1, source_target_pairs={{0,4},{1,3},{2,6},{3,1},{4,0},{5,7},{6,2},{7,5},{8,12},{9,11},{10,... | collective-permute-start | bytes 356360 | tf_op jit(solution)/shard_map/ppermute | solution.py:218
  18.7 6.2 %collective-permute-start.10 = (bf16[32,3712]{1,0:T(8,128)(2,1)S(1)}, bf16[32,3712]{1,0:T(8,128)(2,1)S(1)}, u32[]{:S(2)}, u32[]{:S(2)}) collective-permute-start(bf16[32,3712]{1,0:T(8,128)(2,1)S(1)} %constant_dynamic-update-slice_fusion.4), channel_id=1, source_target_pairs={{0,4},{1,3},{2,6},{3,1},{4,0},{5,7},{6,2},{7,5},{8,12},{9,11},{10,... | collective-permute-start | bytes 712712 | tf_op jit(solution)/shard_map/ppermute | solution.py:218
  20.3 6.5 %collective-permute-start.9 = (bf16[32,3712]{1,0:T(8,128)(2,1)S(1)}, bf16[32,3712]{1,0:T(8,128)(2,1)S(1)}, u32[]{:S(2)}, u32[]{:S(2)}) collective-permute-start(bf16[32,3712]{1,0:T(8,128)(2,1)S(1)} %constant_dynamic-update-slice_fusion.4), channel_id=1, source_target_pairs={{0,2},{1,5},{2,0},{3,7},{4,6},{5,1},{6,4},{7,3},{8,10},{9,13},{10,... | collective-permute-start | bytes 712712 | tf_op jit(solution)/shard_map/ppermute | solution.py:218
  22.7 4.2 %collective-permute-start.11 = (bf16[64,3712]{1,0:T(8,128)(2,1)S(1)}, bf16[64,3712]{1,0:T(8,128)(2,1)S(1)}, u32[]{:S(2)}, u32[]{:S(2)}) collective-permute-start(bf16[64,3712]{1,0:T(8,128)(2,1)S(1)} %pad_maximum_fusion.2.refs_0_), channel_id=1, source_target_pairs={{0,1},{1,0},{2,3},{3,2},{4,5},{5,4},{6,7},{7,6},{8,9},{9,8},{10,11... | collective-permute-start | bytes 1425416 | tf_op jit(solution)/shard_map/ppermute | solution.py:218
  22.8 4.9 %collective-permute-start.6 = (bf16[16,3712]{1,0:T(8,128)(2,1)S(1)}, bf16[16,3712]{1,0:T(8,128)(2,1)S(1)}, u32[]{:S(2)}, u32[]{:S(2)}) collective-permute-start(bf16[16,3712]{1,0:T(8,128)(2,1)S(1)} %collective-permute-done.4), channel_id=1, source_target_pairs={{0,4},{1,3},{2,6},{3,1},{4,0},{5,7},{6,2},{7,5},{8,12},{9,11},{10,... | collective-permute-start | bytes 356360 | tf_op jit(solution)/shard_map/ppermute | solution.py:218
  26.9 8.6 %copy-start = (bf16[96,3712]{1,0:T(8,128)(2,1)}, bf16[96,3712]{1,0:T(8,128)(2,1)S(1)}, u32[]{:S(2)}) copy-start(bf16[96,3712]{1,0:T(8,128)(2,1)S(1)} %pad_maximum_fusion.refs_2_) | copy-start | bytes 2138116
  26.9 8.6 %collective-permute-start.14 = (bf16[96,3712]{1,0:T(8,128)(2,1)S(1)}, bf16[96,3712]{1,0:T(8,128)(2,1)}, u32[]{:S(2)}, u32[]{:S(2)}) collective-permute-start(bf16[96,3712]{1,0:T(8,128)(2,1)S(1)} %pad_maximum_fusion.refs_2_), channel_id=1, source_target_pairs={{0,1},{1,0},{2,3},{3,2},{4,5},{5,4},{6,7},{7,6},{8,9},{9,8},{10,11... | collective-permute-start | bytes 2138120 | tf_op jit(solution)/shard_map/ppermute | solution.py:218
  27.7 6.3 %collective-permute-start.13 = (bf16[64,3712]{1,0:T(8,128)(2,1)S(1)}, bf16[64,3712]{1,0:T(8,128)(2,1)S(1)}, u32[]{:S(2)}, u32[]{:S(2)}) collective-permute-start(bf16[64,3712]{1,0:T(8,128)(2,1)S(1)} %constant_dynamic-update-slice_fusion.refs_1_), channel_id=1, source_target_pairs={{0,1},{1,0},{2,3},{3,2},{4,5},{5,4},{6,7},{7,6},{8,9},{9,8},{10,11... | collective-permute-start | bytes 1425416 | tf_op jit(solution)/shard_map/ppermute | solution.py:218
  27.8 6.1 %collective-permute-start.12 = (bf16[32,3712]{1,0:T(8,128)(2,1)S(1)}, bf16[32,3712]{1,0:T(8,128)(2,1)S(1)}, u32[]{:S(2)}, u32[]{:S(2)}) collective-permute-start(bf16[32,3712]{1,0:T(8,128)(2,1)S(1)} %collective-permute-done.9), channel_id=1, source_target_pairs={{0,4},{1,3},{2,6},{3,1},{4,0},{5,7},{6,2},{7,5},{8,12},{9,11},{10,... | collective-permute-start | bytes 712712 | tf_op jit(solution)/shard_map/ppermute | solution.py:218
  34.0 1.5 %collective-permute-start.15 = (bf16[32,3712]{1,0:T(8,128)(2,1)S(1)}, bf16[32,3712]{1,0:T(8,128)(2,1)S(1)}, u32[]{:S(2)}, u32[]{:S(2)}) collective-permute-start(bf16[32,3712]{1,0:T(8,128)(2,1)S(1)} %collective-permute-done.12.refs_3_), channel_id=1, source_target_pairs={{0,1},{1,0},{2,3},{3,2},{4,5},{5,4},{6,7},{7,6},{8,9},{9,8},{10,11... | collective-permute-start | bytes 712712 | tf_op jit(solution)/shard_map/ppermute | solution.py:218
  42.7 2.0 %collective-permute-start.16 = (bf16[256,1024]{1,0:T(8,128)(2,1)S(1)}, bf16[256,1024]{1,0:T(8,128)(2,1)S(1)}, u32[]{:S(2)}, u32[]{:S(2)}) collective-permute-start(bf16[256,1024]{1,0:T(8,128)(2,1)S(1)} %pad_maximum_fusion.1), channel_id=1, source_target_pairs={{0,1},{1,0},{2,3},{3,2},{4,5},{5,4},{6,7},{7,6},{8,9},{9,8},{10,11... | collective-permute-start | bytes 1572872 | tf_op jit(solution)/shard_map/ppermute | solution.py:218
  45.0 7.3 %collective-permute-start.17 = (bf16[4,16,1024]{2,1,0:T(8,128)(2,1)S(1)}, bf16[4,16,1024]{2,1,0:T(8,128)(2,1)S(1)}, u32[]{:S(2)}, u32[]{:S(2)}) collective-permute-start(bf16[4,16,1024]{2,1,0:T(8,128)(2,1)S(1)} %get-tuple-element.28), channel_id=1, source_target_pairs={{0,6},{1,7},{2,4},{3,5},{4,2},{5,3},{6,0},{7,1},{8,14},{9,15},{10,... | collective-permute-start | bytes 393224 | tf_op jit(solution)/shard_map/ppermute | solution.py:218
  46.7 7.6 %collective-permute-start.19 = (bf16[4,16,1024]{2,1,0:T(8,128)(2,1)S(1)}, bf16[4,16,1024]{2,1,0:T(8,128)(2,1)S(1)}, u32[]{:S(2)}, u32[]{:S(2)}) collective-permute-start(bf16[4,16,1024]{2,1,0:T(8,128)(2,1)S(1)} %get-tuple-element.29), channel_id=1, source_target_pairs={{0,4},{1,3},{2,6},{3,1},{4,0},{5,7},{6,2},{7,5},{8,12},{9,11},{10,... | collective-permute-start | bytes 393224 | tf_op jit(solution)/shard_map/ppermute | solution.py:218
  48.5 5.8 %collective-permute-start.18 = (bf16[4,16,1024]{2,1,0:T(8,128)(2,1)S(1)}, bf16[4,16,1024]{2,1,0:T(8,128)(2,1)S(1)}, u32[]{:S(2)}, u32[]{:S(2)}) collective-permute-start(bf16[4,16,1024]{2,1,0:T(8,128)(2,1)S(1)} %get-tuple-element.30), channel_id=1, source_target_pairs={{0,2},{1,5},{2,0},{3,7},{4,6},{5,1},{6,4},{7,3},{8,10},{9,13},{10,... | collective-permute-start | bytes 393224 | tf_op jit(solution)/shard_map/ppermute | solution.py:218
  54.4 4.0 %collective-permute-start.20 = (bf16[16,1024]{1,0:T(8,128)(2,1)S(1)}, bf16[16,1024]{1,0:T(8,128)(2,1)S(1)}, u32[]{:S(2)}, u32[]{:S(2)}) collective-permute-start(bf16[16,1024]{1,0:T(8,128)(2,1)S(1)} %get-tuple-element.33), channel_id=1, source_target_pairs={{0,8},{1,9},{2,10},{3,11},{4,12},{5,13},{6,14},{7,15},{8,0},{9,1},... | collective-permute-start | bytes 98312 | tf_op jit(solution)/shard_map/ppermute | solution.py:218
  54.9 5.8 %collective-permute-start.22 = (bf16[16,1024]{1,0:T(8,128)(2,1)S(1)}, bf16[16,1024]{1,0:T(8,128)(2,1)S(1)}, u32[]{:S(2)}, u32[]{:S(2)}) collective-permute-start(bf16[16,1024]{1,0:T(8,128)(2,1)S(1)} %get-tuple-element.34), channel_id=1, source_target_pairs={{0,24},{1,25},{2,26},{3,27},{4,28},{5,29},{6,30},{7,31},{8,16},{9,... | collective-permute-start | bytes 98312 | tf_op jit(solution)/shard_map/ppermute | solution.py:218
  57.2 4.8 %collective-permute-start.21 = (bf16[16,1024]{1,0:T(8,128)(2,1)S(1)}, bf16[16,1024]{1,0:T(8,128)(2,1)S(1)}, u32[]{:S(2)}, u32[]{:S(2)}) collective-permute-start(bf16[16,1024]{1,0:T(8,128)(2,1)S(1)} %get-tuple-element.35), channel_id=1, source_target_pairs={{0,16},{1,17},{2,18},{3,19},{4,20},{5,21},{6,22},{7,23},{8,24},{9,... | collective-permute-start | bytes 98312 | tf_op jit(solution)/shard_map/ppermute | solution.py:218

commit v6 on v5

--- a/solution.py
+++ b/solution.py
@@ -263,14 +263,14 @@
         far_two = jnp.swapaxes(parts[2].reshape(4, 2, tok_rows, -1), 0, 1)
         return jnp.concatenate([near_two, far_two], axis=0)
 
-    keep = by_layer(scaled[:3])
-    came = swap(jnp.concatenate(scaled[3:], axis=0), 1)
-    came = by_layer([came[: 4 * tok_rows], came[4 * tok_rows : 8 * tok_rows], came[8 * tok_rows :]])
-    partial = add32(keep, came)
-    leaving = partial[:, 1:].astype(jnp.bfloat16)
+    keep, send = by_layer(scaled[:3]), by_layer(scaled[3:])
+    cross = add32(keep[:, 3], swap(send[:, 3], 1)).astype(jnp.bfloat16)
+    came = swap(send[:, :3], 1)
+    leaving = add32(keep[:, 1:3], came[:, 1:]).astype(jnp.bfloat16)
     partial = add32(
-        partial[:, 0],
-        swap(leaving[:, 2], 6),
+        keep[:, 0],
+        came[:, 0],
+        swap(cross, 6),
         swap(leaving[:, 0], 2, 4),
         swap(leaving[:, 1], 4, 2),
     )

time: 62.9 us -> 62.7 us (level)
  waiting for transfers between devices: 24.6 us -> 23.9 us
    ppermute x23 -> x24, waiting for transfers between devices: 24.6 us -> 23.9 us  [swap(): lax.ppermute(array, 'expert', [(i, i ^ (odd if i & 1 else even)) for i in...]
    ppermute x23 -> x24, starting transfers between devices: 24.3 us -> 24.9 us  [swap(): lax.ppermute(array, 'expert', [(i, i ^ (odd if i & 1 else even)) for i in...]
  transfers between devices with their start and end apart: 23 -> 24, of which waited for: 14 -> 15; matrix products, arithmetic and copies ran while one was open for 2% -> 2% of each run, Pallas kernels for 3% -> 3%
where the time goes in v6:
time: 62.7 us; the launch traced here: 62.6 us
  starting transfers between devices  24.9 us (40%)
  waiting for transfers between devices  23.9 us (38%)
  Pallas kernels  10.9 us (17%)
  other arithmetic  1.93 us (3%)
  between operations  0.8 us (1%)
    ppermute x24, starting transfers between devices, swap(): lax.ppermute(array, 'expert', [(i, i ^ (odd if i & 1 else even)) for i in...  24.9 us
    ppermute x24, waiting for transfers between devices, swap(): lax.ppermute(array, 'expert', [(i, i ^ (odd if i & 1 else even)) for i in...  23.9 us
    pallas_call x1, Pallas kernels, expert_rows(): pl.pallas_call(functools.partial(expert_kernel, chosen, blocks, len(parts...  7.19 us
    pallas_call x1, Pallas kernels, expert_histogram(): pl.pallas_call(functools.partial(histogram_kernel, blocks, len(codes)), o...  2 us
    pallas_call x1, Pallas kernels, pack_rows(): pl.pallas_call(pack_kernel, out_shape=jax.ShapeDtypeStruct((tok_rows, wid...  1.76 us
  transfers between devices with their start and end apart: 24, of which 15 were waited for; matrix products, arithmetic and copies ran while one was open for 2% of the time, Pallas kernels for 3%

profile of v6, /device:TPU:0, one launch (start us, length us, event | category | flops | bytes accessed | tf_op | source)
XLA Modules:
  0.0 62.6 jit_solution(10996596807338242582)
XLA Ops:
  0.6 1.8 %pack_rows.1 = bf16[16,3712]{1,0:T(8,128)(2,1)} custom-call(bf16[16,3584]{1,0:T(8,128)(2,1)} %tokens_ref.1, s32[8,16]{1,0:T(8,128)} %bitcast.73, f32[8,16]{1,0:T(8,128)} %bitcast.74, s32[64,16]{1,0:T(8,128)} %bitcast.72), custom_call_target="tpu_custom_call" | custom-call | tf_op jit(solution)/shard_map/pack_rows/pallas_call | solution.py:46
  2.4 3.0 %collective-permute-start.3 = (bf16[16,3712]{1,0:T(8,128)(2,1)}, bf16[16,3712]{1,0:T(8,128)(2,1)S(1)}, u32[]{:S(2)}, u32[]{:S(2)}) collective-permute-start(bf16[16,3712]{1,0:T(8,128)(2,1)} %pack_rows.1), channel_id=1, source_target_pairs={{0,8},{1,9},{2,10},{3,11},{4,12},{5,13},{6,14},{7,15},{8,0},{9,1},... | collective-permute-start | bytes 356360 | tf_op jit(solution)/shard_map/ppermute | solution.py:218
  5.4 2.6 %collective-permute-start.7 = (bf16[16,3712]{1,0:T(8,128)(2,1)}, bf16[16,3712]{1,0:T(8,128)(2,1)S(1)}, u32[]{:S(2)}, u32[]{:S(2)}) collective-permute-start(bf16[16,3712]{1,0:T(8,128)(2,1)} %pack_rows.1), channel_id=1, source_target_pairs={{0,16},{1,17},{2,18},{3,19},{4,20},{5,21},{6,22},{7,23},{8,24},{9,... | collective-permute-start | bytes 356360 | tf_op jit(solution)/shard_map/ppermute | solution.py:218
  8.0 1.5 %collective-permute-start.1 = (bf16[16,3712]{1,0:T(8,128)(2,1)}, bf16[16,3712]{1,0:T(8,128)(2,1)S(1)}, u32[]{:S(2)}, u32[]{:S(2)}) collective-permute-start(bf16[16,3712]{1,0:T(8,128)(2,1)} %pack_rows.1), channel_id=1, source_target_pairs={{0,4},{1,3},{2,6},{3,1},{4,0},{5,7},{6,2},{7,5},{8,12},{9,11},{10,... | collective-permute-start | bytes 356360 | tf_op jit(solution)/shard_map/ppermute | solution.py:218
  9.5 1.5 %collective-permute-start = (bf16[16,3712]{1,0:T(8,128)(2,1)}, bf16[16,3712]{1,0:T(8,128)(2,1)S(1)}, u32[]{:S(2)}, u32[]{:S(2)}) collective-permute-start(bf16[16,3712]{1,0:T(8,128)(2,1)} %pack_rows.1), channel_id=1, source_target_pairs={{0,2},{1,5},{2,0},{3,7},{4,6},{5,1},{6,4},{7,3},{8,10},{9,13},{10,... | collective-permute-start | bytes 356360 | tf_op jit(solution)/shard_map/ppermute | solution.py:218
  11.0 0.0 collective-permute-done.3
  11.0 1.0 %collective-permute-start.5 = (bf16[16,3712]{1,0:T(8,128)(2,1)S(1)}, bf16[16,3712]{1,0:T(8,128)(2,1)S(1)}, u32[]{:S(2)}, u32[]{:S(2)}) collective-permute-start(bf16[16,3712]{1,0:T(8,128)(2,1)S(1)} %collective-permute-done.3), channel_id=1, source_target_pairs={{0,4},{1,3},{2,6},{3,1},{4,0},{5,7},{6,2},{7,5},{8,12},{9,11},{10,... | collective-permute-start | bytes 356360 | tf_op jit(solution)/shard_map/ppermute | solution.py:218
  12.0 1.5 %collective-permute-start.4 = (bf16[16,3712]{1,0:T(8,128)(2,1)S(1)}, bf16[16,3712]{1,0:T(8,128)(2,1)S(1)}, u32[]{:S(2)}, u32[]{:S(2)}) collective-permute-start(bf16[16,3712]{1,0:T(8,128)(2,1)S(1)} %collective-permute-done.3), channel_id=1, source_target_pairs={{0,2},{1,5},{2,0},{3,7},{4,6},{5,1},{6,4},{7,3},{8,10},{9,13},{10,... | collective-permute-start | bytes 356360 | tf_op jit(solution)/shard_map/ppermute | solution.py:218
  13.5 0.3 collective-permute-done.7
  13.8 0.4 collective-permute-start.8
  14.3 0.6 collective-permute-done
  14.9 1.0 %collective-permute-start.2 = (bf16[16,3712]{1,0:T(8,128)(2,1)S(1)}, bf16[16,3712]{1,0:T(8,128)(2,1)S(1)}, u32[]{:S(2)}, u32[]{:S(2)}) collective-permute-start(bf16[16,3712]{1,0:T(8,128)(2,1)S(1)} %collective-permute-done), channel_id=1, source_target_pairs={{0,4},{1,3},{2,6},{3,1},{4,0},{5,7},{6,2},{7,5},{8,12},{9,11},{10,... | collective-permute-start | bytes 356360 | tf_op jit(solution)/shard_map/ppermute | solution.py:218
  15.9 2.8 %collective-permute-done.8 = bf16[16,3712]{1,0:T(8,128)(2,1)S(1)} collective-permute-done((bf16[16,3712]{1,0:T(8,128)(2,1)S(1)}, bf16[16,3712]{1,0:T(8,128)(2,1)S(1)}, u32[]{:S(2)}, u32[]{:S(2)}) %collective-permute-start.8) | collective-permute-done | bytes 118816 | tf_op jit(solution)/shard_map/ppermute | solution.py:218
  18.7 1.6 %collective-permute-start.10 = (bf16[32,3712]{1,0:T(8,128)(2,1)S(1)}, bf16[32,3712]{1,0:T(8,128)(2,1)S(1)}, u32[]{:S(2)}, u32[]{:S(2)}) collective-permute-start(bf16[32,3712]{1,0:T(8,128)(2,1)S(1)} %constant_dynamic-update-slice_fusion.4), channel_id=1, source_target_pairs={{0,4},{1,3},{2,6},{3,1},{4,0},{5,7},{6,2},{7,5},{8,12},{9,11},{10,... | collective-permute-start | bytes 712712 | tf_op jit(solution)/shard_map/ppermute | solution.py:218
  20.3 0.0 collective-permute-done.1
  20.3 1.5 %collective-permute-start.9 = (bf16[32,3712]{1,0:T(8,128)(2,1)S(1)}, bf16[32,3712]{1,0:T(8,128)(2,1)S(1)}, u32[]{:S(2)}, u32[]{:S(2)}) collective-permute-start(bf16[32,3712]{1,0:T(8,128)(2,1)S(1)} %constant_dynamic-update-slice_fusion.4), channel_id=1, source_target_pairs={{0,2},{1,5},{2,0},{3,7},{4,6},{5,1},{6,4},{7,3},{8,10},{9,13},{10,... | collective-permute-start | bytes 712712 | tf_op jit(solution)/shard_map/ppermute | solution.py:218
  21.8 0.0 collective-permute-done.2
  21.8 0.9 %pad_maximum_fusion.2.refs_0_ = bf16[64,3712]{1,0:T(8,128)(2,1)S(1)} fusion(bf16[16,3712]{1,0:T(8,128)(2,1)S(1)} %collective-permute-done.2, bf16[16,3712]{1,0:T(8,128)(2,1)S(1)} %collective-permute-done.1, bf16[16,3712]{1,0:T(8,128)(2,1)S(1)} %collective-permute-done, bf16[16,3712]{1,0:T(8,128)(2,1)} %pack_rows.1), kind=kLoop, calls=%fused_computation.3 | loop fusion | flops 1900544 | bytes 950272 | tf_op jit(solution)/shard_map/concatenate | solution.py:238
  22.7 0.1 collective-permute-start.11
  22.8 0.0 collective-permute-done.4
  22.8 0.6 collective-permute-start.6
  23.4 0.0 collective-permute-done.5
  23.4 1.4 %collective-permute-done.10 = bf16[32,3712]{1,0:T(8,128)(2,1)S(1)} collective-permute-done((bf16[32,3712]{1,0:T(8,128)(2,1)S(1)}, bf16[32,3712]{1,0:T(8,128)(2,1)S(1)}, u32[]{:S(2)}, u32[]{:S(2)}) %collective-permute-start.10) | collective-permute-done | bytes 237600 | tf_op jit(solution)/shard_map/ppermute | solution.py:218
  24.9 2.0 %collective-permute-done.9 = bf16[32,3712]{1,0:T(8,128)(2,1)S(1)} collective-permute-done((bf16[32,3712]{1,0:T(8,128)(2,1)S(1)}, bf16[32,3712]{1,0:T(8,128)(2,1)S(1)}, u32[]{:S(2)}, u32[]{:S(2)}) %collective-permute-start.9) | collective-permute-done | bytes 237600 | tf_op jit(solution)/shard_map/ppermute | solution.py:218
  26.8 0.1 pad_maximum_fusion.refs_2_
  26.9 0.0 copy-start
  26.9 0.0 collective-permute-done.11.refs_4_
  26.9 0.1 collective-permute-start.14
  27.0 0.7 %collective-permute-done.6 = bf16[16,3712]{1,0:T(8,128)(2,1)S(1)} collective-permute-done((bf16[16,3712]{1,0:T(8,128)(2,1)S(1)}, bf16[16,3712]{1,0:T(8,128)(2,1)S(1)}, u32[]{:S(2)}, u32[]{:S(2)}) %collective-permute-start.6) | collective-permute-done | bytes 118816 | tf_op jit(solution)/shard_map/ppermute | solution.py:218
  27.7 0.1 collective-permute-start.13
  27.8 0.5 collective-permute-start.12
  28.4 5.6 %collective-permute-done.12.refs_3_ = bf16[32,3712]{1,0:T(8,128)(2,1)S(1)} collective-permute-done((bf16[32,3712]{1,0:T(8,128)(2,1)S(1)}, bf16[32,3712]{1,0:T(8,128)(2,1)S(1)}, u32[]{:S(2)}, u32[]{:S(2)}) %collective-permute-start.12) | collective-permute-done | bytes 237600 | tf_op jit(solution)/shard_map/ppermute | solution.py:218
  34.0 0.0 collective-permute-start.15
  34.0 0.0 collective-permute-done.13.refs_5_
  34.0 1.5 %collective-permute-done.15.refs_7_ = bf16[32,3712]{1,0:T(8,128)(2,1)S(1)} collective-permute-done((bf16[32,3712]{1,0:T(8,128)(2,1)S(1)}, bf16[32,3712]{1,0:T(8,128)(2,1)S(1)}, u32[]{:S(2)}, u32[]{:S(2)}) %collective-permute-start.15) | collective-permute-done | bytes 237600 | tf_op jit(solution)/shard_map/ppermute | solution.py:218
  35.5 0.0 collective-permute-done.14.refs_6_
  35.5 0.0 copy-done
  35.5 7.2 %expert_rows.1 = (bf16[64,1024]{1,0:T(8,128)(2,1)S(1)}, bf16[64,1024]{1,0:T(8,128)(2,1)S(1)}, bf16[96,1024]{1,0:T(8,128)(2,1)S(1)}, bf16[32,1024]{1,0:T(8,128)(2...) custom-call(s32[1]{0:T(128)} %bitcast.me_ref, ...), custom_call_target="tpu_custom_call" | custom-call | flops 3758096384 | bytes 7340032 | tf_op jit(solution)/shard_map/expert_rows/pallas_call | solution.py:135
  42.7 0.1 pad_maximum_fusion.1
  42.8 0.2 collective-permute-start.16
  43.0 0.4 collective-permute-start.17
  43.5 1.3 %collective-permute-done.17 = bf16[4,16,1024]{2,1,0:T(8,128)(2,1)S(1)} collective-permute-done((bf16[4,16,1024]{2,1,0:T(8,128)(2,1)S(1)}, bf16[4,16,1024]{2,1,0:T(8,128)(2,1)S(1)}, u32[]{:S(2)}, u32[]{:S(2)}) %collective-permute-start.17) | collective-permute-done | bytes 131104 | tf_op jit(solution)/shard_map/ppermute | solution.py:218
  44.8 1.7 %collective-permute-start.18 = (bf16[4,16,1024]{2,1,0:T(8,128)(2,1)S(1)}, bf16[4,16,1024]{2,1,0:T(8,128)(2,1)S(1)}, u32[]{:S(2)}, u32[]{:S(2)}) collective-permute-start(bf16[4,16,1024]{2,1,0:T(8,128)(2,1)S(1)} %fusion), channel_id=1, source_target_pairs={{0,6},{1,7},{2,4},{3,5},{4,2},{5,3},{6,0},{7,1},{8,14},{9,15},{10,... | collective-permute-start | bytes 393224 | tf_op jit(solution)/shard_map/ppermute | solution.py:218
  46.5 0.0 collective-permute-done.16
  46.5 0.1 add_convert_fusion
  46.6 0.4 collective-permute-start.19
  47.1 1.5 %collective-permute-start.20 = (bf16[4,16,1024]{2,1,0:T(8,128)(2,1)S(1)}, bf16[4,16,1024]{2,1,0:T(8,128)(2,1)S(1)}, u32[]{:S(2)}, u32[]{:S(2)}) collective-permute-start(bf16[4,16,1024]{2,1,0:T(8,128)(2,1)S(1)} %get-tuple-element.27), channel_id=1, source_target_pairs={{0,4},{1,3},{2,6},{3,1},{4,0},{5,7},{6,2},{7,5},{8,12},{9,11},{10,... | collective-permute-start | bytes 393224 | tf_op jit(solution)/shard_map/ppermute | solution.py:218
  48.6 2.0 %expert_histogram.1 = f32[8,2048]{1,0:T(8,128)} custom-call(f32[512,128]{1,0:T(8,128)S(1)} %get-tuple-element.23.refs_0_, f32[512,128]{1,0:T(8,128)S(1)} %get-tuple-element.24.refs_1_), custom_call_target="tpu_custom_call" | custom-call | flops 268435456 | bytes 524288 | tf_op jit(solution)/shard_map/expert_histogram/pallas_call | solution.py:202
  50.6 1.5 %collective-permute-done.18 = bf16[4,16,1024]{2,1,0:T(8,128)(2,1)S(1)} collective-permute-done((bf16[4,16,1024]{2,1,0:T(8,128)(2,1)S(1)}, bf16[4,16,1024]{2,1,0:T(8,128)(2,1)S(1)}, u32[]{:S(2)}, u32[]{:S(2)}) %collective-permute-start.18) | collective-permute-done | bytes 131104 | tf_op jit(solution)/shard_map/ppermute | solution.py:218
  52.1 1.3 %collective-permute-done.19 = bf16[4,16,1024]{2,1,0:T(8,128)(2,1)S(1)} collective-permute-done((bf16[4,16,1024]{2,1,0:T(8,128)(2,1)S(1)}, bf16[4,16,1024]{2,1,0:T(8,128)(2,1)S(1)}, u32[]{:S(2)}, u32[]{:S(2)}) %collective-permute-start.19) | collective-permute-done | bytes 131104 | tf_op jit(solution)/shard_map/ppermute | solution.py:218
  53.4 0.7 %collective-permute-done.20 = bf16[4,16,1024]{2,1,0:T(8,128)(2,1)S(1)} collective-permute-done((bf16[4,16,1024]{2,1,0:T(8,128)(2,1)S(1)}, bf16[4,16,1024]{2,1,0:T(8,128)(2,1)S(1)}, u32[]{:S(2)}, u32[]{:S(2)}) %collective-permute-start.20) | collective-permute-done | bytes 131104 | tf_op jit(solution)/shard_map/ppermute | solution.py:218
  54.1 0.1 fusion.2
  54.2 0.5 collective-permute-start.21
  54.7 2.4 %collective-permute-start.23 = (bf16[16,1024]{1,0:T(8,128)(2,1)S(1)}, bf16[16,1024]{1,0:T(8,128)(2,1)S(1)}, u32[]{:S(2)}, u32[]{:S(2)}) collective-permute-start(bf16[16,1024]{1,0:T(8,128)(2,1)S(1)} %get-tuple-element.29), channel_id=1, source_target_pairs={{0,24},{1,25},{2,26},{3,27},{4,28},{5,29},{6,30},{7,31},{8,16},{9,... | collective-permute-start | bytes 98312 | tf_op jit(solution)/shard_map/ppermute | solution.py:218
  57.1 0.7 %collective-permute-start.22 = (bf16[16,1024]{1,0:T(8,128)(2,1)S(1)}, bf16[16,1024]{1,0:T(8,128)(2,1)S(1)}, u32[]{:S(2)}, u32[]{:S(2)}) collective-permute-start(bf16[16,1024]{1,0:T(8,128)(2,1)S(1)} %get-tuple-element.30), channel_id=1, source_target_pairs={{0,16},{1,17},{2,18},{3,19},{4,20},{5,21},{6,22},{7,23},{8,24},{9,... | collective-permute-start | bytes 98312 | tf_op jit(solution)/shard_map/ppermute | solution.py:218
  57.8 0.4 collective-permute-done.21
  58.2 2.3 %collective-permute-done.23 = bf16[16,1024]{1,0:T(8,128)(2,1)S(1)} collective-permute-done((bf16[16,1024]{1,0:T(8,128)(2,1)S(1)}, bf16[16,1024]{1,0:T(8,128)(2,1)S(1)}, u32[]{:S(2)}, u32[]{:S(2)}) %collective-permute-start.23) | collective-permute-done | bytes 32800 | tf_op jit(solution)/shard_map/ppermute | solution.py:218
  60.5 1.4 %collective-permute-done.22 = bf16[16,1024]{1,0:T(8,128)(2,1)S(1)} collective-permute-done((bf16[16,1024]{1,0:T(8,128)(2,1)S(1)}, bf16[16,1024]{1,0:T(8,128)(2,1)S(1)}, u32[]{:S(2)}, u32[]{:S(2)}) %collective-permute-start.22) | collective-permute-done | bytes 32800 | tf_op jit(solution)/shard_map/ppermute | solution.py:218
  61.9 0.6 %fusion.5 = bf16[16,1024]{1,0:T(8,128)(2,1)} fusion(bf16[16,1024]{1,0:T(8,128)(2,1)S(1)} %collective-permute-done.23, bf16[16,1024]{1,0:T(8,128)(2,1)S(1)} %collective-permute-done.22, bf16[16,1024]{1,0:T(8,128)(2,1)S(1)} %collective-permute-done.21, f32[4,16,1024]{2,1,0:T(8,128)S(1)} %fusion.2), kind=kLoop, calls=%fused_computation.20 | loop fusion | flops 114688 | bytes 196608 | tf_op jit(solution)/shard_map/convert_element_type | solution.py:280
  (14 shorter events, 0.2 us)
Async XLA Ops:
  2.4 8.6 %collective-permute-start.3 = (bf16[16,3712]{1,0:T(8,128)(2,1)}, bf16[16,3712]{1,0:T(8,128)(2,1)S(1)}, u32[]{:S(2)}, u32[]{:S(2)}) collective-permute-start(bf16[16,3712]{1,0:T(8,128)(2,1)} %pack_rows.1), channel_id=1, source_target_pairs={{0,8},{1,9},{2,10},{3,11},{4,12},{5,13},{6,14},{7,15},{8,0},{9,1},... | collective-permute-start | bytes 356360 | tf_op jit(solution)/shard_map/ppermute | solution.py:218
  5.4 8.4 %collective-permute-start.7 = (bf16[16,3712]{1,0:T(8,128)(2,1)}, bf16[16,3712]{1,0:T(8,128)(2,1)S(1)}, u32[]{:S(2)}, u32[]{:S(2)}) collective-permute-start(bf16[16,3712]{1,0:T(8,128)(2,1)} %pack_rows.1), channel_id=1, source_target_pairs={{0,16},{1,17},{2,18},{3,19},{4,20},{5,21},{6,22},{7,23},{8,24},{9,... | collective-permute-start | bytes 356360 | tf_op jit(solution)/shard_map/ppermute | solution.py:218
  8.0 12.3 %collective-permute-start.1 = (bf16[16,3712]{1,0:T(8,128)(2,1)}, bf16[16,3712]{1,0:T(8,128)(2,1)S(1)}, u32[]{:S(2)}, u32[]{:S(2)}) collective-permute-start(bf16[16,3712]{1,0:T(8,128)(2,1)} %pack_rows.1), channel_id=1, source_target_pairs={{0,4},{1,3},{2,6},{3,1},{4,0},{5,7},{6,2},{7,5},{8,12},{9,11},{10,... | collective-permute-start | bytes 356360 | tf_op jit(solution)/shard_map/ppermute | solution.py:218
  9.5 5.3 %collective-permute-start = (bf16[16,3712]{1,0:T(8,128)(2,1)}, bf16[16,3712]{1,0:T(8,128)(2,1)S(1)}, u32[]{:S(2)}, u32[]{:S(2)}) collective-permute-start(bf16[16,3712]{1,0:T(8,128)(2,1)} %pack_rows.1), channel_id=1, source_target_pairs={{0,2},{1,5},{2,0},{3,7},{4,6},{5,1},{6,4},{7,3},{8,10},{9,13},{10,... | collective-permute-start | bytes 356360 | tf_op jit(solution)/shard_map/ppermute | solution.py:218
  11.0 12.4 %collective-permute-start.5 = (bf16[16,3712]{1,0:T(8,128)(2,1)S(1)}, bf16[16,3712]{1,0:T(8,128)(2,1)S(1)}, u32[]{:S(2)}, u32[]{:S(2)}) collective-permute-start(bf16[16,3712]{1,0:T(8,128)(2,1)S(1)} %collective-permute-done.3), channel_id=1, source_target_pairs={{0,4},{1,3},{2,6},{3,1},{4,0},{5,7},{6,2},{7,5},{8,12},{9,11},{10,... | collective-permute-start | bytes 356360 | tf_op jit(solution)/shard_map/ppermute | solution.py:218
  12.0 10.8 %collective-permute-start.4 = (bf16[16,3712]{1,0:T(8,128)(2,1)S(1)}, bf16[16,3712]{1,0:T(8,128)(2,1)S(1)}, u32[]{:S(2)}, u32[]{:S(2)}) collective-permute-start(bf16[16,3712]{1,0:T(8,128)(2,1)S(1)} %collective-permute-done.3), channel_id=1, source_target_pairs={{0,2},{1,5},{2,0},{3,7},{4,6},{5,1},{6,4},{7,3},{8,10},{9,13},{10,... | collective-permute-start | bytes 356360 | tf_op jit(solution)/shard_map/ppermute | solution.py:218
  13.8 4.8 %collective-permute-start.8 = (bf16[16,3712]{1,0:T(8,128)(2,1)S(1)}, bf16[16,3712]{1,0:T(8,128)(2,1)S(1)}, u32[]{:S(2)}, u32[]{:S(2)}) collective-permute-start(bf16[16,3712]{1,0:T(8,128)(2,1)S(1)} %collective-permute-done.7), channel_id=1, source_target_pairs={{0,8},{1,9},{2,10},{3,11},{4,12},{5,13},{6,14},{7,15},{8,0},{9,1},... | collective-permute-start | bytes 356360 | tf_op jit(solution)/shard_map/ppermute | solution.py:218
  14.9 6.9 %collective-permute-start.2 = (bf16[16,3712]{1,0:T(8,128)(2,1)S(1)}, bf16[16,3712]{1,0:T(8,128)(2,1)S(1)}, u32[]{:S(2)}, u32[]{:S(2)}) collective-permute-start(bf16[16,3712]{1,0:T(8,128)(2,1)S(1)} %collective-permute-done), channel_id=1, source_target_pairs={{0,4},{1,3},{2,6},{3,1},{4,0},{5,7},{6,2},{7,5},{8,12},{9,11},{10,... | collective-permute-start | bytes 356360 | tf_op jit(solution)/shard_map/ppermute | solution.py:218
  18.7 6.2 %collective-permute-start.10 = (bf16[32,3712]{1,0:T(8,128)(2,1)S(1)}, bf16[32,3712]{1,0:T(8,128)(2,1)S(1)}, u32[]{:S(2)}, u32[]{:S(2)}) collective-permute-start(bf16[32,3712]{1,0:T(8,128)(2,1)S(1)} %constant_dynamic-update-slice_fusion.4), channel_id=1, source_target_pairs={{0,4},{1,3},{2,6},{3,1},{4,0},{5,7},{6,2},{7,5},{8,12},{9,11},{10,... | collective-permute-start | bytes 712712 | tf_op jit(solution)/shard_map/ppermute | solution.py:218
  20.3 6.5 %collective-permute-start.9 = (bf16[32,3712]{1,0:T(8,128)(2,1)S(1)}, bf16[32,3712]{1,0:T(8,128)(2,1)S(1)}, u32[]{:S(2)}, u32[]{:S(2)}) collective-permute-start(bf16[32,3712]{1,0:T(8,128)(2,1)S(1)} %constant_dynamic-update-slice_fusion.4), channel_id=1, source_target_pairs={{0,2},{1,5},{2,0},{3,7},{4,6},{5,1},{6,4},{7,3},{8,10},{9,13},{10,... | collective-permute-start | bytes 712712 | tf_op jit(solution)/shard_map/ppermute | solution.py:218
  22.7 4.2 %collective-permute-start.11 = (bf16[64,3712]{1,0:T(8,128)(2,1)S(1)}, bf16[64,3712]{1,0:T(8,128)(2,1)S(1)}, u32[]{:S(2)}, u32[]{:S(2)}) collective-permute-start(bf16[64,3712]{1,0:T(8,128)(2,1)S(1)} %pad_maximum_fusion.2.refs_0_), channel_id=1, source_target_pairs={{0,1},{1,0},{2,3},{3,2},{4,5},{5,4},{6,7},{7,6},{8,9},{9,8},{10,11... | collective-permute-start | bytes 1425416 | tf_op jit(solution)/shard_map/ppermute | solution.py:218
  22.8 4.9 %collective-permute-start.6 = (bf16[16,3712]{1,0:T(8,128)(2,1)S(1)}, bf16[16,3712]{1,0:T(8,128)(2,1)S(1)}, u32[]{:S(2)}, u32[]{:S(2)}) collective-permute-start(bf16[16,3712]{1,0:T(8,128)(2,1)S(1)} %collective-permute-done.4), channel_id=1, source_target_pairs={{0,4},{1,3},{2,6},{3,1},{4,0},{5,7},{6,2},{7,5},{8,12},{9,11},{10,... | collective-permute-start | bytes 356360 | tf_op jit(solution)/shard_map/ppermute | solution.py:218
  26.9 8.6 %copy-start = (bf16[96,3712]{1,0:T(8,128)(2,1)}, bf16[96,3712]{1,0:T(8,128)(2,1)S(1)}, u32[]{:S(2)}) copy-start(bf16[96,3712]{1,0:T(8,128)(2,1)S(1)} %pad_maximum_fusion.refs_2_) | copy-start | bytes 2138116
  26.9 8.6 %collective-permute-start.14 = (bf16[96,3712]{1,0:T(8,128)(2,1)S(1)}, bf16[96,3712]{1,0:T(8,128)(2,1)}, u32[]{:S(2)}, u32[]{:S(2)}) collective-permute-start(bf16[96,3712]{1,0:T(8,128)(2,1)S(1)} %pad_maximum_fusion.refs_2_), channel_id=1, source_target_pairs={{0,1},{1,0},{2,3},{3,2},{4,5},{5,4},{6,7},{7,6},{8,9},{9,8},{10,11... | collective-permute-start | bytes 2138120 | tf_op jit(solution)/shard_map/ppermute | solution.py:218
  27.7 6.3 %collective-permute-start.13 = (bf16[64,3712]{1,0:T(8,128)(2,1)S(1)}, bf16[64,3712]{1,0:T(8,128)(2,1)S(1)}, u32[]{:S(2)}, u32[]{:S(2)}) collective-permute-start(bf16[64,3712]{1,0:T(8,128)(2,1)S(1)} %constant_dynamic-update-slice_fusion.refs_1_), channel_id=1, source_target_pairs={{0,1},{1,0},{2,3},{3,2},{4,5},{5,4},{6,7},{7,6},{8,9},{9,8},{10,11... | collective-permute-start | bytes 1425416 | tf_op jit(solution)/shard_map/ppermute | solution.py:218
  27.8 6.1 %collective-permute-start.12 = (bf16[32,3712]{1,0:T(8,128)(2,1)S(1)}, bf16[32,3712]{1,0:T(8,128)(2,1)S(1)}, u32[]{:S(2)}, u32[]{:S(2)}) collective-permute-start(bf16[32,3712]{1,0:T(8,128)(2,1)S(1)} %collective-permute-done.9), channel_id=1, source_target_pairs={{0,4},{1,3},{2,6},{3,1},{4,0},{5,7},{6,2},{7,5},{8,12},{9,11},{10,... | collective-permute-start | bytes 712712 | tf_op jit(solution)/shard_map/ppermute | solution.py:218
  34.0 1.5 %collective-permute-start.15 = (bf16[32,3712]{1,0:T(8,128)(2,1)S(1)}, bf16[32,3712]{1,0:T(8,128)(2,1)S(1)}, u32[]{:S(2)}, u32[]{:S(2)}) collective-permute-start(bf16[32,3712]{1,0:T(8,128)(2,1)S(1)} %collective-permute-done.12.refs_3_), channel_id=1, source_target_pairs={{0,1},{1,0},{2,3},{3,2},{4,5},{5,4},{6,7},{7,6},{8,9},{9,8},{10,11... | collective-permute-start | bytes 712712 | tf_op jit(solution)/shard_map/ppermute | solution.py:218
  42.8 3.8 %collective-permute-start.16 = (bf16[4,3,16,1024]{3,2,0,1:T(8,128)(2,1)S(1)}, bf16[4,3,16,1024]{3,2,0,1:T(8,128)(2,1)S(1)}, u32[]{:S(2)}, u32[]{:S(2)}) collective-permute-start(bf16[4,3,16,1024]{3,2,0,1:T(8,128)(2,1)S(1)} %slice.55), channel_id=1, source_target_pairs={{0,1},{1,0},{2,3},{3,2},{4,5},{5,4},{6,7},{7,6},{8,9},{9,8},{10,11... | collective-permute-start | bytes 1179656 | tf_op jit(solution)/shard_map/ppermute | solution.py:218
  43.0 1.7 %collective-permute-start.17 = (bf16[4,16,1024]{2,1,0:T(8,128)(2,1)S(1)}, bf16[4,16,1024]{2,1,0:T(8,128)(2,1)S(1)}, u32[]{:S(2)}, u32[]{:S(2)}) collective-permute-start(bf16[4,16,1024]{2,1,0:T(8,128)(2,1)S(1)} %maximum_bitcast_fusion), channel_id=1, source_target_pairs={{0,1},{1,0},{2,3},{3,2},{4,5},{5,4},{6,7},{7,6},{8,9},{9,8},{10,11... | collective-permute-start | bytes 393224 | tf_op jit(solution)/shard_map/ppermute | solution.py:218
  44.8 7.3 %collective-permute-start.18 = (bf16[4,16,1024]{2,1,0:T(8,128)(2,1)S(1)}, bf16[4,16,1024]{2,1,0:T(8,128)(2,1)S(1)}, u32[]{:S(2)}, u32[]{:S(2)}) collective-permute-start(bf16[4,16,1024]{2,1,0:T(8,128)(2,1)S(1)} %fusion), channel_id=1, source_target_pairs={{0,6},{1,7},{2,4},{3,5},{4,2},{5,3},{6,0},{7,1},{8,14},{9,15},{10,... | collective-permute-start | bytes 393224 | tf_op jit(solution)/shard_map/ppermute | solution.py:218
  46.6 6.8 %collective-permute-start.19 = (bf16[4,16,1024]{2,1,0:T(8,128)(2,1)S(1)}, bf16[4,16,1024]{2,1,0:T(8,128)(2,1)S(1)}, u32[]{:S(2)}, u32[]{:S(2)}) collective-permute-start(bf16[4,16,1024]{2,1,0:T(8,128)(2,1)S(1)} %get-tuple-element.26), channel_id=1, source_target_pairs={{0,2},{1,5},{2,0},{3,7},{4,6},{5,1},{6,4},{7,3},{8,10},{9,13},{10,... | collective-permute-start | bytes 393224 | tf_op jit(solution)/shard_map/ppermute | solution.py:218
  47.1 7.0 %collective-permute-start.20 = (bf16[4,16,1024]{2,1,0:T(8,128)(2,1)S(1)}, bf16[4,16,1024]{2,1,0:T(8,128)(2,1)S(1)}, u32[]{:S(2)}, u32[]{:S(2)}) collective-permute-start(bf16[4,16,1024]{2,1,0:T(8,128)(2,1)S(1)} %get-tuple-element.27), channel_id=1, source_target_pairs={{0,4},{1,3},{2,6},{3,1},{4,0},{5,7},{6,2},{7,5},{8,12},{9,11},{10,... | collective-permute-start | bytes 393224 | tf_op jit(solution)/shard_map/ppermute | solution.py:218
  54.2 4.0 %collective-permute-start.21 = (bf16[16,1024]{1,0:T(8,128)(2,1)S(1)}, bf16[16,1024]{1,0:T(8,128)(2,1)S(1)}, u32[]{:S(2)}, u32[]{:S(2)}) collective-permute-start(bf16[16,1024]{1,0:T(8,128)(2,1)S(1)} %get-tuple-element.28), channel_id=1, source_target_pairs={{0,8},{1,9},{2,10},{3,11},{4,12},{5,13},{6,14},{7,15},{8,0},{9,1},... | collective-permute-start | bytes 98312 | tf_op jit(solution)/shard_map/ppermute | solution.py:218
  54.7 5.8 %collective-permute-start.23 = (bf16[16,1024]{1,0:T(8,128)(2,1)S(1)}, bf16[16,1024]{1,0:T(8,128)(2,1)S(1)}, u32[]{:S(2)}, u32[]{:S(2)}) collective-permute-start(bf16[16,1024]{1,0:T(8,128)(2,1)S(1)} %get-tuple-element.29), channel_id=1, source_target_pairs={{0,24},{1,25},{2,26},{3,27},{4,28},{5,29},{6,30},{7,31},{8,16},{9,... | collective-permute-start | bytes 98312 | tf_op jit(solution)/shard_map/ppermute | solution.py:218
  57.1 4.8 %collective-permute-start.22 = (bf16[16,1024]{1,0:T(8,128)(2,1)S(1)}, bf16[16,1024]{1,0:T(8,128)(2,1)S(1)}, u32[]{:S(2)}, u32[]{:S(2)}) collective-permute-start(bf16[16,1024]{1,0:T(8,128)(2,1)S(1)} %get-tuple-element.30), channel_id=1, source_target_pairs={{0,16},{1,17},{2,18},{3,19},{4,20},{5,21},{6,22},{7,23},{8,24},{9,... | collective-permute-start | bytes 98312 | tf_op jit(solution)/shard_map/ppermute | solution.py:218
